TPU v7x, 32 devices: a whole 2x2x4 slice. The times are simulated.
32 devices in a mesh: dp: 4 (over x, core), sp: 8 (over z, y).
Axes of the slice: x: 2, y: 2, z: 4, core: 2. Of those that a mesh axis runs over, the one named last changes fastest.
Arguments:
- ssm_input: bfloat16 [4, 1024, 8192], P('dp', 'sp'), may hold values from -6 to 6
- b_input: bfloat16 [4, 1024, 1024], P('dp', 'sp'), may hold values from -6 to 6
- c_input: bfloat16 [4, 1024, 1024], P('dp', 'sp'), may hold values from -6 to 6
- dt_input: bfloat16 [4, 1024, 128], P('dp', 'sp'), may hold values from -4 to 4
- conv_weight: float32 [4, 10240], replicated, may hold values from -3 to 3
- conv_bias: float32 [10240], replicated, may hold values from -3 to 3
- a_log: float32 [128], replicated, may hold values from -12 to 2
- dt_bias: float32 [128], replicated, may hold values from -5 to -3
- skip_gain: float32 [128], replicated, may hold values from 0.5 to 1.5
- grad_out: bfloat16 [4, 1024, 8192], P('dp', 'sp'), may hold values from -6 to 6
Outputs:
- y_out: bfloat16 [4, 1024, 8192], P('dp', 'sp')
- grad_x: bfloat16 [4, 1024, 8192], P('dp', 'sp')
- grad_b: bfloat16 [4, 1024, 1024], P('dp', 'sp')
- grad_c: bfloat16 [4, 1024, 1024], P('dp', 'sp')
- grad_dt: bfloat16 [4, 1024, 128], P('dp', 'sp')
- grad_conv_w: float32 [4, 10240], replicated
- grad_conv_b: float32 [10240], replicated
- grad_heads: float32 [3, 128], P(None, 'sp')
All inputs are finite; a program needn't handle non-finite values.
Results may differ from a plain program's by a relative error of at most 0.015.
Values may be sent and summed in bfloat16 or wider, within the bound.
No kernel may reach another device: no remote copies, remote signals or barrier semaphores. Data moves between devices by JAX's collectives and lax.ppermute only.
A program may use at most 192 MiB of HBM per device.

v0:
```python
import jax
import jax.numpy as jnp
from jax import lax
from jax.sharding import PartitionSpec as P

N = 256
Q = 128


def passed_along(value, axis, by):
    devices = lax.axis_size(axis)
    pairs = [(i, i + by) for i in range(devices) if 0 <= i + by < devices]
    return lax.ppermute(value, axis, pairs)


def conv_silu(padded, kernel_cols, offset_cols):
    span = kernel_cols.shape[0]
    count_rows = padded.shape[0] - span + 1
    summed = offset_cols[None, :] + jnp.zeros((count_rows, offset_cols.shape[0]), jnp.float32)
    for tap_index in range(span):
        summed = (
            summed + kernel_cols[tap_index][None, :] * padded[tap_index : tap_index + count_rows]
        )
    return jax.nn.silu(summed)


def conv_all(x_full, b_full, c_full, kernel, offset):
    x_width = x_full.shape[1]
    b_width = b_full.shape[1]
    x_out = conv_silu(x_full, kernel[:, :x_width], offset[:x_width])
    b_out = conv_silu(
        b_full, kernel[:, x_width : x_width + b_width], offset[x_width : x_width + b_width]
    )
    c_out = conv_silu(c_full, kernel[:, x_width + b_width :], offset[x_width + b_width :])
    return (x_out, b_out, c_out)


def product(form, left, right):
    return jnp.einsum(form, left, right, preferred_element_type=jnp.float32)


def ssd_block(x_heads, dt_heads, b_group, c_group, alog_heads, dtbias_heads, skip_heads):
    length = x_heads.shape[0]
    nheads = dt_heads.shape[1]
    states = b_group.shape[1]
    hwidth = x_heads.shape[1] // nheads
    blocks = length // Q
    step_size = jax.nn.softplus(dt_heads.astype(jnp.float32) + dtbias_heads[None, :])
    steps_t = jnp.transpose(step_size).reshape(nheads, blocks, Q)
    log_t = steps_t * (-jnp.exp(alog_heads))[:, None, None]
    running = jnp.cumsum(log_t, axis=2)
    x_blocks = x_heads.reshape(blocks, Q, nheads * hwidth)
    b_blocks = b_group.reshape(blocks, Q, states)
    c_blocks = c_group.reshape(blocks, Q, states)
    scores = product("cqn,ckn->cqk", c_blocks, b_blocks)
    causal = (jnp.arange(Q)[:, None] >= jnp.arange(Q)[None, :])[None, None, :, :]
    spread_log = jnp.where(causal, running[:, :, :, None] - running[:, :, None, :], -1e30)
    mixing = (scores[None] * jnp.exp(spread_log) * steps_t[:, :, None, :]).astype(jnp.bfloat16)
    within = product("hcqk,ckhp->cqhp", mixing, x_blocks.reshape(blocks, Q, nheads, hwidth))
    to_end = jnp.exp(running[:, :, -1:] - running)
    factor = jnp.transpose(steps_t * to_end, (1, 2, 0))
    x_wide = x_blocks.astype(jnp.float32).reshape(blocks, Q, nheads, hwidth)
    weighted = (
        (x_wide * factor[:, :, :, None]).astype(jnp.bfloat16).reshape(blocks, Q, nheads * hwidth)
    )
    block_states = product("ckn,ckm->cnm", b_blocks, weighted)
    totals = running[:, :, -1]
    before = jnp.cumsum(totals, axis=1) - totals
    earlier = (jnp.arange(blocks)[:, None] > jnp.arange(blocks)[None, :])[None, :, :]
    gap_log = jnp.where(
        earlier, before[:, :, None] - before[:, None, :] - totals[:, None, :], -1e30
    )
    carried = jnp.exp(gap_log)
    entering = jnp.einsum(
        "hcd,dnhp->cnhp",
        carried,
        block_states.reshape(blocks, states, nheads, hwidth),
        precision=lax.Precision.HIGHEST,
    )
    entering_low = entering.reshape(blocks, states, nheads * hwidth).astype(jnp.bfloat16)
    across = product("cqn,cnm->cqm", c_blocks, entering_low).reshape(blocks, Q, nheads, hwidth)
    across = across * jnp.transpose(jnp.exp(running), (1, 2, 0))[:, :, :, None]
    skipped = skip_heads[None, None, :, None] * x_wide
    return (within + across + skipped).reshape(length, nheads * hwidth)


def per_device(
    ssm_input,
    b_input,
    c_input,
    dt_input,
    conv_weight,
    conv_bias,
    a_log,
    dt_bias,
    skip_gain,
    grad_out,
):
    x_rows = ssm_input[0]
    b_rows = b_input[0]
    c_rows = c_input[0]
    dt_rows = dt_input[0]
    dy_rows = grad_out[0]
    edge = conv_weight.shape[0] - 1
    devices = lax.axis_size("sp")
    my_index = lax.axis_index("sp")
    groups = b_rows.shape[1] // N
    group_devs = devices // groups
    tok_rows = x_rows.shape[0]
    rims = passed_along(
        (x_rows[tok_rows - edge :], b_rows[tok_rows - edge :], c_rows[tok_rows - edge :]), "sp", 1
    )
    x_full = jnp.concatenate([rims[0], x_rows], 0).astype(jnp.float32)
    b_full = jnp.concatenate([rims[1], b_rows], 0).astype(jnp.float32)
    c_full = jnp.concatenate([rims[2], c_rows], 0).astype(jnp.float32)
    conv_outs, conv_back = jax.vjp(conv_all, x_full, b_full, c_full, conv_weight, conv_bias)
    x_conv = conv_outs[0].astype(jnp.bfloat16)
    b_conv = conv_outs[1].astype(jnp.bfloat16)
    c_conv = conv_outs[2].astype(jnp.bfloat16)
    b_copies = jnp.broadcast_to(
        b_conv.reshape(tok_rows, groups, 1, N), (tok_rows, groups, group_devs, N)
    ).reshape(tok_rows, groups * group_devs * N)
    c_copies = jnp.broadcast_to(
        c_conv.reshape(tok_rows, groups, 1, N), (tok_rows, groups, group_devs, N)
    ).reshape(tok_rows, groups * group_devs * N)
    x_heads, dt_heads, b_group, c_group, dy_heads = (
        lax.all_to_all(x_conv, "sp", split_axis=1, concat_axis=0, tiled=True),
        lax.all_to_all(dt_rows, "sp", split_axis=1, concat_axis=0, tiled=True),
        lax.all_to_all(b_copies, "sp", split_axis=1, concat_axis=0, tiled=True),
        lax.all_to_all(c_copies, "sp", split_axis=1, concat_axis=0, tiled=True),
        lax.all_to_all(dy_rows, "sp", split_axis=1, concat_axis=0, tiled=True),
    )
    per_dev = dt_heads.shape[1]
    first_head = my_index * per_dev
    alog_heads = lax.dynamic_slice_in_dim(a_log, first_head, per_dev)
    dtbias_heads = lax.dynamic_slice_in_dim(dt_bias, first_head, per_dev)
    skip_heads = lax.dynamic_slice_in_dim(skip_gain, first_head, per_dev)
    y_heads, ssd_back = jax.vjp(
        ssd_block, x_heads, dt_heads, b_group, c_group, alog_heads, dtbias_heads, skip_heads
    )
    y_low = y_heads.astype(jnp.bfloat16)
    gx_heads, gdt_heads, gb_heads, gc_heads, galog, gdtbias, gskip = ssd_back(
        dy_heads.astype(jnp.float32)
    )
    y_rows, gx_rows, gdt_rows, gb_rows, gc_rows = (
        lax.all_to_all(y_low, "sp", split_axis=0, concat_axis=1, tiled=True),
        lax.all_to_all(gx_heads, "sp", split_axis=0, concat_axis=1, tiled=True),
        lax.all_to_all(gdt_heads, "sp", split_axis=0, concat_axis=1, tiled=True),
        lax.all_to_all(gb_heads, "sp", split_axis=0, concat_axis=1, tiled=True),
        lax.all_to_all(gc_heads, "sp", split_axis=0, concat_axis=1, tiled=True),
    )
    gb_sum = (
        gb_rows.astype(jnp.float32)
        .reshape(tok_rows, groups, group_devs, N)
        .sum(axis=2)
        .reshape(tok_rows, groups * N)
    )
    gc_sum = (
        gc_rows.astype(jnp.float32)
        .reshape(tok_rows, groups, group_devs, N)
        .sum(axis=2)
        .reshape(tok_rows, groups * N)
    )
    d_xfull, d_bfull, d_cfull, d_kernel, d_offset = conv_back(
        (gx_rows.astype(jnp.float32), gb_sum, gc_sum)
    )
    rim_back = passed_along((d_xfull[:edge], d_bfull[:edge], d_cfull[:edge]), "sp", -1)
    grad_x = d_xfull[edge:].at[tok_rows - edge :].add(rim_back[0]).astype(jnp.bfloat16)
    grad_b = d_bfull[edge:].at[tok_rows - edge :].add(rim_back[1]).astype(jnp.bfloat16)
    grad_c = d_cfull[edge:].at[tok_rows - edge :].add(rim_back[2]).astype(jnp.bfloat16)
    head_terms = jnp.stack([galog, gdtbias, gskip])
    kernel_total, offset_total = lax.psum((d_kernel, d_offset), ("dp", "sp"))
    head_total = lax.psum(head_terms, "dp")
    return (
        y_rows[None],
        grad_x[None],
        grad_b[None],
        grad_c[None],
        gdt_rows[None],
        kernel_total,
        offset_total,
        head_total,
    )


def solution(mesh):
    in_specs = (
        P("dp", "sp", None),
        P("dp", "sp", None),
        P("dp", "sp", None),
        P("dp", "sp", None),
        P(),
        P(),
        P(),
        P(),
        P(),
        P("dp", "sp", None),
    )
    out_specs = (
        P("dp", "sp", None),
        P("dp", "sp", None),
        P("dp", "sp", None),
        P("dp", "sp", None),
        P("dp", "sp", None),
        P(),
        P(),
        P(None, "sp"),
    )
    return jax.shard_map(
        per_device, mesh=mesh, in_specs=in_specs, out_specs=out_specs, check_vma=False
    )
```

profile of v0, /device:TPU:0, one launch (start us, length us, event | category | flops | bytes accessed | tf_op | source)
XLA Modules:
  0.0 685.9 jit_solution(11815102494471192315)
XLA Ops:
  8.7 7.3 %all-to-all-start.3 = ((bf16[128,8,16]{0,2,1:T(8,128)(2,1)}), bf16[128,8,16]{0,2,1:T(8,128)(2,1)S(1)}, u32[]{:S(2)}, u32[]{:S(2)}) async-start(bf16[128,8,16]{0,2,1:T(8,128)(2,1)} %bitcast.27), calls=%async_computation.3 | async-start | bytes 65536 | tf_op jit(solution)/shard_map/all_to_all | solution.py:128
  29.4 6.4 all-to-all-start.2
  40.2 6.3 collective-permute-done.1
  50.8 10.8 %all-to-all-start.1 = ((bf16[128,8,256]{2,0,1:T(8,128)(2,1)}), bf16[128,8,256]{2,0,1:T(8,128)(2,1)S(1)}, u32[]{:S(2)}, u32[]{:S(2)}) async-start(bf16[128,8,256]{2,0,1:T(8,128)(2,1)} %bitcast.16), calls=%async_computation.1 | async-start | bytes 1048576 | tf_op jit(solution)/shard_map/all_to_all | solution.py:130
  69.6 6.0 all-to-all-done.1
  105.2 22.9 %all-to-all-done.5 = bf16[128,8,1024]{2,0,1:T(8,128)(2,1)S(1)} async-done(((bf16[128,8,1024]{2,0,1:T(8,128)(2,1)}), bf16[128,8,1024]{2,0,1:T(8,128)(2,1)S(1)}, u32[]{:S(2)}, u32[]{:S(2)}) %all-to-all-start.5) | async-done | bytes 2097184 | tf_op jit(solution)/shard_map/all_to_all | solution.py:131
  145.0 6.9 %copy.437 = bf16[8,256,1024]{1,0,2:T(8,128)(2,1)} copy(bf16[8,256,1024]{2,1,0:T(8,128)(2,1)} %fusion.26) | data formatting | bytes 8388608 | tf_op jit(solution)/shard_map/transpose(jvp(hcd,dnhp->cnhp))/transpose | solution.py:74
  152.0 7.7 %fusion.63 = bf16[16,256,64,8]{1,3,2,0:T(8,128)(2,1)} fusion(bf16[16,256,64,8]{1,3,2,0:T(8,128)(2,1)} %bitcast.306, f32[16,8]{1,0:T(8,128)S(1)} %bitcast.331, f32[16,8]{1,0:T(8,128)S(1)} %copy.382, f32[16,8]{1,0:T(8,128)S(1)} %copy.381, pred[8,8]{1,0:T(8,128)(4,1)S(1)} %iota_compare_fusion.1), kind=kOutput, calls=%fused_computation.143 | convolution fusion | flops 201329664 | bytes 8390208 | tf_op jit(solution)/shard_map/transpose(jvp(hcd,dnhp->cnhp))/dot_general | solution.py:74
  159.7 6.8 copy.396
  166.4 8.2 %fusion.30 = (bf16[8,128,1024]{2,1,0:T(8,128)(2,1)}, f32[8,128,1024]{2,1,0:T(8,128)}) fusion(bf16[8,128,1024]{2,1,0:T(8,128)(2,1)} %copy.399, f32[8,128,1024]{2,1,0:T(8,128)} %copy.378, f32[1024]{0:T(1024)S(1)} %mul.487, bf16[128,8,1024]{2,0,1:T(8,128)(2,1)S(1)} %all-to-all-done.5, bf16[8,256,1024]{2,1,0:T(8,128)(2,1)} %copy.396, ...), kind=kOutput, calls=%fused_computation.55 | convolution fusion | flops 544210944 | bytes 19402752 | tf_op jit(solution)/shard_map/transpose(jvp(ckn,ckm->cnm))/dot_general | solution.py:39
  189.5 8.0 %collective-permute-done = bf16[3,8192]{1,0:T(4,128)(2,1)S(1)} collective-permute-done((bf16[3,8192]{1,0:T(4,128)(2,1)S(1)}, bf16[3,8192]{1,0:T(4,128)(2,1)S(1)}, u32[]{:S(2)}, u32[]{:S(2)}) %collective-permute-start) | collective-permute-done | bytes 49184 | tf_op jit(solution)/shard_map/ppermute | solution.py:13
  199.4 6.9 %maximum_convert_fusion = f32[131,8192]{0,1:T(8,128)} fusion(bf16[128,8192]{0,1:T(8,128)(2,1)} %bitcast.319, bf16[3,8192]{0,1:T(8,128)(2,1)} %copy.361), kind=kLoop, calls=%fused_computation.35 | loop fusion | flops 4292608 | bytes 6438912 | tf_op jit(solution)/shard_map/convert_element_type | solution.py:113
  211.6 15.2 %all-to-all-done.6 = bf16[8,128,1024]{2,1,0:T(8,128)(2,1)} async-done(((bf16[8,128,1024]{2,1,0:T(8,128)(2,1)}), bf16[8,128,1024]{2,1,0:T(8,128)(2,1)}, u32[]{:S(2)}, u32[]{:S(2)}) %all-to-all-start.6) | async-done | bytes 2097184 | tf_op jit(solution)/shard_map/all_to_all | solution.py:147
  236.3 25.0 %multiply_reduce_fusion.3 = (f32[8192]{0:T(1024)S(1)}, f32[8192]{0:T(1024)S(1)}, f32[8192]{0:T(1024)S(1)}, f32[8192]{0:T(1024)}, f32[8192]{0:T(1024)}, /*index=5*/f32[128,8192]{0,1:T(8,128)}, f32[128,8192]{0,1:T(8,128)S(1)}) fusion(f32[131,8192]{0,1:T(8,128)} %maximum_convert_fusion, f32[128,8,1024]{0,2,1:T(8,128)} %copy.400, f32[8192]{0:T(1024)S(1)} %bitcast.339, ...), kind=kLoop, calls=%fused_computation.43 | loop fusion | flops 27222016 | bytes 29687808 | tf_op jit(solution)/shard_map/transpose(jvp())/reduce_sum | solution.py:22
  267.6 18.1 %all-to-all-start = ((bf16[128,8,1024]{2,0,1:T(8,128)(2,1)}), bf16[128,8,1024]{2,0,1:T(8,128)(2,1)}, u32[]{:S(2)}, u32[]{:S(2)}) async-start(bf16[128,8,1024]{2,0,1:T(8,128)(2,1)} %copy.362), calls=%async_computation | async-start | bytes 4194304 | tf_op jit(solution)/shard_map/all_to_all | solution.py:127
  285.7 6.0 broadcast_multiply_fusion
  291.8 6.6 pad_add_fusion
  328.4 22.6 %scatter-add.10 = bf16[128,8192]{0,1:T(8,128)(2,1)} dynamic-update-slice(bf16[128,8192]{0,1:T(8,128)(2,1)} %slice.254, bf16[3,8192]{0,1:T(8,128)(2,1)} %slice_add_fusion, s32[]{:T(128)} %constant.107.clone.1, s32[]{:T(128)} %constant.103.clone.1) | dynamic-update-slice | bytes 98308 | tf_op jit(solution)/shard_map/scatter-add | solution.py:168
  359.6 13.3 %fusion.97 = (f32[16,8]{1,0:T(8,128)}, f32[16,8]{1,0:T(8,128)}) fusion(f32[16,8]{1,0:T(8,128)S(1)} %bitcast.332, f32[16,8]{1,0:T(8,128)S(1)} %copy-done.24, f32[16,8]{1,0:T(8,128)S(1)} %copy.381, bf16[16,256,64,8]{1,3,2,0:T(8,128)(2,1)S(1)} %bitcast.307, f32[8,256,16,64]{1,3,2,0:T(8,128)S(1)} %bitcast.303, pred[8,8]{1,0:T(8,128)(4,1)S(1)} %copy-done.49), kind=kOutput, calls=%fused_computation.197 | convolution fusion | flops 201333504 | bytes 12585536 | tf_op jit(solution)/shard_map/transpose(jvp(hcd,dnhp->cnhp))/dot_general | solution.py:74
  372.9 12.0 %fusion.27 = bf16[16,256,64,8]{1,3,2,0:T(8,128)(2,1)} fusion(f32[8,256,16,64]{1,3,2,0:T(8,128)S(1)} %bitcast.304, f32[16,8]{1,0:T(8,128)S(1)} %bitcast.333, f32[16,8]{1,0:T(8,128)S(1)} %copy-done.24, f32[16,8]{1,0:T(8,128)S(1)} %copy.381, pred[8,8]{1,0:T(8,128)(4,1)S(1)} %copy-done.49), kind=kOutput, calls=%fused_computation.54 | convolution fusion | flops 203426816 | bytes 12584512 | tf_op jit(solution)/shard_map/jvp(hcd,dnhp->cnhp)/dot_general | solution.py:74
  388.8 10.2 %fusion.12 = (f32[16,8,128]{2,0,1:T(8,128)}, f32[16,8,128]{2,0,1:T(8,128)}, f32[16,8,128]{2,0,1:T(8,128)}, bf16[8,128,128]{2,1,0:T(8,128)(2,1)S(1)}) fusion(f32[16,8,128]{2,0,1:T(8,128)} %bitcast.353, f32[16,8,128]{2,0,1:T(8,128)} %copy.372, f32[8,128,128]{2,1,0:T(8,128)} %fusion.52, pred[128,128]{1,0:T(8,128)(4,1)} %copy-done.46, ...), kind=kOutput, calls=%fused_computation.17 | convolution fusion | flops 299712512 | bytes 5324800 | tf_op jit(solution)/shard_map/transpose(jvp(hcqk,ckhp->cqhp))/dot_general | solution.py:39
  399.0 7.1 %copy.385 = bf16[8,256,1024]{2,1,0:T(8,128)(2,1)} copy(bf16[8,256,1024]{1,0,2:T(8,128)(2,1)} %bitcast.309) | data formatting | bytes 8388608 | tf_op jit(solution)/shard_map/jvp()/convert_element_type | solution.py:80
  421.4 6.7 multiply_reduce_fusion.4
  428.9 21.1 %reduce_window_sum.52 = f32[16,8,128]{2,1,0:T(8,128)} reduce-window(f32[16,8,128]{2,1,0:T(8,128)} %fusion.70, f32[]{:T(128)} %constant.105.clone.1), window={size=1x1x128 pad=0_0x0_0x0_127}, to_apply=%region_14.15 | reduce-window | flops 2080768 | bytes 131076 | tf_op jit(solution)/shard_map/transpose(jvp(jit(cumsum)))/reduce_window_sum | solution.py:51
  453.1 20.9 %all-to-all-start.9 = ((bf16[8,128,16]{1,2,0:T(8,128)(2,1)}), bf16[8,128,16]{1,2,0:T(8,128)(2,1)S(1)}, u32[]{:S(2)}, u32[]{:S(2)}) async-start(bf16[8,128,16]{1,2,0:T(8,128)(2,1)} %copy_bitcast_fusion.1), calls=%async_computation.9 | async-start | bytes 65536 | tf_op jit(solution)/shard_map/all_to_all | solution.py:148
  483.6 6.0 all-to-all-start.7
  496.0 7.3 %all-to-all-done.7 = bf16[8,128,256]{2,1,0:T(8,128)(2,1)} async-done(((bf16[8,128,256]{2,1,0:T(8,128)(2,1)}), bf16[8,128,256]{2,1,0:T(8,128)(2,1)}, u32[]{:S(2)}, u32[]{:S(2)}) %all-to-all-start.7) | async-done | bytes 524320 | tf_op jit(solution)/shard_map/all_to_all | solution.py:149
  507.1 7.1 %fusion.15 = bf16[8,128,16,64]{1,3,2,0:T(8,128)(2,1)} fusion(bf16[8,128,16,64]{1,3,2,0:T(8,128)(2,1)} %bitcast.313, f32[8,128,16,64]{1,3,2,0:T(8,128)} %bitcast.320, f32[16]{0:T(128)S(1)} %copy-done.56, f32[8,128,16]{1,2,0:T(8,128)S(1)} %copy-done.17, f32[16,8,128]{2,0,1:T(8,128)} %bitcast.354, f32[16,8,128]{2,0,1:T(8,128)} %copy.372, ...), kind=kOutput, calls=%fused_computation.27 | convolution fusion | flops 285212672 | bytes 9125952 | tf_op jit(solution)/shard_map/jvp(hcqk,ckhp->cqhp)/dot_general | solution.py:39
  514.2 6.6 all-to-all-done.8
  525.3 6.4 psum.23
  547.2 74.8 %psum.22 = f32[10240]{0:T(1024)} all-reduce(f32[10240]{0:T(1024)S(1)} %pad_add_fusion.5), channel_id=1, replica_groups=mesh['dp'=4,'sp'=8] {'dp','sp'}, use_global_device_ids=true, to_apply=%region_31.32 | all-reduce | flops 10240 | bytes 81920 | tf_op jit(solution)/shard_map/psum | solution.py:172
  633.7 43.6 %all-reduce.34.cloned.1.call-done = f32[4,10240]{1,0:T(4,128)} async-done(((f32[4,10240]{1,0:T(4,128)}), f32[4,10240]{1,0:T(4,128)}) %all-reduce.34.cloned.1.call-update) | async-done | bytes 163856 | tf_op jit(solution)/shard_map/psum | solution.py:172
  (264 shorter events, 229.7 us)
Async XLA Ops:
  7.2 28.7 %copy-start.18 = (bf16[1,128,1024]{2,1,0:T(8,128)(2,1)S(1)}, bf16[1,128,1024]{2,1,0:T(8,128)(2,1)}, u32[]{:S(2)}) copy-start(bf16[1,128,1024]{2,1,0:T(8,128)(2,1)} %param.18) | copy-start | bytes 786436
  8.7 19.9 %all-to-all-start.3 = ((bf16[128,8,16]{0,2,1:T(8,128)(2,1)}), bf16[128,8,16]{0,2,1:T(8,128)(2,1)S(1)}, u32[]{:S(2)}, u32[]{:S(2)}) async-start(bf16[128,8,16]{0,2,1:T(8,128)(2,1)} %bitcast.27), calls=%async_computation.3 | async-start | bytes 65536 | tf_op jit(solution)/shard_map/all_to_all | solution.py:128
  17.2 9.0 %collective-permute-start.2 = (bf16[3,1024]{0,1:T(8,128)(2,1)S(1)}, bf16[3,1024]{0,1:T(8,128)(2,1)S(1)}, u32[]{:S(2)}, u32[]{:S(2)}) collective-permute-start(bf16[3,1024]{0,1:T(8,128)(2,1)S(1)} %slice_bitcast_fusion), channel_id=1, source_target_pairs={{0,1},{1,2},{2,3},{3,4},{4,5},{5,6},{6,7},{8,9},{9,10},{10,11},{11... | collective-permute-start | bytes 18440 | tf_op jit(solution)/shard_map/ppermute | solution.py:13
  22.2 24.5 %copy-start.29 = (f32[1,1024]{1,0:T(1,128)}, f32[1,1024]{1,0:T(1,128)S(1)}, u32[]{:S(2)}) copy-start(f32[1,1024]{1,0:T(1,128)S(1)} %get-tuple-element.139) | copy-start | bytes 12292
  22.2 24.5 %copy-start.31 = (f32[1,1024]{1,0:T(1,128)}, f32[1,1024]{1,0:T(1,128)S(1)}, u32[]{:S(2)}) copy-start(f32[1,1024]{1,0:T(1,128)S(1)} %get-tuple-element.142) | copy-start | bytes 12292
  22.2 24.5 %copy-start.33 = (f32[1,1024]{1,0:T(1,128)}, f32[1,1024]{1,0:T(1,128)S(1)}, u32[]{:S(2)}) copy-start(f32[1,1024]{1,0:T(1,128)S(1)} %get-tuple-element.143) | copy-start | bytes 12292
  22.2 24.5 %copy-start.35 = (f32[1,1024]{1,0:T(1,128)}, f32[1,1024]{1,0:T(1,128)S(1)}, u32[]{:S(2)}) copy-start(f32[1,1024]{1,0:T(1,128)S(1)} %get-tuple-element.144) | copy-start | bytes 12292
  28.6 52.4 %copy-start.13 = (bf16[128,8,16]{0,2,1:T(8,128)(2,1)}, bf16[128,8,16]{0,2,1:T(8,128)(2,1)S(1)}, u32[]{:S(2)}) copy-start(bf16[128,8,16]{0,2,1:T(8,128)(2,1)S(1)} %all-to-all-done.3) | copy-start | bytes 98308
  29.4 20.3 %all-to-all-start.2 = ((bf16[128,8,256]{2,0,1:T(8,128)(2,1)}), bf16[128,8,256]{2,0,1:T(8,128)(2,1)S(1)}, u32[]{:S(2)}, u32[]{:S(2)}) async-start(bf16[128,8,256]{2,0,1:T(8,128)(2,1)} %bitcast.25), calls=%async_computation.2 | async-start | bytes 1048576 | tf_op jit(solution)/shard_map/all_to_all | solution.py:129
  36.2 10.2 %collective-permute-start.1 = (bf16[3,1024]{0,1:T(8,128)(2,1)S(1)}, bf16[3,1024]{0,1:T(8,128)(2,1)S(1)}, u32[]{:S(2)}, u32[]{:S(2)}) collective-permute-start(bf16[3,1024]{0,1:T(8,128)(2,1)S(1)} %slice_bitcast_fusion.1), channel_id=1, source_target_pairs={{0,1},{1,2},{2,3},{3,4},{4,5},{5,6},{6,7},{8,9},{9,10},{10,11},{11... | collective-permute-start | bytes 18440 | tf_op jit(solution)/shard_map/ppermute | solution.py:13
  50.8 24.8 %all-to-all-start.1 = ((bf16[128,8,256]{2,0,1:T(8,128)(2,1)}), bf16[128,8,256]{2,0,1:T(8,128)(2,1)S(1)}, u32[]{:S(2)}, u32[]{:S(2)}) async-start(bf16[128,8,256]{2,0,1:T(8,128)(2,1)} %bitcast.16), calls=%async_computation.1 | async-start | bytes 1048576 | tf_op jit(solution)/shard_map/all_to_all | solution.py:130
  76.4 51.7 %all-to-all-start.5 = ((bf16[128,8,1024]{2,0,1:T(8,128)(2,1)}), bf16[128,8,1024]{2,0,1:T(8,128)(2,1)S(1)}, u32[]{:S(2)}, u32[]{:S(2)}) async-start(bf16[128,8,1024]{2,0,1:T(8,128)(2,1)} %copy.390), calls=%async_computation.5 | async-start | bytes 4194304 | tf_op jit(solution)/shard_map/all_to_all | solution.py:131
  81.0 71.0 %copy-start.48 = (pred[8,8]{1,0:T(8,128)(4,1)}, pred[8,8]{1,0:T(8,128)(4,1)S(1)}, u32[]{:S(2)}) copy-start(pred[8,8]{1,0:T(8,128)(4,1)S(1)} %iota_compare_fusion.1) | copy-start | bytes 196
  81.0 49.5 %copy-start.46 = (pred[128,128]{1,0:T(8,128)(4,1)}, pred[128,128]{1,0:T(8,128)(4,1)S(1)}, u32[]{:S(2)}) copy-start(pred[128,128]{1,0:T(8,128)(4,1)S(1)} %iota_compare_fusion) | copy-start | bytes 49156
  87.0 65.0 %copy-start.23 = (f32[16,8]{1,0:T(8,128)}, f32[16,8]{1,0:T(8,128)S(1)}, u32[]{:S(2)}) copy-start(f32[16,8]{1,0:T(8,128)S(1)} %copy.382) | copy-start | bytes 1540
  102.9 27.6 %copy-start.25 = (f32[16,8,128]{2,0,1:T(8,128)S(1)}, f32[16,8,128]{2,0,1:T(8,128)}, u32[]{:S(2)}) copy-start(f32[16,8,128]{2,0,1:T(8,128)} %copy.372) | copy-start | bytes 196612
  102.9 27.6 %copy-start.26 = (f32[2,8,8,128]{3,2,0,1:T(8,128)S(1)}, f32[2,8,8,128]{3,2,0,1:T(8,128)}, u32[]{:S(2)}) copy-start(f32[2,8,8,128]{3,2,0,1:T(8,128)} %copy.494) | copy-start | bytes 196612
  174.6 52.2 %all-to-all-start.6 = ((bf16[8,128,1024]{2,1,0:T(8,128)(2,1)}), bf16[8,128,1024]{2,1,0:T(8,128)(2,1)}, u32[]{:S(2)}, u32[]{:S(2)}) async-start(bf16[8,128,1024]{2,1,0:T(8,128)(2,1)} %get-tuple-element.153), calls=%async_computation.6 | async-start | bytes 4194304 | tf_op jit(solution)/shard_map/all_to_all | solution.py:147
  180.0 17.6 %collective-permute-start = (bf16[3,8192]{1,0:T(4,128)(2,1)S(1)}, bf16[3,8192]{1,0:T(4,128)(2,1)S(1)}, u32[]{:S(2)}, u32[]{:S(2)}) collective-permute-start(bf16[3,8192]{1,0:T(4,128)(2,1)S(1)} %slice_bitcast_fusion.2), channel_id=1, source_target_pairs={{0,1},{1,2},{2,3},{3,4},{4,5},{5,6},{6,7},{8,9},{9,10},{10,11},{11... | collective-permute-start | bytes 147464 | tf_op jit(solution)/shard_map/ppermute | solution.py:13
  267.6 87.5 %all-to-all-start = ((bf16[128,8,1024]{2,0,1:T(8,128)(2,1)}), bf16[128,8,1024]{2,0,1:T(8,128)(2,1)}, u32[]{:S(2)}, u32[]{:S(2)}) async-start(bf16[128,8,1024]{2,0,1:T(8,128)(2,1)} %copy.362), calls=%async_computation | async-start | bytes 4194304 | tf_op jit(solution)/shard_map/all_to_all | solution.py:127
  306.7 13.1 %collective-permute-start.3 = (f32[3,8192]{1,0:T(4,128)S(1)}, f32[3,8192]{1,0:T(4,128)}, u32[]{:S(2)}, u32[]{:S(2)}) collective-permute-start(f32[3,8192]{1,0:T(4,128)S(1)} %copy.401), channel_id=1, source_target_pairs={{1,0},{2,1},{3,2},{4,3},{5,4},{6,5},{7,6},{9,8},{10,9},{11,10},{12... | collective-permute-start | bytes 294920 | tf_op jit(solution)/shard_map/ppermute | solution.py:13
  421.4 28.6 %copy-start.9 = (f32[8,128,16]{1,2,0:T(8,128)S(1)}, f32[8,128,16]{1,2,0:T(8,128)}, u32[]{:S(2)}) copy-start(f32[8,128,16]{1,2,0:T(8,128)} %copy-done.8) | copy-start | bytes 196612
  421.4 28.6 %copy-start.53 = (f32[16]{0:T(128)S(1)}, f32[16]{0:T(128)}, u32[]{:S(2)}) copy-start(f32[16]{0:T(128)} %copy-done.52) | copy-start | bytes 196
  421.4 29.6 %copy-start.51 = (f32[16]{0:T(128)S(1)}, f32[16]{0:T(128)}, u32[]{:S(2)}) copy-start(f32[16]{0:T(128)} %copy-done.50) | copy-start | bytes 196
  453.1 30.4 %all-to-all-start.9 = ((bf16[8,128,16]{1,2,0:T(8,128)(2,1)}), bf16[8,128,16]{1,2,0:T(8,128)(2,1)S(1)}, u32[]{:S(2)}, u32[]{:S(2)}) async-start(bf16[8,128,16]{1,2,0:T(8,128)(2,1)} %copy_bitcast_fusion.1), calls=%async_computation.9 | async-start | bytes 65536 | tf_op jit(solution)/shard_map/all_to_all | solution.py:148
  483.6 19.7 %all-to-all-start.7 = ((bf16[8,128,256]{2,1,0:T(8,128)(2,1)}), bf16[8,128,256]{2,1,0:T(8,128)(2,1)}, u32[]{:S(2)}, u32[]{:S(2)}) async-start(bf16[8,128,256]{2,1,0:T(8,128)(2,1)} %fusion.33), calls=%async_computation.7 | async-start | bytes 1048576 | tf_op jit(solution)/shard_map/all_to_all | solution.py:149
  489.8 17.2 %copy-start.17 = (f32[8,128,16]{1,2,0:T(8,128)S(1)}, f32[8,128,16]{1,2,0:T(8,128)}, u32[]{:S(2)}) copy-start(f32[8,128,16]{1,2,0:T(8,128)} %copy-done.16) | copy-start | bytes 196612
  503.3 17.5 %all-to-all-start.8 = ((bf16[8,128,256]{2,1,0:T(8,128)(2,1)}), bf16[8,128,256]{2,1,0:T(8,128)(2,1)S(1)}, u32[]{:S(2)}, u32[]{:S(2)}) async-start(bf16[8,128,256]{2,1,0:T(8,128)(2,1)} %fusion.34), calls=%async_computation.8 | async-start | bytes 1048576 | tf_op jit(solution)/shard_map/all_to_all | solution.py:150
  520.7 108.9 %all-to-all-start.4 = ((bf16[8,128,1024]{1,2,0:T(8,128)(2,1)}), bf16[8,128,1024]{1,2,0:T(8,128)(2,1)}, u32[]{:S(2)}, u32[]{:S(2)}) async-start(bf16[8,128,1024]{1,2,0:T(8,128)(2,1)} %bitcast.323), calls=%async_computation.4 | async-start | bytes 4194304 | tf_op jit(solution)/shard_map/all_to_all | solution.py:146
  525.3 152.0 %all-reduce.34.cloned.1.call-start = ((), (), s32[]{:S(2)}) async-start(), calls=%async_computation.10 | async-start | bytes 327680 | tf_op jit(solution)/shard_map/psum | solution.py:172
  544.6 77.4 %collective-permute-start.4 = (f32[3,1024]{0,1:T(8,128)S(1)}, f32[3,1024]{0,1:T(8,128)}, u32[]{:S(2)}, u32[]{:S(2)}) collective-permute-start(f32[3,1024]{0,1:T(8,128)S(1)} %slice.259), channel_id=1, source_target_pairs={{1,0},{2,1},{3,2},{4,3},{5,4},{6,5},{7,6},{9,8},{10,9},{11,10},{12... | collective-permute-start | bytes 36872 | tf_op jit(solution)/shard_map/ppermute | solution.py:13
  545.9 77.2 %collective-permute-start.5 = (f32[3,1024]{0,1:T(8,128)}, f32[3,1024]{0,1:T(8,128)}, u32[]{:S(2)}, u32[]{:S(2)}) collective-permute-start(f32[3,1024]{0,1:T(8,128)} %slice.262), channel_id=1, source_target_pairs={{1,0},{2,1},{3,2},{4,3},{5,4},{6,5},{7,6},{9,8},{10,9},{11,10},{12... | collective-permute-start | bytes 36872 | tf_op jit(solution)/shard_map/ppermute | solution.py:13
  (47 other events, 337.8 us)
Sparse Core Ops, SparseCore 0:
  544.7 132.4 all-reduce.33
where the time goes:
time: 695 us; the launch traced here: 686 us
  local copies, waits for them, and re-layouts  153 us (22%)
  waiting for transfers between devices  125 us (18%)
  other arithmetic  115 us (17%)
  starting transfers between devices  102 us (15%)
  matrix products  95.5 us (14%)
  blocking collectives  81.2 us (12%)
  between operations  15.3 us (2%)
    psum x1, blocking collectives, per_device(): kernel_total, offset_total = lax.psum((d_kernel, d_offset), ('dp', 'sp'))  74.8 us
    dot_general x12, matrix products, product(): return jnp.einsum(form, left, right, preferred_element_type=jnp.float32)  62.5 us
    psum x1, waiting for transfers between devices, per_device(): kernel_total, offset_total = lax.psum((d_kernel, d_offset), ('dp', 'sp'))  43.6 us
    dot_general x3, matrix products, ssd_block(): jnp.einsum('hcd,dnhp->cnhp', carried, block_states.reshape(blocks, states...  33 us
    reduce_sum x2, other arithmetic, conv_silu(): kernel_cols[tap_index][None, :] * padded[tap_index:tap_index + count_rows]  28.8 us
    unnamed x134, local copies, waits for them, and re-layouts  25.8 us
    another operation x2, other arithmetic, ssd_block(): running = jnp.cumsum(log_t, axis=2)  25.6 us
    ppermute x6, waiting for transfers between devices, passed_along(): return lax.ppermute(value, axis, pairs)  23.1 us
  transfers between devices with their start and end apart: 17, of which 10 were waited for; matrix products, arithmetic and copies ran while one was open for 24% of the time, Pallas kernels for 0%

commit v1 on v0

v1 whole, which is shorter than its diff:
```python
import functools

import jax
import jax.numpy as jnp
from jax import lax
from jax.experimental import pallas as pl
from jax.experimental.pallas import tpu as pltpu
from jax.sharding import PartitionSpec as P

N = 256
Q = 128
HEAD = 64
SUB = 256
LOG2E = 1.4426950408889634
F32 = jnp.float32
BF16 = jnp.bfloat16
NEG = -1e30


def params():
    return pltpu.CompilerParams(vmem_limit_bytes=40 * 1024 * 1024)


def cost(micros, nbytes):
    return pl.CostEstimate(flops=int(micros * 1e9), bytes_accessed=nbytes, transcendentals=0)


def dot(a, b):
    return jnp.dot(a, b, preferred_element_type=F32)


def dot_tb(a, b):
    return lax.dot_general(a, b, (((1,), (1,)), ((), ())), preferred_element_type=F32)


def dot_ta(a, b):
    return lax.dot_general(a, b, (((0,), (0,)), ((), ())), preferred_element_type=F32)


def halves(v):
    hi = v.astype(BF16)
    return hi, (v - hi.astype(F32)).astype(BF16)


def split_dot(v, m):
    hi, lo = halves(v)
    return dot(hi, m) + dot(lo, m)


def exact_dot(m, v):
    hi = v.astype(BF16)
    rest = v - hi.astype(F32)
    mid = rest.astype(BF16)
    low = (rest - mid.astype(F32)).astype(BF16)
    return dot(m, hi) + dot(m, mid) + dot(m, low)


def triangle(lower):
    row = lax.broadcasted_iota(jnp.int32, (Q, Q), 0)
    col = lax.broadcasted_iota(jnp.int32, (Q, Q), 1)
    return row >= col if lower else row <= col


def in_order(y, own, rec, dst, first=0):
    rows = own.shape[0]

    @pl.when(y == 0)
    def _():
        dst[first : first + rows] = own.astype(dst.dtype)
        dst[first + rows : first + 2 * rows] = rec.astype(dst.dtype)

    @pl.when(y != 0)
    def _():
        dst[first : first + rows] = rec.astype(dst.dtype)
        dst[first + rows : first + 2 * rows] = own.astype(dst.dtype)


def conv_sum(xs, w, rows):
    total = w[4:5]
    for k in range(4):
        total = total + w[k : k + 1] * xs[5 + k : 5 + k + rows]
    return total


def conv_back(g, s, xs, gs, w, rows):
    sig = 1.0 / (1.0 + jnp.exp(-s))
    ds = g * (sig * (1.0 + s * (1.0 - sig)))
    gs[0:rows] = ds
    gs[rows : rows + 8] = jnp.zeros((8, ds.shape[1]), F32)
    dx = w[3:4] * ds
    for k in range(3):
        dx = dx + w[k : k + 1] * gs[3 - k : 3 - k + rows]
    dw = [jnp.sum(ds * xs[5 + k : 5 + k + rows], axis=0, keepdims=True) for k in range(4)]
    dw.append(jnp.sum(ds, axis=0, keepdims=True))
    dw.append(jnp.zeros((3, ds.shape[1]), F32))
    return dx, jnp.concatenate(dw, axis=0), ds[0:8]


def setup_kernel(
    yv, b_own, c_own, dt_own, rec, halo, w, par, exp2,
    bc_ref, cc_ref, fe_ref, rows_ref, cols_ref, rowt_ref, st_ref, xs, dts, xs2,
):
    y = yv[0]
    width = b_own.shape[1]
    heads = par.shape[1]
    for own, at, out in ((b_own, 0, bc_ref), (c_own, width, cc_ref)):
        xs[0:8] = halo[:, at : at + width]
        in_order(y, own[...], rec[:, at : at + width], xs, 8)
        s = conv_sum(xs, w[:, at : at + width], 2 * Q)
        out[...] = (s / (1.0 + jnp.exp(-s))).astype(BF16)

    @pl.when(y == 0)
    def _():
        dts[0:Q] = dt_own[:, 0:heads].astype(F32)
        dts[Q : 2 * Q] = rec[:, 2 * width : 2 * width + heads].astype(F32)

    @pl.when(y != 0)
    def _():
        dts[0:Q] = rec[:, 2 * width + heads : 2 * width + 2 * heads].astype(F32)
        dts[Q : 2 * Q] = dt_own[:, heads : 2 * heads].astype(F32)

    step = jnp.log1p(jnp.exp(dts[...] + par[1:2]))
    logs = -step * jnp.exp(par[0:1])
    tri = jnp.where(triangle(True), 1.0, 0.0).astype(BF16)
    run0 = exact_dot(tri, logs[0:Q])
    run1 = exact_dot(tri, logs[Q:])
    tot0, tot1 = run0[Q - 1 : Q], run1[Q - 1 : Q]
    run = jnp.concatenate([run0, run1], axis=0)
    to_end = jnp.concatenate([jnp.exp(tot0 - run0), jnp.exp(tot1 - run1)], axis=0)
    hi, lo = halves(step * to_end)
    fe_ref[0] = jnp.concatenate([hi, lo], axis=1)
    hi, lo = halves(jnp.exp(run))
    fe_ref[1] = jnp.concatenate([hi, lo], axis=1)
    st_ref[...] = step
    small = jnp.concatenate(
        [jnp.exp(tot0), jnp.exp(tot1), jnp.exp(tot0 + tot1), par[2:3], jnp.zeros((4, heads), F32)],
        axis=0,
    )
    hi, lo = halves(small)
    rows_ref[...] = dot(jnp.concatenate([hi, lo], axis=1), exp2[...])
    r2 = run * LOG2E
    q2 = (run - jnp.log(step)) * LOG2E
    both = jnp.concatenate([r2, q2], axis=1)
    xs2[...] = jnp.transpose(both)
    for j in range(heads // 4):
        cols_ref[j] = jnp.concatenate([r2[:, 4 * j : 4 * j + 4], q2[:, 4 * j : 4 * j + 4]], axis=1)
        rowt_ref[j] = jnp.concatenate(
            [xs2[4 * j : 4 * j + 4], xs2[heads + 4 * j : heads + 4 * j + 4]], axis=0
        )


def state_kernel(
    yv, x_own, dy_own, rec, halo, w, bc, cc, fe, exp2, rows, xc_ref, dyo_ref, t_ref, u_ref, xs
):
    y = yv[0]
    xs[0:8] = halo[...]
    in_order(y, x_own[...], rec[0], xs, 8)
    in_order(y, dy_own[...], rec[1], dyo_ref)
    s = conv_sum(xs, w, 2 * Q)
    xc = (s / (1.0 + jnp.exp(-s))).astype(BF16)
    xc_ref[...] = xc
    wt = (xc.astype(F32) * dot(fe[0], exp2[...])).astype(BF16)
    dyr = (dyo_ref[...].astype(F32) * dot(fe[1], exp2[...])).astype(BF16)
    t_ref[...] = (rows[1:2] * dot_ta(bc[0:Q], wt[0:Q]) + dot_ta(bc[Q:], wt[Q:])).astype(BF16)
    u_ref[...] = (dot_ta(cc[0:Q], dyr[0:Q]) + rows[0:1] * dot_ta(cc[Q:], dyr[Q:])).astype(BF16)


def within_kernel(xc, dyo, cols, rowt, bc, cc, yi_ref, dxi_ref, dcb_ref, cb):
    @pl.when(pl.program_id(0) == 0)
    def _():
        dcb_ref[...] = jnp.zeros(dcb_ref.shape, F32)
        for b in range(2):
            at = slice(b * Q, b * Q + Q)
            cb[b] = dot_tb(cc[at], bc[at])
            cb[2 + b] = dot_tb(bc[at], cc[at])

    low = triangle(True)
    high = triangle(False)
    lane = lax.broadcasted_iota(jnp.int32, (1, 2 * HEAD), 1)
    first = jnp.where(lane < HEAD, 1.0, 0.0).astype(BF16)
    second = jnp.where(lane < HEAD, 0.0, 1.0).astype(BF16)
    for b in range(2):
        at = slice(b * Q, b * Q + Q)
        dcb = dcb_ref[b]
        for p in range(2):
            ls = slice(p * 2 * HEAD, (p + 1) * 2 * HEAD)
            xp = xc[at, ls]
            dyp = dyo[at, ls]
            xbd = jnp.concatenate([xp * first, xp * second], axis=0)
            dbd = jnp.concatenate([dyp * first, dyp * second], axis=0)
            decay, mix, mixt = [], [], []
            for i in range(2):
                h = 2 * p + i
                ex = cols[0, at, h : h + 1] - rowt[0, 4 + h : 5 + h, at]
                lt = jnp.exp2(jnp.where(low, ex, NEG))
                ext = rowt[0, h : h + 1, at] - cols[0, at, 4 + h : 5 + h]
                ltt = jnp.exp2(jnp.where(high, ext, NEG))
                decay.append(lt)
                mix.append((cb[b] * lt).astype(BF16))
                mixt.append((cb[2 + b] * ltt).astype(BF16))
            yi_ref[at, ls] = dot(jnp.concatenate(mix, axis=1), xbd)
            dxi_ref[at, ls] = dot(jnp.concatenate(mixt, axis=1), dbd)
            dm = dot_tb(dyp, xbd)
            dcb = dcb + dm[:, 0:Q] * decay[0] + dm[:, Q:] * decay[1]
        dcb_ref[b] = dcb


def across_kernel(
    yv, x_own, rec, halo, w, xc, dyo, yi, dxi, ent, lea, bc, cc, fe, exp2, seg, rows, *rest
):
    (y_ref, gx_ref, send_ref, dc_ref, db_ref, wv_ref, ends_ref, dw_ref, head_ref, xs, gs, gy) = rest[-12:]
    y = yv[0]

    @pl.when(pl.program_id(0) == 0)
    def _():
        dc_ref[...] = jnp.zeros(dc_ref.shape, F32)
        db_ref[...] = jnp.zeros(db_ref.shape, F32)
        wv_ref[...] = jnp.zeros(wv_ref.shape, F32)

    xs[0:8] = halo[...]
    in_order(y, x_own[...], rec[0], xs, 8)
    s = conv_sum(xs, w, 2 * Q)
    x = xc[...].astype(F32)
    dy = dyo[...].astype(F32)
    f = dot(fe[0], exp2[...])
    er = dot(fe[1], exp2[...])
    wt = (x * f).astype(BF16)
    dyr = (dy * er).astype(BF16)
    d0, d1, skip = rows[0:1], rows[1:2], rows[3:4]
    top, end = slice(0, Q), slice(Q, 2 * Q)
    e0 = ent[...]
    r1 = lea[...]
    e1 = (d0 * e0.astype(F32) + dot_ta(bc[top], wt[top])).astype(BF16)
    r0 = (d1 * r1.astype(F32) + dot_ta(cc[end], dyr[end])).astype(BF16)
    over = jnp.concatenate([dot(cc[top], e0), dot(cc[end], e1)], axis=0) * er
    back = jnp.concatenate([dot(bc[top], r0), dot(bc[end], r1)], axis=0) * f
    yn = yi[...] + over
    dxn = dxi[...] + back
    dc_ref[top] += dot_tb(dyr[top], e0)
    dc_ref[end] += dot_tb(dyr[end], e1)
    db_ref[top] += dot_tb(wt[top], r0)
    db_ref[end] += dot_tb(wt[end], r1)
    wv_ref[0] += split_dot(dy * yn, seg[...])
    wv_ref[1] += split_dot(x * dxn, seg[...])
    xb = x * back
    ends_ref[...] = jnp.concatenate(
        [
            jnp.sum(xb[top], axis=0, keepdims=True)
            + d0 * jnp.sum(r0.astype(F32) * e0.astype(F32), axis=0, keepdims=True),
            jnp.sum(xb[end], axis=0, keepdims=True)
            + d1 * jnp.sum(r1.astype(F32) * e1.astype(F32), axis=0, keepdims=True),
            jnp.sum(x * dy, axis=0, keepdims=True),
            jnp.zeros((5, SUB), F32),
        ],
        axis=0,
    )
    gx, dw, head = conv_back(dxn + skip * dy, s, xs, gs, w, 2 * Q)
    dw_ref[...] = dw
    head_ref[...] = head
    gy[0] = (yn + skip * x).astype(BF16)
    gy[1] = gx.astype(BF16)

    @pl.when(y == 0)
    def _():
        y_ref[...] = gy[0, top]
        gx_ref[...] = gy[1, top]
        send_ref[...] = gy[:, end]

    @pl.when(y != 0)
    def _():
        y_ref[...] = gy[0, end]
        gx_ref[...] = gy[1, end]
        send_ref[...] = gy[:, top]


def finish_kernel(
    yv, b_own, c_own, dt_own, rec, halo, w, par, bc, cc, st, seg, dc, db, dcb, wv, ends,
    gb_ref, gc_ref, send_ref, gdt_ref, dw_ref, head_ref, gh_ref, xs, gs, gv, dts, gd,
):
    y = yv[0]
    width = b_own.shape[1]
    heads = par.shape[1]
    groups = width // N
    per = dc.shape[0] // groups
    for g in range(groups):
        cs = slice(g * N, (g + 1) * N)
        dcg = dc[g * per]
        dbg = db[g * per]
        dcbg = dcb[g * per]
        for i in range(1, per):
            dcg = dcg + dc[g * per + i]
            dbg = dbg + db[g * per + i]
            dcbg = dcbg + dcb[g * per + i]
        dcbg = dcbg.astype(BF16)
        for b in range(2):
            at = slice(b * Q, b * Q + Q)
            gv[1, at, cs] = dcg[at] + dot(dcbg[b], bc[at, cs])
            gv[0, at, cs] = dbg[at] + dot_ta(dcbg[b], cc[at, cs])
    for i, (own, out) in enumerate(((b_own, gb_ref), (c_own, gc_ref))):
        at = i * width
        xs[0:8] = halo[:, at : at + width]
        in_order(y, own[...], rec[:, at : at + width], xs, 8)
        wi = w[:, at : at + width]
        s = conv_sum(xs, wi, 2 * Q)
        gx, dw, head = conv_back(gv[i], s, xs, gs, wi, 2 * Q)
        dw_ref[:, at : at + width] = dw
        head_ref[:, at : at + width] = head

        @pl.when(y == 0)
        def _():
            out[...] = gx[0:Q].astype(BF16)
            send_ref[:, at : at + width] = gx[Q:].astype(BF16)

        @pl.when(y != 0)
        def _():
            out[...] = gx[Q:].astype(BF16)
            send_ref[:, at : at + width] = gx[0:Q].astype(BF16)

    @pl.when(y == 0)
    def _():
        dts[0:Q] = dt_own[:, 0:heads].astype(F32)
        dts[Q : 2 * Q] = rec[:, 2 * width : 2 * width + heads].astype(F32)

    @pl.when(y != 0)
    def _():
        dts[0:Q] = rec[:, 2 * width + heads : 2 * width + 2 * heads].astype(F32)
        dts[Q : 2 * Q] = dt_own[:, heads : 2 * heads].astype(F32)

    raw = dts[...] + par[1:2]
    step = st[...]
    rate = jnp.exp(par[0:1])
    chunks = wv.shape[0]
    w_sum, v_sum, e_sum = wv[0, 0], wv[0, 1], split_dot(ends[0], seg[0])
    for i in range(1, chunks):
        w_sum = w_sum + wv[i, 0]
        v_sum = v_sum + wv[i, 1]
        e_sum = e_sum + split_dot(ends[i], seg[i])
    tri = jnp.where(triangle(False), 1.0, 0.0).astype(BF16)
    diff = w_sum - v_sum
    dl = jnp.concatenate(
        [exact_dot(tri, diff[0:Q]) + e_sum[0:1], exact_dot(tri, diff[Q:]) + e_sum[1:2]], axis=0
    )
    ds = v_sum / step - rate * dl
    draw = ds / (1.0 + jnp.exp(-raw))
    gh_ref[...] = jnp.concatenate(
        [
            jnp.sum(dl * (-rate * step), axis=0, keepdims=True),
            jnp.sum(draw, axis=0, keepdims=True),
            e_sum[2:3],
            jnp.zeros((5, heads), F32),
        ],
        axis=0,
    )
    gd[...] = jnp.concatenate([draw, draw], axis=1).astype(BF16)

    @pl.when(y == 0)
    def _():
        gdt_ref[...] = gd[0:Q]
        send_ref[:, 2 * width :] = gd[Q:]

    @pl.when(y != 0)
    def _():
        gdt_ref[...] = gd[Q:]
        send_ref[:, 2 * width :] = gd[0:Q]


def whole(shape):
    return pl.BlockSpec(shape, lambda *_: (0,) * len(shape))


def shape_of(*dims, dtype=F32):
    return jax.ShapeDtypeStruct(dims, dtype)


def call(kernel, grid, in_specs, out_specs, out_shape, scratch, micros, nbytes, aliases=None):
    return pl.pallas_call(
        kernel,
        out_shape=out_shape,
        grid_spec=pltpu.PrefetchScalarGridSpec(
            num_scalar_prefetch=1,
            grid=grid,
            in_specs=in_specs,
            out_specs=out_specs,
            scratch_shapes=scratch,
        ),
        compiler_params=params(),
        cost_estimate=cost(micros, nbytes),
        input_output_aliases=aliases or {},
    )


def per_device(
    ssm_input, b_input, c_input, dt_input, conv_weight, conv_bias, a_log, dt_bias, skip_gain, grad_out
):
    x_rows, b_rows, c_rows = ssm_input[0], b_input[0], c_input[0]
    dt_rows, dy_rows = dt_input[0], grad_out[0]
    devices = lax.axis_size("sp")
    dp_size = lax.axis_size("dp")
    spots = devices // 2
    me = lax.axis_index("sp")
    y = lax.rem(me, 2)
    z = me // 2
    yv = jnp.reshape(y, (1,)).astype(jnp.int32)
    xw = x_rows.shape[1] // 2
    bw = b_rows.shape[1] // 2
    hl = dt_rows.shape[1] // 2
    chunks = 4
    cw = xw // chunks
    subs = cw // SUB
    per_group = chunks // (bw // N)
    edge = 8

    def pairs(fn):
        return [(i, fn(i)) for i in range(devices) if fn(i) is not None and 0 <= fn(i) < devices]

    swap = pairs(lambda i: i ^ 1)

    def half(v, which, width):
        return lax.dynamic_slice_in_dim(v, which * width, width, v.ndim - 1)

    msg = jnp.concatenate([half(b_rows, 1 - y, bw), half(c_rows, 1 - y, bw), dt_rows], axis=1)
    rec_bc = lax.ppermute(msg, "sp", swap)

    def rim(k):
        return jnp.concatenate(
            [
                x_rows[Q - edge :, k * xw : (k + 1) * xw],
                b_rows[Q - edge :, k * bw : (k + 1) * bw],
                c_rows[Q - edge :, k * bw : (k + 1) * bw],
            ],
            axis=1,
        )

    rim0 = lax.ppermute(rim(0), "sp", pairs(lambda i: i + 1 if i % 2 else None))
    rim1 = lax.ppermute(rim(1), "sp", pairs(lambda i: i + 2 if i % 2 else None))
    halo = rim0.astype(F32) + rim1.astype(F32)
    rec = []
    for c in range(chunks):
        at = (1 - y) * xw + c * cw
        out = jnp.stack(
            [lax.dynamic_slice_in_dim(x_rows, at, cw, 1), lax.dynamic_slice_in_dim(dy_rows, at, cw, 1)]
        )
        rec.append(lax.ppermute(out, "sp", swap))

    wb = jnp.concatenate([conv_weight, conv_bias[None], jnp.zeros((3, conv_bias.shape[0]), F32)], 0)
    wbx = half(wb[:, : 2 * xw], y, xw)
    wbc = jnp.concatenate(
        [half(wb[:, 2 * xw : 2 * xw + 2 * bw], y, bw), half(wb[:, 2 * xw + 2 * bw :], y, bw)], axis=1
    )
    halo_x, halo_bc = halo[:, :xw], halo[:, xw:]
    par = half(
        jnp.concatenate([jnp.stack([a_log, dt_bias, skip_gain]), jnp.zeros((5, 2 * hl), F32)], 0), y, hl
    )
    lanes = jnp.arange(xw) // HEAD
    expand = (jnp.arange(hl)[:, None] == lanes[None, :]).astype(BF16)
    exp2 = jnp.concatenate([expand, expand], axis=0)
    seg = (lanes[:, None] == jnp.arange(hl)[None, :]).astype(BF16)

    nq = hl // 4
    two = 2 * Q
    own_b = pl.BlockSpec((Q, bw), lambda j, yr: (0, yr[0]))
    bcc, ccc, fe, rows, cols, rowt, st = call(
        setup_kernel,
        (1,),
        [
            own_b, own_b, whole(dt_rows.shape), whole(rec_bc.shape), whole((edge, 2 * bw)),
            whole((8, 2 * bw)), whole((8, hl)), whole((2 * hl, xw)),
        ],
        [
            whole((two, bw)), whole((two, bw)), whole((2, two, 2 * hl)), whole((8, xw)),
            whole((nq, two, 8)), whole((nq, 8, two)), whole((two, hl)),
        ],
        [
            shape_of(two, bw, dtype=BF16), shape_of(two, bw, dtype=BF16),
            shape_of(2, two, 2 * hl, dtype=BF16), shape_of(8, xw), shape_of(nq, two, 8),
            shape_of(nq, 8, two), shape_of(two, hl),
        ],
        [
            pltpu.VMEM((two + 8, bw), F32), pltpu.VMEM((two, hl), F32),
            pltpu.VMEM((2 * hl, two), F32),
        ],
        4, 4 << 20,
    )(yv, b_rows, c_rows, dt_rows, rec_bc, halo_bc, wbc, par, exp2)

    def own(c):
        return pl.BlockSpec((Q, SUB), lambda j, yr: (0, (yr[0] * chunks + c) * subs + j))

    def band(rows_, c):
        return pl.BlockSpec((rows_, SUB), lambda j, yr: (0, c * subs + j))

    def group(c):
        return pl.BlockSpec((two, N), lambda j, yr: (0, c // per_group))

    local = pl.BlockSpec((two, SUB), lambda j, yr: (0, j))
    local8 = pl.BlockSpec((8, SUB), lambda j, yr: (0, j))
    full_fe = whole(fe.shape)

    xcs, dyos, ts, us = [], [], [], []
    for c in range(chunks):
        xc, dyo, t, u = call(
            state_kernel,
            (subs,),
            [
                own(c), own(c), pl.BlockSpec((2, Q, SUB), lambda j, yr: (0, 0, j)), band(edge, c),
                band(8, c), group(c), group(c), full_fe, band(2 * hl, c), band(8, c),
            ],
            [local] * 4,
            [shape_of(two, cw, dtype=BF16)] * 4,
            [pltpu.VMEM((two + 8, SUB), F32)],
            3, 4 << 20,
        )(yv, x_rows, dy_rows, rec[c], halo_x, wbx, bcc, ccc, fe, exp2, rows)
        xcs.append(xc)
        dyos.append(dyo)
        ts.append(t)
        us.append(u)

    zero = jnp.zeros((N, cw), BF16)
    both = rows[2]
    ent_in, lea_in = zero, zero
    ents = [zero] * chunks
    leas = [zero] * chunks
    back_spot = spots - 1 - z
    for t in range(chunks + spots - 2):
        def pick(items, at):
            out = items[0]
            for c in range(1, min(t, chunks - 1) + 1):
                out = jnp.where(at == c, items[c], out)
            return out

        decays = [both[c * cw : (c + 1) * cw] for c in range(chunks)]
        go = pick(decays, t - z) * ent_in.astype(F32) + pick(ts, t - z).astype(F32)
        ent_in = lax.ppermute(go.astype(BF16), "sp", pairs(lambda i: i + 2))
        go = pick(decays, t - back_spot) * lea_in.astype(F32) + pick(us, t - back_spot).astype(F32)
        lea_in = lax.ppermute(go.astype(BF16), "sp", pairs(lambda i: i - 2))
        for c in range(max(0, t + 2 - spots), min(t, chunks - 1) + 1):
            ents[c] = jnp.where(t + 1 - z == c, ent_in, ents[c])
            leas[c] = jnp.where(t + 1 - back_spot == c, lea_in, leas[c])

    yis, dxis, dcbs = [], [], []
    for c in range(chunks):
        yi, dxi, dcb = call(
            lambda yr, *refs: within_kernel(*refs),
            (subs,),
            [
                local, local,
                pl.BlockSpec((1, two, 8), lambda j, yr: (c * subs + j, 0, 0)),
                pl.BlockSpec((1, 8, two), lambda j, yr: (c * subs + j, 0, 0)),
                group(c), group(c),
            ],
            [local, local, whole((2, Q, Q))],
            [shape_of(two, cw), shape_of(two, cw), shape_of(2, Q, Q)],
            [pltpu.VMEM((4, Q, Q), F32)],
            5, 4 << 20,
        )(yv, xcs[c], dyos[c], cols, rowt, bcc, ccc)
        yis.append(yi)
        dxis.append(dxi)
        dcbs.append(dcb)

    y_all, gx_all = None, None
    parts = []
    for c in range(chunks):
        ins = [
            x_rows, rec[c], halo_x, wbx, xcs[c], dyos[c], yis[c], dxis[c], ents[c], leas[c],
            bcc, ccc, fe, exp2, seg, rows,
        ]
        specs = [
            own(c), pl.BlockSpec((1, Q, SUB), lambda j, yr: (0, 0, j)), band(edge, c), band(8, c),
            local, local, local, local, local, local, group(c), group(c), full_fe,
            band(2 * hl, c), pl.BlockSpec((SUB, hl), lambda j, yr: (c * subs + j, 0)), band(8, c),
        ]
        aliases = {}
        if c:
            aliases = {len(ins) + 1: 0, len(ins) + 2: 1}
            ins += [y_all, gx_all]
            specs += [pl.BlockSpec(memory_space=pl.ANY)] * 2
        full = shape_of(Q, 2 * xw, dtype=BF16)
        y_all, gx_all, send, *part = call(
            across_kernel,
            (subs,),
            specs,
            [
                own(c), own(c), pl.BlockSpec((2, Q, SUB), lambda j, yr: (0, 0, j)),
                whole((two, N)), whole((two, N)), whole((2, two, hl)), local8, local8, local8,
            ],
            [
                full, full, shape_of(2, Q, cw, dtype=BF16), shape_of(two, N), shape_of(two, N),
                shape_of(2, two, hl), shape_of(8, cw), shape_of(8, cw), shape_of(8, cw),
            ],
            [
                pltpu.VMEM((two + 8, SUB), F32), pltpu.VMEM((two + 8, SUB), F32),
                pltpu.VMEM((2, two, SUB), BF16),
            ],
            6, 6 << 20, aliases,
        )(yv, *ins)
        parts.append(part)
        got = lax.ppermute(send, "sp", swap)
        at = (1 - y) * xw + c * cw
        y_all = lax.dynamic_update_slice(y_all, got[0], (0, at))
        gx_all = lax.dynamic_update_slice(gx_all, got[1], (0, at))

    dcs, dbs, wvs, ends, dws, heads_ = [jnp.stack(v) for v in zip(*parts)]
    gb_own, gc_own, send, gdt_own, dw_bc, head_bc, gh = call(
        finish_kernel,
        (1,),
        [
            own_b, own_b, whole(dt_rows.shape), whole(rec_bc.shape), whole((edge, 2 * bw)),
            whole((8, 2 * bw)), whole((8, hl)), whole((two, bw)), whole((two, bw)), whole((two, hl)),
            whole((chunks, cw, hl)), whole(dcs.shape), whole(dbs.shape),
            whole((chunks, 2, Q, Q)), whole(wvs.shape), whole(ends.shape),
        ],
        [
            own_b, own_b, whole((Q, 2 * bw + 2 * hl)), whole((Q, 2 * hl)), whole((8, 2 * bw)),
            whole((8, 2 * bw)), whole((8, hl)),
        ],
        [
            shape_of(Q, 2 * bw, dtype=BF16), shape_of(Q, 2 * bw, dtype=BF16),
            shape_of(Q, 2 * bw + 2 * hl, dtype=BF16), shape_of(Q, 2 * hl, dtype=BF16),
            shape_of(8, 2 * bw), shape_of(8, 2 * bw), shape_of(8, hl),
        ],
        [
            pltpu.VMEM((two + 8, bw), F32), pltpu.VMEM((two + 8, bw), F32),
            pltpu.VMEM((2, two, bw), F32), pltpu.VMEM((two, hl), F32), pltpu.VMEM((two, 2 * hl), BF16),
        ],
        6, 8 << 20,
    )(
        yv, b_rows, c_rows, dt_rows, rec_bc, halo_bc, wbc, par, bcc, ccc, st,
        seg.reshape(chunks, cw, hl), dcs, dbs, jnp.stack(dcbs), wvs, ends,
    )
    got = lax.ppermute(send, "sp", swap)
    gb = lax.dynamic_update_slice(gb_own, got[:, :bw], (0, (1 - y) * bw))
    gc = lax.dynamic_update_slice(gc_own, got[:, bw : 2 * bw], (0, (1 - y) * bw))
    low_lane = jnp.arange(2 * hl)[None, :] < hl
    gdt = jnp.where(low_lane == (y == 0), gdt_own, got[:, 2 * bw :])

    first_rows = jnp.concatenate([jnp.concatenate(list(heads_), axis=1), head_bc], axis=1).astype(BF16)
    next0 = lax.ppermute(first_rows, "sp", pairs(lambda i: i - 1 if i % 2 == 0 else None)).astype(F32)
    next1 = lax.ppermute(first_rows, "sp", pairs(lambda i: i - 2 if i % 2 else None)).astype(F32)

    def rim_add(grad, lo, width, w):
        g = jnp.concatenate([next0[:, lo : lo + width], next1[:, lo : lo + width]], axis=1)
        add = jnp.concatenate(
            [
                jnp.zeros((5, 2 * width), F32),
                w[0:1] * g[0:1],
                w[0:1] * g[1:2] + w[1:2] * g[0:1],
                w[0:1] * g[2:3] + w[1:2] * g[1:2] + w[2:3] * g[0:1],
            ],
            axis=0,
        )
        tail = (grad[Q - 8 :].astype(F32) + add).astype(BF16)
        return lax.dynamic_update_slice(grad, tail, (Q - 8, 0))

    grad_x = rim_add(gx_all, 0, xw, conv_weight[:, : 2 * xw])
    grad_b = rim_add(gb, xw, bw, conv_weight[:, 2 * xw : 2 * xw + 2 * bw])
    grad_c = rim_add(gc, xw + bw, bw, conv_weight[:, 2 * xw + 2 * bw :])

    red = jnp.concatenate(
        [
            jnp.concatenate(list(dws) + [dw_bc], axis=1)[:5].reshape(-1),
            gh[:3].reshape(-1),
            jnp.zeros((5 * 128 - 3 * hl,), F32),
        ]
    ).reshape(-1, 128)
    size = 1
    while size < dp_size:
        red = red + lax.ppermute(red, "dp", [(i, i ^ size) for i in range(dp_size)])
        size *= 2
    size = 2
    while size < devices:
        red = red + lax.ppermute(red, "sp", [(i, i ^ size) for i in range(devices)])
        size *= 2
    other = lax.ppermute(red, "sp", swap)
    first = jnp.where(y == 0, red, other).reshape(-1)
    second = jnp.where(y == 0, other, red).reshape(-1)
    count = 5 * (xw + 2 * bw)
    g0 = first[:count].reshape(5, xw + 2 * bw)
    g1 = second[:count].reshape(5, xw + 2 * bw)
    total = jnp.concatenate(
        [g0[:, :xw], g1[:, :xw], g0[:, xw : xw + bw], g1[:, xw : xw + bw], g0[:, xw + bw :], g1[:, xw + bw :]],
        axis=1,
    )
    gheads = jnp.concatenate(
        [first[count : count + 3 * hl].reshape(3, hl), second[count : count + 3 * hl].reshape(3, hl)], axis=1
    )
    per_dev = 2 * hl // devices
    head_total = lax.dynamic_slice_in_dim(gheads, me * per_dev, per_dev, 1)
    return (
        y_all[None], grad_x[None], grad_b[None], grad_c[None], gdt[None], total[:4], total[4], head_total,
    )


def solution(mesh):
    rows = P("dp", "sp", None)
    in_specs = (rows, rows, rows, rows, P(), P(), P(), P(), P(), rows)
    out_specs = (rows, rows, rows, rows, rows, P(), P(), P(None, "sp"))
    return jax.shard_map(
        per_device, mesh=mesh, in_specs=in_specs, out_specs=out_specs, check_vma=False
    )
```

time: 695 us -> 238 us (0.34); the launches traced: 686 us -> 237 us
  local copies, waits for them, and re-layouts: 153 us -> 30 us
  matrix products: 95.5 us -> 0 us
  other arithmetic: 115 us -> 31.6 us
  waiting for transfers between devices: 125 us -> 43.2 us
  blocking collectives: 81.2 us -> 0 us
  Pallas kernels: 0 us -> 63.7 us
  starting transfers between devices: 102 us -> 66.7 us
  between operations: 15.3 us -> 1.87 us
    dot_general x15 -> x0, matrix products: 95.5 us -> none  [the longest x12 62.5 us: product(): return jnp.einsum(form, left, right, preferred_element_type=jnp.float32)]
    all_to_all x10 -> x0, starting transfers between devices: 85.9 us -> none  [the longest x1 20.9 us: per_device(): lax.all_to_all(gdt_heads, 'sp', split_axis=0, concat_axis=1, tiled=True)]
    psum x2 -> x0, blocking collectives: 81.2 us -> none  [the longest x1 74.8 us: per_device(): kernel_total, offset_total = lax.psum((d_kernel, d_offset), ('dp', 'sp'))]
    pallas_call x0 -> x14, Pallas kernels: none -> 63.7 us  [the longest x4 31.9 us: per_device(): call(across_kernel, (subs,), specs, [own(c), own(c), pl.BlockSpec((2, Q,...]
    all_to_all x10 -> x0, waiting for transfers between devices: 57.9 us -> none  [the longest x1 22.9 us: per_device(): lax.all_to_all(dy_rows, 'sp', split_axis=1, concat_axis=0, tiled=True)]
    ppermute x6 -> x31, starting transfers between devices: 16.1 us -> 66.7 us  [the longest x6 28 us: per_device(): ent_in = lax.ppermute(go.astype(BF16), 'sp', pairs(lambda i: i + 2))]
    psum x1 -> x0, waiting for transfers between devices: 43.6 us -> none  [per_device(): kernel_total, offset_total = lax.psum((d_kernel, d_offset), ('dp', 'sp'))]
    reduce_sum x10 -> x0, other arithmetic: 38.5 us -> none  [the longest x2 28.8 us: conv_silu(): kernel_cols[tap_index][None, :] * padded[tap_index:tap_index + count_rows]]
  transfers between devices with their start and end apart: 17 -> 31, of which waited for: 10 -> 13; matrix products, arithmetic and copies ran while one was open for 24% -> 16% of each run, Pallas kernels for 0% -> 12%
where the time goes in v1:
time: 238 us; the launch traced here: 237 us
  starting transfers between devices  66.7 us (28%)
  Pallas kernels  63.7 us (27%)
  waiting for transfers between devices  43.2 us (18%)
  other arithmetic  31.6 us (13%)
  local copies, waits for them, and re-layouts  30 us (13%)
    pallas_call x4, Pallas kernels, per_device(): call(across_kernel, (subs,), specs, [own(c), own(c), pl.BlockSpec((2, Q,...  31.9 us
    ppermute x6, starting transfers between devices, per_device(): ent_in = lax.ppermute(go.astype(BF16), 'sp', pairs(lambda i: i + 2))  28 us
    ppermute x6, waiting for transfers between devices, per_device(): lea_in = lax.ppermute(go.astype(BF16), 'sp', pairs(lambda i: i - 2))  16.8 us
    unnamed x140, local copies, waits for them, and re-layouts  15 us
    ppermute x5, waiting for transfers between devices, per_device(): got = lax.ppermute(send, 'sp', swap)  14.2 us
    pallas_call x4, Pallas kernels, per_device(): call(state_kernel, (subs,), [own(c), own(c), pl.BlockSpec((2, Q, SUB), la...  13.4 us
    pallas_call x4, Pallas kernels, per_device(): call(lambda yr, *refs: within_kernel(*refs), (subs,), [local, local, pl.B...  11.6 us
    ppermute x4, starting transfers between devices, per_device(): rec.append(lax.ppermute(out, 'sp', swap))  9.74 us
  transfers between devices with their start and end apart: 31, of which 13 were waited for; matrix products, arithmetic and copies ran while one was open for 16% of the time, Pallas kernels for 12%

profile of v1, /device:TPU:0, one launch (start us, length us, event | category | flops | bytes accessed | tf_op | source)
XLA Modules:
  0.0 237.1 jit_solution(17480444415973476592)
XLA Ops:
  3.1 3.0 %collective-permute-start.3 = (bf16[128,1152]{1,0:T(8,128)(2,1)}, bf16[128,1152]{1,0:T(8,128)(2,1)S(1)}, u32[]{:S(2)}, u32[]{:S(2)}) collective-permute-start(bf16[128,1152]{1,0:T(8,128)(2,1)} %pad_maximum_fusion.8), channel_id=1, source_target_pairs={{0,1},{1,0},{2,3},{3,2},{4,5},{5,4},{6,7},{7,6},{8,9},{9,8},{10,11... | collective-permute-start | bytes 884744 | tf_op jit(solution)/shard_map/ppermute | solution.py:422
  13.7 7.1 %collective-permute-start.4 = (bf16[2,128,1024]{2,1,0:T(8,128)(2,1)}, bf16[2,128,1024]{2,1,0:T(8,128)(2,1)S(1)}, u32[]{:S(2)}, u32[]{:S(2)}) collective-permute-start(bf16[2,128,1024]{2,1,0:T(8,128)(2,1)} %pad_maximum_fusion.4), channel_id=1, source_target_pairs={{0,1},{1,0},{2,3},{3,2},{4,5},{5,4},{6,7},{7,6},{8,9},{9,8},{10,11... | collective-permute-start | bytes 1572872 | tf_op jit(solution)/shard_map/ppermute | solution.py:443
  22.7 2.7 %fusion.seg = bf16[4096,64]{1,0:T(8,128)(2,1)} fusion(s32[4096]{0:T(1024)S(1)} %add_select_fusion.1), kind=kLoop, calls=%fused_computation.2 | loop fusion | flops 524288 | bytes 540672 | tf_op jit(solution)/shard_map/convert_element_type | solution.py:457
  36.9 2.6 %shard_map.161 = (bf16[256,512]{1,0:T(8,128)(2,1)S(1)}, bf16[256,512]{1,0:T(8,128)(2,1)S(1)}, bf16[2,256,128]{2,1,0:T(8,128)(2,1)S(1)}, f32[8,4096]{1,0:T(8,128)...) custom-call(s32[1]{0:T(128)} %bitcast.yv.yr, bf16[128,1024]{1,0:T(8,128)(2,1)S(1)} %bitcast.130, ...), custom_call_target="tpu_custom_call" | custom-call | flops 4000000000 | bytes 4194304 | tf_op jit(solution)/shard_map/pallas_call | solution.py:462
  40.9 3.3 %shard_map.164 = (bf16[256,1024]{1,0:T(8,128)(2,1)S(1)}, bf16[256,1024]{1,0:T(8,128)(2,1)S(1)}, bf16[256,1024]{1,0:T(8,128)(2,1)S(1)}, bf16[256,1024]{1,0:T(8,128)(2,1)S(1)}) custom-call(s32[1]{0:T(128)} %bitcast.yv.yr, bf16[128,8192]{1,0:T(8,128)(2,1)S(1)} %bitcast.99, bf16[128,8192]{1,0:T(8,128)(2,1)S(1)} %bitcast.107, ...), custom_call_target="tpu_custom_call" | custom-call | flops 3000000000 | bytes 4194304 | tf_op jit(solution)/shard_map/pallas_call | solution.py:500
  45.8 4.6 %collective-permute-start.5 = (bf16[256,1024]{1,0:T(8,128)(2,1)S(1)}, bf16[256,1024]{1,0:T(8,128)(2,1)S(1)}, u32[]{:S(2)}, u32[]{:S(2)}) collective-permute-start(bf16[256,1024]{1,0:T(8,128)(2,1)S(1)} %get-tuple-element.227), channel_id=1, source_target_pairs={{0,2},{1,3},{2,4},{3,5},{4,6},{5,7},{8,10},{9,11},{10,12},{11,13},... | collective-permute-start | bytes 1572872 | tf_op jit(solution)/shard_map/ppermute | solution.py:532
  50.4 3.4 %shard_map.165 = (bf16[256,1024]{1,0:T(8,128)(2,1)S(1)}, bf16[256,1024]{1,0:T(8,128)(2,1)S(1)}, bf16[256,1024]{1,0:T(8,128)(2,1)S(1)}, bf16[256,1024]{1,0:T(8,128)(2,1)S(1)}) custom-call(s32[1]{0:T(128)} %bitcast.yv.yr, bf16[128,8192]{1,0:T(8,128)(2,1)S(1)} %bitcast.100, bf16[128,8192]{1,0:T(8,128)(2,1)S(1)} %bitcast.108, ...), custom_call_target="tpu_custom_call" | custom-call | flops 3000000000 | bytes 4194304 | tf_op jit(solution)/shard_map/pallas_call | solution.py:500
  53.8 4.5 %collective-permute-done.13 = bf16[256,1024]{1,0:T(8,128)(2,1)S(1)} collective-permute-done((bf16[256,1024]{1,0:T(8,128)(2,1)S(1)}, bf16[256,1024]{1,0:T(8,128)(2,1)S(1)}, u32[]{:S(2)}, u32[]{:S(2)}) %collective-permute-start.13) | collective-permute-done | bytes 524320 | tf_op jit(solution)/shard_map/ppermute | solution.py:534
  60.2 4.6 %collective-permute-start.7 = (bf16[256,1024]{1,0:T(8,128)(2,1)S(1)}, bf16[256,1024]{1,0:T(8,128)(2,1)S(1)}, u32[]{:S(2)}, u32[]{:S(2)}) collective-permute-start(bf16[256,1024]{1,0:T(8,128)(2,1)S(1)} %add_convert_fusion.11), channel_id=1, source_target_pairs={{0,2},{1,3},{2,4},{3,5},{4,6},{5,7},{8,10},{9,11},{10,12},{11,13},... | collective-permute-start | bytes 1572872 | tf_op jit(solution)/shard_map/ppermute | solution.py:532
  64.8 3.4 %shard_map.166 = (bf16[256,1024]{1,0:T(8,128)(2,1)S(1)}, bf16[256,1024]{1,0:T(8,128)(2,1)S(1)}, bf16[256,1024]{1,0:T(8,128)(2,1)S(1)}, bf16[256,1024]{1,0:T(8,128)(2,1)S(1)}) custom-call(s32[1]{0:T(128)} %bitcast.yv.yr, bf16[128,8192]{1,0:T(8,128)(2,1)S(1)} %bitcast.101, bf16[128,8192]{1,0:T(8,128)(2,1)S(1)} %bitcast.109, ...), custom_call_target="tpu_custom_call" | custom-call | flops 3000000000 | bytes 4194304 | tf_op jit(solution)/shard_map/pallas_call | solution.py:500
  68.2 3.4 %collective-permute-done.14 = bf16[256,1024]{1,0:T(8,128)(2,1)S(1)} collective-permute-done((bf16[256,1024]{1,0:T(8,128)(2,1)S(1)}, bf16[256,1024]{1,0:T(8,128)(2,1)S(1)}, u32[]{:S(2)}, u32[]{:S(2)}) %collective-permute-start.14) | collective-permute-done | bytes 524320 | tf_op jit(solution)/shard_map/ppermute | solution.py:534
  73.7 4.6 %collective-permute-start.9 = (bf16[256,1024]{1,0:T(8,128)(2,1)S(1)}, bf16[256,1024]{1,0:T(8,128)(2,1)S(1)}, u32[]{:S(2)}, u32[]{:S(2)}) collective-permute-start(bf16[256,1024]{1,0:T(8,128)(2,1)S(1)} %add_convert_fusion.10), channel_id=1, source_target_pairs={{0,2},{1,3},{2,4},{3,5},{4,6},{5,7},{8,10},{9,11},{10,12},{11,13},... | collective-permute-start | bytes 1572872 | tf_op jit(solution)/shard_map/ppermute | solution.py:532
  78.3 3.4 %shard_map.162 = (bf16[256,1024]{1,0:T(8,128)(2,1)S(1)}, bf16[256,1024]{1,0:T(8,128)(2,1)S(1)}, bf16[256,1024]{1,0:T(8,128)(2,1)S(1)}, bf16[256,1024]{1,0:T(8,128)(2,1)S(1)}) custom-call(s32[1]{0:T(128)} %bitcast.yv.yr, bf16[128,8192]{1,0:T(8,128)(2,1)S(1)} %bitcast.102, bf16[128,8192]{1,0:T(8,128)(2,1)S(1)} %bitcast.110, ...), custom_call_target="tpu_custom_call" | custom-call | flops 3000000000 | bytes 4194304 | tf_op jit(solution)/shard_map/pallas_call | solution.py:500
  86.5 4.6 %collective-permute-start.10 = (bf16[256,1024]{1,0:T(8,128)(2,1)S(1)}, bf16[256,1024]{1,0:T(8,128)(2,1)S(1)}, u32[]{:S(2)}, u32[]{:S(2)}) collective-permute-start(bf16[256,1024]{1,0:T(8,128)(2,1)S(1)} %add_convert_fusion.9), channel_id=1, source_target_pairs={{0,2},{1,3},{2,4},{3,5},{4,6},{5,7},{8,10},{9,11},{10,12},{11,13},... | collective-permute-start | bytes 1572872 | tf_op jit(solution)/shard_map/ppermute | solution.py:532
  91.1 4.5 %collective-permute-done.16 = bf16[256,1024]{1,0:T(8,128)(2,1)S(1)} collective-permute-done((bf16[256,1024]{1,0:T(8,128)(2,1)S(1)}, bf16[256,1024]{1,0:T(8,128)(2,1)S(1)}, u32[]{:S(2)}, u32[]{:S(2)}) %collective-permute-start.16) | collective-permute-done | bytes 524320 | tf_op jit(solution)/shard_map/ppermute | solution.py:534
  99.7 4.6 %collective-permute-start.11 = (bf16[256,1024]{1,0:T(8,128)(2,1)}, bf16[256,1024]{1,0:T(8,128)(2,1)S(1)}, u32[]{:S(2)}, u32[]{:S(2)}) collective-permute-start(bf16[256,1024]{1,0:T(8,128)(2,1)} %add_convert_fusion.8), channel_id=1, source_target_pairs={{0,2},{1,3},{2,4},{3,5},{4,6},{5,7},{8,10},{9,11},{10,12},{11,13},... | collective-permute-start | bytes 1572872 | tf_op jit(solution)/shard_map/ppermute | solution.py:532
  104.3 2.9 %shard_map.169 = (f32[256,1024]{1,0:T(8,128)S(1)}, f32[256,1024]{1,0:T(8,128)S(1)}, f32[2,128,128]{2,1,0:T(8,128)S(1)}) custom-call(s32[1]{0:T(128)} %bitcast.yv.yr, bf16[256,1024]{1,0:T(8,128)(2,1)S(1)} %get-tuple-element.112.refs_0_.xc, bf16[256,1024]{1,0:T(8,128)(2,1)S(1)} %get-tuple-element.113.refs_1_.dyo, f32[16,256,8]{2,1,0:T(8,128)S(1)} %copy-done.41, ...), custom_call_target="tpu_custom_call" | custom-call | flops 5000000000 | bytes 4194304 | tf_op jit(solution)/shard_map/pallas_call | solution.py:541
  113.4 5.1 %collective-permute-start.12 = (bf16[256,1024]{1,0:T(8,128)(2,1)}, bf16[256,1024]{1,0:T(8,128)(2,1)}, u32[]{:S(2)}, u32[]{:S(2)}) collective-permute-start(bf16[256,1024]{1,0:T(8,128)(2,1)} %add_convert_fusion.7), channel_id=1, source_target_pairs={{0,2},{1,3},{2,4},{3,5},{4,6},{5,7},{8,10},{9,11},{10,12},{11,13},... | collective-permute-start | bytes 1572872 | tf_op jit(solution)/shard_map/ppermute | solution.py:532
  118.5 2.9 %shard_map.168 = (f32[256,1024]{1,0:T(8,128)S(1)}, f32[256,1024]{1,0:T(8,128)S(1)}, f32[2,128,128]{2,1,0:T(8,128)S(1)}) custom-call(s32[1]{0:T(128)} %bitcast.yv.yr, bf16[256,1024]{1,0:T(8,128)(2,1)S(1)} %get-tuple-element.108.refs_0_.xc, bf16[256,1024]{1,0:T(8,128)(2,1)S(1)} %get-tuple-element.109.refs_1_.dyo, f32[16,256,8]{2,1,0:T(8,128)S(1)} %copy-done.41, ...), custom_call_target="tpu_custom_call" | custom-call | flops 5000000000 | bytes 4194304 | tf_op jit(solution)/shard_map/pallas_call | solution.py:541
  125.2 7.9 %shard_map.170 = (bf16[128,8192]{1,0:T(8,128)(2,1)}, bf16[128,8192]{1,0:T(8,128)(2,1)S(1)}, bf16[2,128,1024]{2,1,0:T(8,128)(2,1)S(1)}, f32[256,256]{1,0:T(8,128)...) custom-call(s32[1]{0:T(128)} %bitcast.yv.yr, ...), custom_call_target="tpu_custom_call" | custom-call | flops 6000000000 | bytes 6291456 | tf_op jit(solution)/shard_map/pallas_call | solution.py:577
  137.5 2.9 %shard_map.167 = (f32[256,1024]{1,0:T(8,128)S(1)}, f32[256,1024]{1,0:T(8,128)S(1)}, f32[2,128,128]{2,1,0:T(8,128)S(1)}) custom-call(s32[1]{0:T(128)} %bitcast.yv.yr, bf16[256,1024]{1,0:T(8,128)(2,1)S(1)} %get-tuple-element.104.refs_0_.xc, bf16[256,1024]{1,0:T(8,128)(2,1)S(1)} %get-tuple-element.105.refs_1_.dyo, f32[16,256,8]{2,1,0:T(8,128)S(1)} %copy-done.42, ...), custom_call_target="tpu_custom_call" | custom-call | flops 5000000000 | bytes 4194304 | tf_op jit(solution)/shard_map/pallas_call | solution.py:541
  142.4 2.9 %shard_map.163 = (f32[256,1024]{1,0:T(8,128)S(1)}, f32[256,1024]{1,0:T(8,128)S(1)}, f32[2,128,128]{2,1,0:T(8,128)S(1)}) custom-call(s32[1]{0:T(128)} %bitcast.yv.yr, bf16[256,1024]{1,0:T(8,128)(2,1)S(1)} %get-tuple-element.90.refs_0_.xc, bf16[256,1024]{1,0:T(8,128)(2,1)S(1)} %get-tuple-element.91.refs_1_.dyo, f32[16,256,8]{2,1,0:T(8,128)S(1)} %copy-done.42, ...), custom_call_target="tpu_custom_call" | custom-call | flops 5000000000 | bytes 4194304 | tf_op jit(solution)/shard_map/pallas_call | solution.py:541
  147.7 8.0 %shard_map.171 = (bf16[128,8192]{1,0:T(8,128)(2,1)}, bf16[128,8192]{1,0:T(8,128)(2,1)S(1)}, bf16[2,128,1024]{2,1,0:T(8,128)(2,1)S(1)}, f32[256,256]{1,0:T(8,128)...) custom-call(s32[1]{0:T(128)} %bitcast.yv.yr, ...), custom_call_target="tpu_custom_call", output_to_operand_aliasing={{0}: (17, {}), {1}: (18, {})} | custom-call | flops 6000000000 | bytes 6291456 | tf_op jit(solution)/shard_map/pallas_call | solution.py:577
  157.5 7.4 %collective-permute-done.20 = bf16[2,128,1024]{2,1,0:T(8,128)(2,1)S(1)} collective-permute-done((bf16[2,128,1024]{2,1,0:T(8,128)(2,1)S(1)}, bf16[2,128,1024]{2,1,0:T(8,128)(2,1)S(1)}, u32[]{:S(2)}, u32[]{:S(2)}) %collective-permute-start.20) | collective-permute-done | bytes 524320 | tf_op jit(solution)/shard_map/ppermute | solution.py:596
  165.6 8.0 %shard_map.172 = (bf16[128,8192]{1,0:T(8,128)(2,1)}, bf16[128,8192]{1,0:T(8,128)(2,1)S(1)}, bf16[2,128,1024]{2,1,0:T(8,128)(2,1)S(1)}, f32[256,256]{1,0:T(8,128)...) custom-call(s32[1]{0:T(128)} %bitcast.yv.yr, ...), custom_call_target="tpu_custom_call", output_to_operand_aliasing={{0}: (17, {}), {1}: (18, {})} | custom-call | flops 6000000000 | bytes 6291456 | tf_op jit(solution)/shard_map/pallas_call | solution.py:577
  176.0 6.8 %collective-permute-done.21 = bf16[2,128,1024]{2,1,0:T(8,128)(2,1)S(1)} collective-permute-done((bf16[2,128,1024]{2,1,0:T(8,128)(2,1)S(1)}, bf16[2,128,1024]{2,1,0:T(8,128)(2,1)S(1)}, u32[]{:S(2)}, u32[]{:S(2)}) %collective-permute-start.21) | collective-permute-done | bytes 524320 | tf_op jit(solution)/shard_map/ppermute | solution.py:596
  183.6 8.0 %shard_map.173 = (bf16[128,8192]{1,0:T(8,128)(2,1)}, bf16[128,8192]{1,0:T(8,128)(2,1)S(1)}, bf16[2,128,1024]{2,1,0:T(8,128)(2,1)S(1)}, f32[256,256]{1,0:T(8,128)...) custom-call(s32[1]{0:T(128)} %bitcast.yv.yr, ...), custom_call_target="tpu_custom_call", output_to_operand_aliasing={{0}: (17, {}), {1}: (18, {})} | custom-call | flops 6000000000 | bytes 6291456 | tf_op jit(solution)/shard_map/pallas_call | solution.py:577
  193.7 4.1 %shard_map.174 = (bf16[128,1024]{1,0:T(8,128)(2,1)S(1)}, bf16[128,1024]{1,0:T(8,128)(2,1)S(1)}, bf16[128,1152]{1,0:T(8,128)(2,1)S(1)}, bf16[128,128]{1,0:T(8,128...) custom-call(s32[1]{0:T(128)} %bitcast.yv.yr, bf16[128,1024]{1,0:T(8,128)(2,1)S(1)} %bitcast.131, ...), custom_call_target="tpu_custom_call" | custom-call | flops 6000000000 | bytes 8388608 | tf_op jit(solution)/shard_map/pallas_call | solution.py:602
  212.9 2.6 %collective-permute-done.27 = f32[205,128]{1,0:T(8,128)S(1)} collective-permute-done((f32[205,128]{1,0:T(8,128)S(1)}, f32[205,128]{1,0:T(8,128)S(1)}, u32[]{:S(2)}, u32[]{:S(2)}) %collective-permute-start.27) | collective-permute-done | bytes 104992 | tf_op jit(solution)/shard_map/ppermute | solution.py:666
  215.5 3.8 %collective-permute-start.28 = (f32[205,128]{1,0:T(8,128)S(1)}, f32[205,128]{1,0:T(8,128)S(1)}, u32[]{:S(2)}, u32[]{:S(2)}) collective-permute-start(f32[205,128]{1,0:T(8,128)S(1)} %fusion.36), channel_id=1, source_target_pairs={{0,2},{1,3},{2,0},{3,1},{4,6},{5,7},{6,4},{7,5},{8,10},{9,11},{10,... | collective-permute-start | bytes 314888 | tf_op jit(solution)/shard_map/ppermute | solution.py:670
  222.1 4.0 %collective-permute-start.29 = (f32[205,128]{1,0:T(8,128)S(1)}, f32[205,128]{1,0:T(8,128)S(1)}, u32[]{:S(2)}, u32[]{:S(2)}) collective-permute-start(f32[205,128]{1,0:T(8,128)S(1)} %add.200), channel_id=1, source_target_pairs={{0,4},{1,5},{2,6},{3,7},{4,0},{5,1},{6,2},{7,3},{8,12},{9,13},{10,... | collective-permute-start | bytes 314888 | tf_op jit(solution)/shard_map/ppermute | solution.py:670
  226.2 3.7 %collective-permute-done.29 = f32[205,128]{1,0:T(8,128)S(1)} collective-permute-done((f32[205,128]{1,0:T(8,128)S(1)}, f32[205,128]{1,0:T(8,128)S(1)}, u32[]{:S(2)}, u32[]{:S(2)}) %collective-permute-start.29) | collective-permute-done | bytes 104992 | tf_op jit(solution)/shard_map/ppermute | solution.py:670
  (286 shorter events, 90.1 us)
Async XLA Ops:
  3.1 33.7 %collective-permute-start.3 = (bf16[128,1152]{1,0:T(8,128)(2,1)}, bf16[128,1152]{1,0:T(8,128)(2,1)S(1)}, u32[]{:S(2)}, u32[]{:S(2)}) collective-permute-start(bf16[128,1152]{1,0:T(8,128)(2,1)} %pad_maximum_fusion.8), channel_id=1, source_target_pairs={{0,1},{1,0},{2,3},{3,2},{4,5},{5,4},{6,7},{7,6},{8,9},{9,8},{10,11... | collective-permute-start | bytes 884744 | tf_op jit(solution)/shard_map/ppermute | solution.py:422
  8.4 24.1 %collective-permute-start.1 = (bf16[8,5120]{1,0:T(8,128)(2,1)}, bf16[8,5120]{1,0:T(8,128)(2,1)S(1)}, u32[]{:S(2)}, u32[]{:S(2)}) collective-permute-start(bf16[8,5120]{1,0:T(8,128)(2,1)} %pad_maximum_fusion.10), channel_id=1, source_target_pairs={{1,2},{3,4},{5,6},{9,10},{11,12},{13,14},{17,18},{19,20},{21,22},{... | collective-permute-start | bytes 245768 | tf_op jit(solution)/shard_map/ppermute | solution.py:434
  9.7 24.9 %collective-permute-start.2 = (bf16[8,5120]{1,0:T(8,128)(2,1)}, bf16[8,5120]{1,0:T(8,128)(2,1)S(1)}, u32[]{:S(2)}, u32[]{:S(2)}) collective-permute-start(bf16[8,5120]{1,0:T(8,128)(2,1)} %pad_maximum_fusion.11), channel_id=1, source_target_pairs={{1,3},{3,5},{5,7},{9,11},{11,13},{13,15},{17,19},{19,21},{21,23},{... | collective-permute-start | bytes 245768 | tf_op jit(solution)/shard_map/ppermute | solution.py:435
  13.7 27.1 %collective-permute-start.4 = (bf16[2,128,1024]{2,1,0:T(8,128)(2,1)}, bf16[2,128,1024]{2,1,0:T(8,128)(2,1)S(1)}, u32[]{:S(2)}, u32[]{:S(2)}) collective-permute-start(bf16[2,128,1024]{2,1,0:T(8,128)(2,1)} %pad_maximum_fusion.4), channel_id=1, source_target_pairs={{0,1},{1,0},{2,3},{3,2},{4,5},{5,4},{6,7},{7,6},{8,9},{9,8},{10,11... | collective-permute-start | bytes 1572872 | tf_op jit(solution)/shard_map/ppermute | solution.py:443
  21.7 28.7 %collective-permute-start.6 = (bf16[2,128,1024]{2,1,0:T(8,128)(2,1)}, bf16[2,128,1024]{2,1,0:T(8,128)(2,1)S(1)}, u32[]{:S(2)}, u32[]{:S(2)}) collective-permute-start(bf16[2,128,1024]{2,1,0:T(8,128)(2,1)} %pad_maximum_fusion.5), channel_id=1, source_target_pairs={{0,1},{1,0},{2,3},{3,2},{4,5},{5,4},{6,7},{7,6},{8,9},{9,8},{10,11... | collective-permute-start | bytes 1572872 | tf_op jit(solution)/shard_map/ppermute | solution.py:443
  32.5 32.2 %collective-permute-start.8 = (bf16[2,128,1024]{2,1,0:T(8,128)(2,1)}, bf16[2,128,1024]{2,1,0:T(8,128)(2,1)S(1)}, u32[]{:S(2)}, u32[]{:S(2)}) collective-permute-start(bf16[2,128,1024]{2,1,0:T(8,128)(2,1)} %pad_maximum_fusion.6), channel_id=1, source_target_pairs={{0,1},{1,0},{2,3},{3,2},{4,5},{5,4},{6,7},{7,6},{8,9},{9,8},{10,11... | collective-permute-start | bytes 1572872 | tf_op jit(solution)/shard_map/ppermute | solution.py:443
  35.3 43.0 %collective-permute-start = (bf16[2,128,1024]{2,1,0:T(8,128)(2,1)}, bf16[2,128,1024]{2,1,0:T(8,128)(2,1)S(1)}, u32[]{:S(2)}, u32[]{:S(2)}) collective-permute-start(bf16[2,128,1024]{2,1,0:T(8,128)(2,1)} %pad_maximum_fusion.3), channel_id=1, source_target_pairs={{0,1},{1,0},{2,3},{3,2},{4,5},{5,4},{6,7},{7,6},{8,9},{9,8},{10,11... | collective-permute-start | bytes 1572872 | tf_op jit(solution)/shard_map/ppermute | solution.py:443
  40.8 84.2 %copy-start.43 = (bf16[2,256,128]{2,1,0:T(8,128)(2,1)}, bf16[2,256,128]{2,1,0:T(8,128)(2,1)S(1)}, u32[]{:S(2)}) copy-start(bf16[2,256,128]{2,1,0:T(8,128)(2,1)S(1)} %get-tuple-element.88.fe) | copy-start | bytes 393220
  44.4 13.9 %collective-permute-start.13 = (bf16[256,1024]{1,0:T(8,128)(2,1)S(1)}, bf16[256,1024]{1,0:T(8,128)(2,1)S(1)}, u32[]{:S(2)}, u32[]{:S(2)}) collective-permute-start(bf16[256,1024]{1,0:T(8,128)(2,1)S(1)} %get-tuple-element.226), channel_id=1, source_target_pairs={{2,0},{3,1},{4,2},{5,3},{6,4},{7,5},{10,8},{11,9},{12,10},{13,11},... | collective-permute-start | bytes 1572872 | tf_op jit(solution)/shard_map/ppermute | solution.py:534
  45.8 14.1 %collective-permute-start.5 = (bf16[256,1024]{1,0:T(8,128)(2,1)S(1)}, bf16[256,1024]{1,0:T(8,128)(2,1)S(1)}, u32[]{:S(2)}, u32[]{:S(2)}) collective-permute-start(bf16[256,1024]{1,0:T(8,128)(2,1)S(1)} %get-tuple-element.227), channel_id=1, source_target_pairs={{0,2},{1,3},{2,4},{3,5},{4,6},{5,7},{8,10},{9,11},{10,12},{11,13},... | collective-permute-start | bytes 1572872 | tf_op jit(solution)/shard_map/ppermute | solution.py:532
  58.6 13.0 %collective-permute-start.14 = (bf16[256,1024]{1,0:T(8,128)(2,1)S(1)}, bf16[256,1024]{1,0:T(8,128)(2,1)S(1)}, u32[]{:S(2)}, u32[]{:S(2)}) collective-permute-start(bf16[256,1024]{1,0:T(8,128)(2,1)S(1)} %add_convert_fusion.5), channel_id=1, source_target_pairs={{2,0},{3,1},{4,2},{5,3},{6,4},{7,5},{10,8},{11,9},{12,10},{13,11},... | collective-permute-start | bytes 1572872 | tf_op jit(solution)/shard_map/ppermute | solution.py:534
  60.2 13.1 %collective-permute-start.7 = (bf16[256,1024]{1,0:T(8,128)(2,1)S(1)}, bf16[256,1024]{1,0:T(8,128)(2,1)S(1)}, u32[]{:S(2)}, u32[]{:S(2)}) collective-permute-start(bf16[256,1024]{1,0:T(8,128)(2,1)S(1)} %add_convert_fusion.11), channel_id=1, source_target_pairs={{0,2},{1,3},{2,4},{3,5},{4,6},{5,7},{8,10},{9,11},{10,12},{11,13},... | collective-permute-start | bytes 1572872 | tf_op jit(solution)/shard_map/ppermute | solution.py:532
  72.0 12.0 %collective-permute-start.15 = (bf16[256,1024]{1,0:T(8,128)(2,1)S(1)}, bf16[256,1024]{1,0:T(8,128)(2,1)S(1)}, u32[]{:S(2)}, u32[]{:S(2)}) collective-permute-start(bf16[256,1024]{1,0:T(8,128)(2,1)S(1)} %add_convert_fusion.4), channel_id=1, source_target_pairs={{2,0},{3,1},{4,2},{5,3},{6,4},{7,5},{10,8},{11,9},{12,10},{13,11},... | collective-permute-start | bytes 1572872 | tf_op jit(solution)/shard_map/ppermute | solution.py:534
  73.7 12.3 %collective-permute-start.9 = (bf16[256,1024]{1,0:T(8,128)(2,1)S(1)}, bf16[256,1024]{1,0:T(8,128)(2,1)S(1)}, u32[]{:S(2)}, u32[]{:S(2)}) collective-permute-start(bf16[256,1024]{1,0:T(8,128)(2,1)S(1)} %add_convert_fusion.10), channel_id=1, source_target_pairs={{0,2},{1,3},{2,4},{3,5},{4,6},{5,7},{8,10},{9,11},{10,12},{11,13},... | collective-permute-start | bytes 1572872 | tf_op jit(solution)/shard_map/ppermute | solution.py:532
  84.5 11.1 %collective-permute-start.16 = (bf16[256,1024]{1,0:T(8,128)(2,1)S(1)}, bf16[256,1024]{1,0:T(8,128)(2,1)S(1)}, u32[]{:S(2)}, u32[]{:S(2)}) collective-permute-start(bf16[256,1024]{1,0:T(8,128)(2,1)S(1)} %add_convert_fusion.3), channel_id=1, source_target_pairs={{2,0},{3,1},{4,2},{5,3},{6,4},{7,5},{10,8},{11,9},{12,10},{13,11},... | collective-permute-start | bytes 1572872 | tf_op jit(solution)/shard_map/ppermute | solution.py:534
  86.5 11.9 %collective-permute-start.10 = (bf16[256,1024]{1,0:T(8,128)(2,1)S(1)}, bf16[256,1024]{1,0:T(8,128)(2,1)S(1)}, u32[]{:S(2)}, u32[]{:S(2)}) collective-permute-start(bf16[256,1024]{1,0:T(8,128)(2,1)S(1)} %add_convert_fusion.9), channel_id=1, source_target_pairs={{0,2},{1,3},{2,4},{3,5},{4,6},{5,7},{8,10},{9,11},{10,12},{11,13},... | collective-permute-start | bytes 1572872 | tf_op jit(solution)/shard_map/ppermute | solution.py:532
  96.9 12.3 %collective-permute-start.17 = (bf16[256,1024]{1,0:T(8,128)(2,1)}, bf16[256,1024]{1,0:T(8,128)(2,1)S(1)}, u32[]{:S(2)}, u32[]{:S(2)}) collective-permute-start(bf16[256,1024]{1,0:T(8,128)(2,1)} %add_convert_fusion.2), channel_id=1, source_target_pairs={{2,0},{3,1},{4,2},{5,3},{6,4},{7,5},{10,8},{11,9},{12,10},{13,11},... | collective-permute-start | bytes 1572872 | tf_op jit(solution)/shard_map/ppermute | solution.py:534
  99.7 12.4 %collective-permute-start.11 = (bf16[256,1024]{1,0:T(8,128)(2,1)}, bf16[256,1024]{1,0:T(8,128)(2,1)S(1)}, u32[]{:S(2)}, u32[]{:S(2)}) collective-permute-start(bf16[256,1024]{1,0:T(8,128)(2,1)} %add_convert_fusion.8), channel_id=1, source_target_pairs={{0,2},{1,3},{2,4},{3,5},{4,6},{5,7},{8,10},{9,11},{10,12},{11,13},... | collective-permute-start | bytes 1572872 | tf_op jit(solution)/shard_map/ppermute | solution.py:532
  110.5 11.9 %collective-permute-start.18 = (bf16[256,1024]{1,0:T(8,128)(2,1)}, bf16[256,1024]{1,0:T(8,128)(2,1)S(1)}, u32[]{:S(2)}, u32[]{:S(2)}) collective-permute-start(bf16[256,1024]{1,0:T(8,128)(2,1)} %add_convert_fusion.1), channel_id=1, source_target_pairs={{2,0},{3,1},{4,2},{5,3},{6,4},{7,5},{10,8},{11,9},{12,10},{13,11},... | collective-permute-start | bytes 1572872 | tf_op jit(solution)/shard_map/ppermute | solution.py:534
  113.4 11.3 %collective-permute-start.12 = (bf16[256,1024]{1,0:T(8,128)(2,1)}, bf16[256,1024]{1,0:T(8,128)(2,1)}, u32[]{:S(2)}, u32[]{:S(2)}) collective-permute-start(bf16[256,1024]{1,0:T(8,128)(2,1)} %add_convert_fusion.7), channel_id=1, source_target_pairs={{0,2},{1,3},{2,4},{3,5},{4,6},{5,7},{8,10},{9,11},{10,12},{11,13},... | collective-permute-start | bytes 1572872 | tf_op jit(solution)/shard_map/ppermute | solution.py:532
  133.1 12.3 %collective-permute-start.19 = (bf16[2,128,1024]{2,1,0:T(8,128)(2,1)S(1)}, bf16[2,128,1024]{2,1,0:T(8,128)(2,1)S(1)}, u32[]{:S(2)}, u32[]{:S(2)}) collective-permute-start(bf16[2,128,1024]{2,1,0:T(8,128)(2,1)S(1)} %get-tuple-element.117), channel_id=1, source_target_pairs={{0,1},{1,0},{2,3},{3,2},{4,5},{5,4},{6,7},{7,6},{8,9},{9,8},{10,11... | collective-permute-start | bytes 1572872 | tf_op jit(solution)/shard_map/ppermute | solution.py:596
  155.7 9.2 %collective-permute-start.20 = (bf16[2,128,1024]{2,1,0:T(8,128)(2,1)S(1)}, bf16[2,128,1024]{2,1,0:T(8,128)(2,1)S(1)}, u32[]{:S(2)}, u32[]{:S(2)}) collective-permute-start(bf16[2,128,1024]{2,1,0:T(8,128)(2,1)S(1)} %get-tuple-element.120), channel_id=1, source_target_pairs={{0,1},{1,0},{2,3},{3,2},{4,5},{5,4},{6,7},{7,6},{8,9},{9,8},{10,11... | collective-permute-start | bytes 1572872 | tf_op jit(solution)/shard_map/ppermute | solution.py:596
  173.6 9.2 %collective-permute-start.21 = (bf16[2,128,1024]{2,1,0:T(8,128)(2,1)S(1)}, bf16[2,128,1024]{2,1,0:T(8,128)(2,1)S(1)}, u32[]{:S(2)}, u32[]{:S(2)}) collective-permute-start(bf16[2,128,1024]{2,1,0:T(8,128)(2,1)S(1)} %get-tuple-element.123), channel_id=1, source_target_pairs={{0,1},{1,0},{2,3},{3,2},{4,5},{5,4},{6,7},{7,6},{8,9},{9,8},{10,11... | collective-permute-start | bytes 1572872 | tf_op jit(solution)/shard_map/ppermute | solution.py:596
  199.2 5.9 %collective-permute-start.23 = (bf16[8,5120]{1,0:T(8,128)(2,1)}, bf16[8,5120]{1,0:T(8,128)(2,1)S(1)}, u32[]{:S(2)}, u32[]{:S(2)}) collective-permute-start(bf16[8,5120]{1,0:T(8,128)(2,1)} %constant_dynamic-update-slice_fusion), channel_id=1, source_target_pairs={{2,1},{4,3},{6,5},{10,9},{12,11},{14,13},{18,17},{20,19},{22,21},{... | collective-permute-start | bytes 245768 | tf_op jit(solution)/shard_map/ppermute | solution.py:636
  199.9 5.2 %collective-permute-start.24 = (bf16[8,5120]{1,0:T(8,128)(2,1)}, bf16[8,5120]{1,0:T(8,128)(2,1)}, u32[]{:S(2)}, u32[]{:S(2)}) collective-permute-start(bf16[8,5120]{1,0:T(8,128)(2,1)} %constant_dynamic-update-slice_fusion), channel_id=1, source_target_pairs={{3,1},{5,3},{7,5},{11,9},{13,11},{15,13},{19,17},{21,19},{23,21},{... | collective-permute-start | bytes 245768 | tf_op jit(solution)/shard_map/ppermute | solution.py:637
  202.9 7.5 %collective-permute-start.26 = (f32[205,128]{1,0:T(8,128)S(1)}, f32[205,128]{1,0:T(8,128)S(1)}, u32[]{:S(2)}, u32[]{:S(2)}) collective-permute-start(f32[205,128]{1,0:T(8,128)S(1)} %bitcast.142), channel_id=1, source_target_pairs={{0,8},{8,0},{16,24},{24,16},{1,9},{9,1},{17,25},{25,17},{2,10},{10... | collective-permute-start | bytes 314888 | tf_op jit(solution)/shard_map/ppermute | solution.py:666
  203.0 16.4 %collective-permute-start.25 = (bf16[128,1152]{1,0:T(8,128)(2,1)}, bf16[128,1152]{1,0:T(8,128)(2,1)S(1)}, u32[]{:S(2)}, u32[]{:S(2)}) collective-permute-start(bf16[128,1152]{1,0:T(8,128)(2,1)} %copy-done.19), channel_id=1, source_target_pairs={{0,1},{1,0},{2,3},{3,2},{4,5},{5,4},{6,7},{7,6},{8,9},{9,8},{10,11... | collective-permute-start | bytes 884744 | tf_op jit(solution)/shard_map/ppermute | solution.py:629
  205.0 25.0 %collective-permute-start.22 = (bf16[2,128,1024]{2,1,0:T(8,128)(2,1)S(1)}, bf16[2,128,1024]{2,1,0:T(8,128)(2,1)S(1)}, u32[]{:S(2)}, u32[]{:S(2)}) collective-permute-start(bf16[2,128,1024]{2,1,0:T(8,128)(2,1)S(1)} %copy-done.16), channel_id=1, source_target_pairs={{0,1},{1,0},{2,3},{3,2},{4,5},{5,4},{6,7},{7,6},{8,9},{9,8},{10,11... | collective-permute-start | bytes 1572872 | tf_op jit(solution)/shard_map/ppermute | solution.py:596
  210.5 5.0 %collective-permute-start.27 = (f32[205,128]{1,0:T(8,128)S(1)}, f32[205,128]{1,0:T(8,128)S(1)}, u32[]{:S(2)}, u32[]{:S(2)}) collective-permute-start(f32[205,128]{1,0:T(8,128)S(1)} %bitcast_add_fusion), channel_id=1, source_target_pairs={{0,16},{8,24},{16,0},{24,8},{1,17},{9,25},{17,1},{25,9},{2,18},{10... | collective-permute-start | bytes 314888 | tf_op jit(solution)/shard_map/ppermute | solution.py:666
  215.5 6.5 %collective-permute-start.28 = (f32[205,128]{1,0:T(8,128)S(1)}, f32[205,128]{1,0:T(8,128)S(1)}, u32[]{:S(2)}, u32[]{:S(2)}) collective-permute-start(f32[205,128]{1,0:T(8,128)S(1)} %fusion.36), channel_id=1, source_target_pairs={{0,2},{1,3},{2,0},{3,1},{4,6},{5,7},{6,4},{7,5},{8,10},{9,11},{10,... | collective-permute-start | bytes 314888 | tf_op jit(solution)/shard_map/ppermute | solution.py:670
  222.1 7.8 %collective-permute-start.29 = (f32[205,128]{1,0:T(8,128)S(1)}, f32[205,128]{1,0:T(8,128)S(1)}, u32[]{:S(2)}, u32[]{:S(2)}) collective-permute-start(f32[205,128]{1,0:T(8,128)S(1)} %add.200), channel_id=1, source_target_pairs={{0,4},{1,5},{2,6},{3,7},{4,0},{5,1},{6,2},{7,3},{8,12},{9,13},{10,... | collective-permute-start | bytes 314888 | tf_op jit(solution)/shard_map/ppermute | solution.py:670
  229.9 4.8 %collective-permute-start.30 = (f32[205,128]{1,0:T(8,128)S(1)}, f32[205,128]{1,0:T(8,128)S(1)}, u32[]{:S(2)}, u32[]{:S(2)}) collective-permute-start(f32[205,128]{1,0:T(8,128)S(1)} %add.201), channel_id=1, source_target_pairs={{0,1},{1,0},{2,3},{3,2},{4,5},{5,4},{6,7},{7,6},{8,9},{9,8},{10,11... | collective-permute-start | bytes 314888 | tf_op jit(solution)/shard_map/ppermute | solution.py:672
  (63 other events, 556.4 us)

commit v2 on v1

v2 whole, which is shorter than its diff:
```python
import jax
import jax.numpy as jnp
import numpy as np
from jax import lax
from jax.experimental import pallas as pl
from jax.experimental.pallas import tpu as pltpu
from jax.sharding import PartitionSpec as P

N = 256
Q = 128
HEAD = 64
SUB = 256
LOG2E = 1.4426950408889634
F32 = jnp.float32
BF16 = jnp.bfloat16
NEG = -1e30


def params():
    return pltpu.CompilerParams(vmem_limit_bytes=14 * 1024 * 1024)


def cost(micros, nbytes):
    return pl.CostEstimate(flops=int(micros * 1e9), bytes_accessed=nbytes, transcendentals=0)


def dot(a, b):
    return jnp.dot(a, b, preferred_element_type=F32)


def dot_tb(a, b):
    return lax.dot_general(a, b, (((1,), (1,)), ((), ())), preferred_element_type=F32)


def dot_ta(a, b):
    return lax.dot_general(a, b, (((0,), (0,)), ((), ())), preferred_element_type=F32)


def halves(v):
    hi = v.astype(BF16)
    return hi, (v - hi.astype(F32)).astype(BF16)


def split_dot(v, m):
    hi, lo = halves(v)
    return dot(hi, m) + dot(lo, m)


def exact_dot(m, v):
    hi = v.astype(BF16)
    rest = v - hi.astype(F32)
    mid = rest.astype(BF16)
    low = (rest - mid.astype(F32)).astype(BF16)
    return dot(m, hi) + dot(m, mid) + dot(m, low)


def triangle(lower):
    row = lax.broadcasted_iota(jnp.int32, (Q, Q), 0)
    col = lax.broadcasted_iota(jnp.int32, (Q, Q), 1)
    return row >= col if lower else row <= col


def in_order(y, own, rec, dst, first=0):
    rows = own.shape[0]

    @pl.when(y == 0)
    def _():
        dst[first : first + rows] = own.astype(dst.dtype)
        dst[first + rows : first + 2 * rows] = rec.astype(dst.dtype)

    @pl.when(y != 0)
    def _():
        dst[first : first + rows] = rec.astype(dst.dtype)
        dst[first + rows : first + 2 * rows] = own.astype(dst.dtype)


def conv_sum(xs, w, bias, rows):
    total = bias[...]
    for k in range(4):
        total = total + w[k : k + 1] * xs[5 + k : 5 + k + rows]
    return total


def gates(s):
    sig = 0.5 + 0.5 * jnp.tanh(0.5 * s)
    out = s * sig
    return out, sig + out * (1.0 - sig)


def conv_back(ds, xs, gs, w, rows):
    gs[0:rows] = ds
    gs[rows : rows + 8] = jnp.zeros((8, ds.shape[1]), F32)
    dx = w[3:4] * ds
    for k in range(3):
        dx = dx + w[k : k + 1] * gs[3 - k : 3 - k + rows]
    dw = [jnp.sum(ds * xs[5 + k : 5 + k + rows], axis=0, keepdims=True) for k in range(4)]
    dw.append(jnp.sum(ds, axis=0, keepdims=True))
    dw.append(jnp.zeros((3, ds.shape[1]), F32))
    return dx, jnp.concatenate(dw, axis=0)


def pack_small_kernel(yv, b, c, dt, xr, br, cr, msg_ref, rim_ref):
    width = b.shape[1]
    msg_ref[:, 0:width] = b[...]
    msg_ref[:, width : 2 * width] = c[...]
    msg_ref[:, 2 * width :] = dt[...]
    half = xr.shape[1] // 2
    for k in range(2):
        rim_ref[k, :, 0:half] = xr[:, k * half : (k + 1) * half]
        rim_ref[k, :, half : half + width] = br[:, k * width : (k + 1) * width]
        rim_ref[k, :, half + width :] = cr[:, k * width : (k + 1) * width]


def pack_kernel(yv, x, dy, out):
    out[0] = x[...]
    out[1] = dy[...]


def unpack_kernel(yv, got, y_ref, gx_ref):
    y_ref[...] = got[0]
    gx_ref[...] = got[1]


def setup_kernel(
    yv, b_own, c_own, dt_own, rec, rim0, rim1, wb, wc, bb, bc_, par, exp2,
    halo_ref, bc_ref, cc_ref, bt_ref, ct_ref, ds_ref, fe_ref, rows_ref, cols_ref, rowt_ref, st_ref,
    xs, dts, xs2,
):
    y = yv[0]
    width = b_own.shape[1]
    heads = par.shape[1]
    half = halo_ref.shape[1] - 2 * width
    halo_ref[...] = (rim0[...].astype(F32) + rim1[...].astype(F32))[8:16]
    for i, (own, w, bias, out, out_t) in enumerate(
        ((b_own, wb, bb, bc_ref, bt_ref), (c_own, wc, bc_, cc_ref, ct_ref))
    ):
        at = i * width
        xs[0:8] = halo_ref[:, half + at : half + at + width]
        in_order(y, own[...], rec[:, at : at + width], xs, 8)
        v, slope = gates(conv_sum(xs, w, bias, 2 * Q))
        out[...] = v.astype(BF16)
        out_t[...] = jnp.transpose(v).astype(BF16)
        ds_ref[i] = slope

    @pl.when(y == 0)
    def _():
        dts[0:Q] = dt_own[:, 0:heads].astype(F32)
        dts[Q : 2 * Q] = rec[:, 2 * width : 2 * width + heads].astype(F32)

    @pl.when(y != 0)
    def _():
        dts[0:Q] = rec[:, 2 * width + heads : 2 * width + 2 * heads].astype(F32)
        dts[Q : 2 * Q] = dt_own[:, heads : 2 * heads].astype(F32)

    raw = dts[...] + par[1:2]
    step = jnp.log1p(jnp.exp(raw))
    logs = -step * jnp.exp(par[0:1])
    tri = jnp.where(triangle(True), 1.0, 0.0).astype(BF16)
    run0 = exact_dot(tri, logs[0:Q])
    run1 = exact_dot(tri, logs[Q:])
    tot0, tot1 = run0[Q - 1 : Q], run1[Q - 1 : Q]
    run = jnp.concatenate([run0, run1], axis=0)
    to_end = jnp.concatenate([jnp.exp(tot0 - run0), jnp.exp(tot1 - run1)], axis=0)
    hi, lo = halves(step * to_end)
    fe_ref[0] = jnp.concatenate([hi, lo], axis=1)
    hi, lo = halves(jnp.exp(run))
    fe_ref[1] = jnp.concatenate([hi, lo], axis=1)
    st_ref[...] = jnp.concatenate([step, raw], axis=1)
    small = jnp.concatenate(
        [jnp.exp(tot0), jnp.exp(tot1), jnp.exp(tot0 + tot1), par[2:3], jnp.zeros((4, heads), F32)],
        axis=0,
    )
    hi, lo = halves(small)
    rows_ref[...] = dot(jnp.concatenate([hi, lo], axis=1), exp2[...])
    r2 = run * LOG2E
    q2 = (run - jnp.log(step)) * LOG2E
    xs2[...] = jnp.transpose(jnp.concatenate([r2, q2], axis=1))
    for j in range(heads // 4):
        cols_ref[j] = jnp.concatenate([r2[:, 4 * j : 4 * j + 4], q2[:, 4 * j : 4 * j + 4]], axis=1)
        rowt_ref[j] = jnp.concatenate(
            [xs2[4 * j : 4 * j + 4], xs2[heads + 4 * j : heads + 4 * j + 4]], axis=0
        )


def state_kernel(
    yv, x_own, dy_own, rec, halo, w, bias, bt, ct, fe, exp2, rows,
    t_ref, u_ref, xc_ref, dyo_ref, sl_ref, xs,
):
    y = yv[0]
    xs[0:8] = halo[...]
    in_order(y, x_own[...], rec[0], xs, 8)
    in_order(y, dy_own[...], rec[1], dyo_ref)
    v, slope = gates(conv_sum(xs, w, bias, 2 * Q))
    xc = v.astype(BF16)
    xc_ref[...] = xc
    sl_ref[...] = slope.astype(BF16)
    wt = (xc.astype(F32) * dot(fe[0], exp2[...])).astype(BF16)
    dyr = (dyo_ref[...].astype(F32) * dot(fe[1], exp2[...])).astype(BF16)
    top, end = slice(0, Q), slice(Q, 2 * Q)
    t_ref[0] = (rows[1:2] * dot(bt[:, top], wt[top]) + dot(bt[:, end], wt[end])).astype(BF16)
    u_ref[0] = (dot(ct[:, top], dyr[top]) + rows[0:1] * dot(ct[:, end], dyr[end])).astype(BF16)


def hop_kernel(yv, in_e, in_o, t, u, row_f, row_b, out_e, out_o):
    @pl.when(yv[2] == 0)
    def _():
        out_e[...] = (row_f[2:3] * in_o[...].astype(F32) + t[0].astype(F32)).astype(BF16)
        out_o[...] = (row_b[2:3] * in_e[...].astype(F32) + u[0].astype(F32)).astype(BF16)

    @pl.when(yv[2] != 0)
    def _():
        out_o[...] = (row_f[2:3] * in_e[...].astype(F32) + t[0].astype(F32)).astype(BF16)
        out_e[...] = (row_b[2:3] * in_o[...].astype(F32) + u[0].astype(F32)).astype(BF16)


def within_kernel(yv, xc, dyo, cols, rowt, bc, cc, yi_ref, dxi_ref, dcb_ref, cb):
    @pl.when(pl.program_id(0) == 0)
    def _():
        dcb_ref[...] = jnp.zeros(dcb_ref.shape, F32)
        for b in range(2):
            at = slice(b * Q, b * Q + Q)
            cb[b] = dot_tb(cc[at], bc[at])
            cb[2 + b] = dot_tb(bc[at], cc[at])

    low = triangle(True)
    high = triangle(False)
    lane = lax.broadcasted_iota(jnp.int32, (1, 2 * HEAD), 1)
    first = jnp.where(lane < HEAD, 1.0, 0.0).astype(BF16)
    second = jnp.where(lane < HEAD, 0.0, 1.0).astype(BF16)
    for b in range(2):
        at = slice(b * Q, b * Q + Q)
        dcb = dcb_ref[b]
        for p in range(2):
            ls = slice(p * 2 * HEAD, (p + 1) * 2 * HEAD)
            xp = xc[at, ls]
            dyp = dyo[at, ls]
            xbd = jnp.concatenate([xp * first, xp * second], axis=0)
            dbd = jnp.concatenate([dyp * first, dyp * second], axis=0)
            decay, mix, mixt = [], [], []
            for i in range(2):
                h = 2 * p + i
                ex = cols[0, at, h : h + 1] - rowt[0, 4 + h : 5 + h, at]
                lt = jnp.exp2(jnp.where(low, ex, NEG))
                ext = rowt[0, h : h + 1, at] - cols[0, at, 4 + h : 5 + h]
                ltt = jnp.exp2(jnp.where(high, ext, NEG))
                decay.append(lt)
                mix.append((cb[b] * lt).astype(BF16))
                mixt.append((cb[2 + b] * ltt).astype(BF16))
            yi_ref[at, ls] = dot(jnp.concatenate(mix, axis=1), xbd)
            dxi_ref[at, ls] = dot(jnp.concatenate(mixt, axis=1), dbd)
            dm = dot_tb(dyp, xbd)
            dcb = dcb + dm[:, 0:Q] * decay[0] + dm[:, Q:] * decay[1]
        dcb_ref[b] = dcb


def fetch(spot, choices, dst, sem):
    @pl.when(spot == 0)
    def _():
        dst[...] = jnp.zeros(dst.shape, dst.dtype)

    for k, src in enumerate(choices, 1):

        @pl.when(spot == k)
        def _():
            copy = pltpu.make_async_copy(src, dst, sem)
            copy.start()
            copy.wait()


def across_kernel(
    yv, x_own, rec, halo, w, xc, dyo, sl, yi, dxi, bc, cc, bt, ct, fe, exp2, seg, rows, *rest
):
    hops = (len(rest) - 16) // 2
    (y_ref, gx_ref, red_ref, head_ref, send_ref, dc_ref, db_ref, wv_ref, ends_ref) = rest[2 * hops : -7]
    xs, gs, gy, ent, lea, sem0, sem1 = rest[-7:]
    y = yv[0]

    @pl.when(pl.program_id(0) == 0)
    def _():
        dc_ref[...] = jnp.zeros(dc_ref.shape, F32)
        db_ref[...] = jnp.zeros(db_ref.shape, F32)
        wv_ref[...] = jnp.zeros(wv_ref.shape, F32)
        fetch(yv[1], rest[:hops], ent, sem0)
        fetch(hops - yv[1], rest[hops : 2 * hops], lea, sem1)

    at = pl.multiple_of(pl.program_id(0) * SUB, SUB)
    xs[0:8] = halo[...]
    in_order(y, x_own[...], rec[0], xs, 8)
    x = xc[...].astype(F32)
    dy = dyo[...].astype(F32)
    f = dot(fe[0], exp2[...])
    er = dot(fe[1], exp2[...])
    wt = (x * f).astype(BF16)
    dyr = (dy * er).astype(BF16)
    d0, d1, skip = rows[0:1], rows[1:2], rows[3:4]
    top, end = slice(0, Q), slice(Q, 2 * Q)
    e0 = ent[:, pl.ds(at, SUB)]
    r1 = lea[:, pl.ds(at, SUB)]
    e1 = (d0 * e0.astype(F32) + dot(bt[:, top], wt[top])).astype(BF16)
    r0 = (d1 * r1.astype(F32) + dot(ct[:, end], dyr[end])).astype(BF16)
    over = jnp.concatenate([dot(cc[top], e0), dot(cc[end], e1)], axis=0) * er
    back = jnp.concatenate([dot(bc[top], r0), dot(bc[end], r1)], axis=0) * f
    yn = yi[...] + over
    dxn = dxi[...] + back
    dc_ref[top] += dot_tb(dyr[top], e0)
    dc_ref[end] += dot_tb(dyr[end], e1)
    db_ref[top] += dot_tb(wt[top], r0)
    db_ref[end] += dot_tb(wt[end], r1)
    wv_ref[0] += split_dot(dy * yn, seg[...])
    wv_ref[1] += split_dot(x * dxn, seg[...])
    xb = x * back
    ends_ref[...] = jnp.concatenate(
        [
            jnp.sum(xb[top], axis=0, keepdims=True)
            + d0 * jnp.sum(r0.astype(F32) * e0.astype(F32), axis=0, keepdims=True),
            jnp.sum(xb[end], axis=0, keepdims=True)
            + d1 * jnp.sum(r1.astype(F32) * e1.astype(F32), axis=0, keepdims=True),
            jnp.sum(x * dy, axis=0, keepdims=True),
            jnp.zeros((5, SUB), F32),
        ],
        axis=0,
    )
    ds = (dxn + skip * dy) * sl[...].astype(F32)
    gx, dw = conv_back(ds, xs, gs, w, 2 * Q)
    red_ref[...] = dw
    head_ref[...] = ds[0:8]
    gy[0] = (yn + skip * x).astype(BF16)
    gy[1] = gx.astype(BF16)

    @pl.when(y == 0)
    def _():
        y_ref[...] = gy[0, top]
        gx_ref[...] = gy[1, top]
        send_ref[...] = gy[:, end]

    @pl.when(y != 0)
    def _():
        y_ref[...] = gy[0, end]
        gx_ref[...] = gy[1, end]
        send_ref[...] = gy[:, top]


def finish_group(
    yv, b_own, c_own, b_rec, c_rec, b_halo, c_halo, wb, wc, slope, bc, cc, parts,
    gb_ref, gc_ref, red_ref, head_ref, send_ref, xs, gs, gv,
):
    y = yv[0]
    dc, db, dcb = [sum(r[...] for r in refs[1:]) + refs[0][...] for refs in zip(*parts)]
    dcb = dcb.astype(BF16)
    for b in range(2):
        at = slice(b * Q, b * Q + Q)
        gv[0, at] = db[at] + dot_ta(dcb[b], cc[at])
        gv[1, at] = dc[at] + dot(dcb[b], bc[at])
    for i, (own, rec, halo, w, out) in enumerate(
        ((b_own, b_rec, b_halo, wb, gb_ref), (c_own, c_rec, c_halo, wc, gc_ref))
    ):
        cs = slice(i * N, (i + 1) * N)
        xs[0:8] = halo[...]
        in_order(y, own[...], rec[...], xs, 8)
        ds = gv[i] * slope[i]
        gx, dw = conv_back(ds, xs, gs, w, 2 * Q)
        red_ref[:, cs] = dw
        head_ref[:, cs] = ds[0:8]

        @pl.when(y == 0)
        def _():
            out[...] = gx[0:Q].astype(BF16)
            send_ref[:, cs] = gx[Q:].astype(BF16)

        @pl.when(y != 0)
        def _():
            out[...] = gx[Q:].astype(BF16)
            send_ref[:, cs] = gx[0:Q].astype(BF16)


def finish_kernel(
    yv, b_own, c_own, b_rec, c_rec, b_halo, c_halo, wb, wc, slope, bc, cc,
    dc0, db0, dcb0, dc1, db1, dcb1,
    gb_ref, gc_ref, red_ref, head_ref, send_ref, xs, gs, gv,
):
    finish_group(
        yv, b_own, c_own, b_rec, c_rec, b_halo, c_halo, wb, wc, slope, bc, cc,
        [(dc0, db0, dcb0), (dc1, db1, dcb1)],
        gb_ref, gc_ref, red_ref, head_ref, send_ref, xs, gs, gv,
    )
    red_ref[:, 2 * N :] = jnp.zeros((8, red_ref.shape[1] - 2 * N), F32)
    head_ref[:, 2 * N :] = jnp.zeros((8, head_ref.shape[1] - 2 * N), F32)


def finish_last_kernel(
    yv, b_own, c_own, b_rec, c_rec, b_halo, c_halo, wb, wc, slope, bc, cc,
    dc0, db0, dcb0, dc1, db1, dcb1, st, par, seg, *rest,
):
    chunks = (len(rest) - 10) // 2
    wvs, ends, rest = rest[:chunks], rest[chunks : 2 * chunks], rest[2 * chunks :]
    gb_ref, gc_ref, red_ref, head_ref, send_ref, gdt_ref, xs, gs, gv, gd = rest
    y = yv[0]
    finish_group(
        yv, b_own, c_own, b_rec, c_rec, b_halo, c_halo, wb, wc, slope, bc, cc,
        [(dc0, db0, dcb0), (dc1, db1, dcb1)],
        gb_ref, gc_ref, red_ref, head_ref, send_ref, xs, gs, gv,
    )
    heads = par.shape[1]
    step, raw = st[:, 0:heads], st[:, heads:]
    rate = jnp.exp(par[0:1])
    cw = ends[0].shape[1]
    w_sum = sum(wv[0] for wv in wvs[1:]) + wvs[0][0]
    v_sum = sum(wv[1] for wv in wvs[1:]) + wvs[0][1]
    e_sum = split_dot(ends[0][...], seg[0:cw])
    for i in range(1, chunks):
        e_sum = e_sum + split_dot(ends[i][...], seg[i * cw : (i + 1) * cw])
    tri = jnp.where(triangle(False), 1.0, 0.0).astype(BF16)
    diff = w_sum - v_sum
    dl = jnp.concatenate(
        [exact_dot(tri, diff[0:Q]) + e_sum[0:1], exact_dot(tri, diff[Q:]) + e_sum[1:2]], axis=0
    )
    draw = (v_sum / step - rate * dl) / (1.0 + jnp.exp(-raw))
    red_ref[:, 2 * N :] = jnp.concatenate(
        [
            jnp.concatenate(
                [
                    jnp.sum(dl * (-rate * step), axis=0, keepdims=True),
                    jnp.sum(draw, axis=0, keepdims=True),
                    e_sum[2:3],
                    jnp.zeros((5, heads), F32),
                ],
                axis=0,
            ),
            jnp.zeros((8, red_ref.shape[1] - 2 * N - heads), F32),
        ],
        axis=1,
    )
    head_ref[:, 2 * N :] = jnp.zeros((8, head_ref.shape[1] - 2 * N), F32)
    gd[...] = jnp.concatenate([draw, draw], axis=1).astype(BF16)

    @pl.when(y == 0)
    def _():
        gdt_ref[...] = gd[0:Q]
        send_ref[:, 2 * N :] = gd[Q:]

    @pl.when(y != 0)
    def _():
        gdt_ref[...] = gd[Q:]
        send_ref[:, 2 * N :] = gd[0:Q]


def add_kernel(yv, *refs):
    total = refs[0][...]
    for r in refs[1:-1]:
        total = total + r[...]
    refs[-1][...] = total


def close_kernel(yv, got0, got1, gdt_own, gb_ref, gc_ref, gdt_ref):
    at = [got0, got1]
    for g in range(2):
        gb_ref[:, g * N : (g + 1) * N] = at[g][:, 0:N]
        gc_ref[:, g * N : (g + 1) * N] = at[g][:, N : 2 * N]
    lane = lax.broadcasted_iota(jnp.int32, gdt_own.shape, 1)
    low = lane < gdt_own.shape[1] // 2
    own, got = gdt_own[...].astype(F32), got1[:, 2 * N :].astype(F32)

    @pl.when(yv[0] == 0)
    def _():
        gdt_ref[...] = jnp.where(low, own, got).astype(BF16)

    @pl.when(yv[0] != 0)
    def _():
        gdt_ref[...] = jnp.where(low, got, own).astype(BF16)


def rim_kernel(yv, next0, next1, w, gx, gb, gc, gx_ref, gb_ref, gc_ref):
    wide = gx.shape[1] // 2
    base = next0.shape[1] - wide
    step = base // 2

    def add(src, dst, pieces):
        at = 0
        for ref, lo, size, wlo in pieces:
            h = ref[:, lo : lo + size]
            k = w[:, wlo : wlo + size]
            more = jnp.concatenate(
                [
                    jnp.zeros((13, size), F32),
                    k[0:1] * h[0:1],
                    k[0:1] * h[1:2] + k[1:2] * h[0:1],
                    k[0:1] * h[2:3] + k[1:2] * h[1:2] + k[2:3] * h[0:1],
                ],
                axis=0,
            )
            dst[:, at : at + size] = (src[:, at : at + size].astype(F32) + more).astype(BF16)
            at += size

    both = (next0, next1)
    add(gx, gx_ref, [(both[k], base, wide, k * wide) for k in range(2)])
    for i, (src, dst) in enumerate(((gb, gb_ref), (gc, gc_ref))):
        first = 2 * wide + i * 4 * N
        add(
            src, dst,
            [(both[k], g * step + i * N, N, first + (2 * k + g) * N) for k in range(2) for g in range(2)],
        )


def sums_kernel(yv, mine, theirs, gw_ref, gb_ref, gh_ref, both, *, wide):
    width = mine.shape[2]

    @pl.when(yv[3] == 0)
    def _():
        both[:, :, 0:width] = mine[...]
        both[:, :, width:] = theirs[...]

    @pl.when(yv[3] != 0)
    def _():
        both[:, :, 0:width] = theirs[...]
        both[:, :, width:] = mine[...]

    base = 2 * width - wide
    step = base // 2
    heads = gh_ref.shape[1] // 2

    def fill(order):
        for k in range(2):
            v = both[order[k]]
            gw_ref[:, k * wide : (k + 1) * wide] = v[0:4, base:]
            gb_ref[:, k * wide : (k + 1) * wide] = v[4:5, base:]
            for i in range(2):
                for g in range(2):
                    to = 2 * wide + i * 4 * N + (2 * k + g) * N
                    gw_ref[:, to : to + N] = v[0:4, g * step + i * N : g * step + (i + 1) * N]
                    gb_ref[:, to : to + N] = v[4:5, g * step + i * N : g * step + (i + 1) * N]
        at = step + 2 * N
        gh_ref[...] = jnp.concatenate(
            [both[order[0]][:, at : at + heads], both[order[1]][:, at : at + heads]], axis=1
        )

    @pl.when(yv[0] == 0)
    def _():
        fill((0, 1))

    @pl.when(yv[0] != 0)
    def _():
        fill((1, 0))


def whole(shape):
    return pl.BlockSpec(shape, lambda *_: (0,) * len(shape))


def shape_of(*dims, dtype=F32):
    return jax.ShapeDtypeStruct(dims, dtype)


def call(kernel, yv, grid, ins, outs, scratch, micros, nbytes, keep=(), after=()):
    count = len(ins)
    extra = len(keep) + len(after)

    def run(yr, *refs):
        kernel(yr, *refs[:count], *refs[count + extra :])

    anywhere = pl.BlockSpec(memory_space=pl.ANY)
    return pl.pallas_call(
        run,
        out_shape=[o[0] for o in outs],
        grid_spec=pltpu.PrefetchScalarGridSpec(
            num_scalar_prefetch=1,
            grid=grid,
            in_specs=[i[1] for i in ins] + [anywhere] * extra,
            out_specs=[o[1] for o in outs],
            scratch_shapes=scratch,
        ),
        compiler_params=params(),
        cost_estimate=cost(micros, nbytes),
        input_output_aliases={1 + count + k: k for k in range(len(keep))},
    )(yv, *[i[0] for i in ins], *keep, *after)


def per_device(
    ssm_input, b_input, c_input, dt_input, conv_weight, conv_bias, a_log, dt_bias, skip_gain, grad_out
):
    x_rows, b_rows, c_rows = ssm_input[0], b_input[0], c_input[0]
    dt_rows, dy_rows = dt_input[0], grad_out[0]
    devices = lax.axis_size("sp")
    dp_size = lax.axis_size("dp")
    spots = devices // 2
    me = lax.axis_index("sp")
    y = lax.rem(me, 2)
    z = me // 2
    core = lax.rem(lax.axis_index("dp"), 2)
    yv = jnp.stack([y, z, lax.rem(z, 2), core]).astype(jnp.int32)
    xw = x_rows.shape[1] // 2
    bw = b_rows.shape[1] // 2
    hl = dt_rows.shape[1] // 2
    chunks = 4
    cw = xw // chunks
    subs = cw // SUB
    groups = bw // N
    per_group = chunks // groups
    two = 2 * Q
    piece = 2 * N + 2 * hl
    base = groups * piece
    bands = base // SUB
    bias = conv_bias[None]

    def pairs(fn, n=devices):
        return [(i, fn(i)) for i in range(n) if fn(i) is not None and 0 <= fn(i) < n]

    swap = pairs(lambda i: i ^ 1)

    def cols(width, other, step=1, plus=0):
        if other:
            return pl.BlockSpec((Q, width), lambda j, yr: (0, (1 - yr[0]) * step + plus))
        return pl.BlockSpec((Q, width), lambda j, yr: (0, yr[0] * step + plus))

    def tail(width):
        return pl.BlockSpec((16, width), lambda j, yr: (Q // 16 - 1, 0))

    msg, rims = call(
        pack_small_kernel, yv, (1,),
        [
            (b_rows, cols(bw, True)), (c_rows, cols(bw, True)), (dt_rows, whole(dt_rows.shape)),
            (x_rows, tail(2 * xw)), (b_rows, tail(2 * bw)), (c_rows, tail(2 * bw)),
        ],
        [
            (shape_of(Q, 2 * bw + 2 * hl, dtype=BF16), whole((Q, 2 * bw + 2 * hl))),
            (shape_of(2, 16, xw + 2 * bw, dtype=BF16), whole((2, 16, xw + 2 * bw))),
        ],
        [], 1, 2 << 20,
    )
    rec_bc = lax.ppermute(msg, "sp", swap)
    rim0 = lax.ppermute(rims[0], "sp", pairs(lambda i: i + 1 if i % 2 else None))
    rim1 = lax.ppermute(rims[1], "sp", pairs(lambda i: i + 2 if i % 2 else None))

    rec = []

    def send_chunk(c, after):
        (out,) = call(
            pack_kernel, yv, (1,),
            [(x_rows, cols(cw, True, chunks, c)), (dy_rows, cols(cw, True, chunks, c))],
            [(shape_of(2, Q, cw, dtype=BF16), whole((2, Q, cw)))],
            [], 1, 1 << 20, after=after,
        )
        rec.append(lax.ppermute(out, "sp", swap))

    send_chunk(0, [msg])

    par = lax.dynamic_slice_in_dim(
        jnp.concatenate([jnp.stack([a_log, dt_bias, skip_gain]), jnp.zeros((5, 2 * hl), F32)], 0),
        y * hl, hl, 1,
    )
    lanes = np.arange(xw) // HEAD
    expand = (np.arange(hl)[:, None] == lanes[None, :]).astype(BF16)
    exp2 = jnp.asarray(np.concatenate([expand, expand], axis=0))
    seg = jnp.asarray(np.ascontiguousarray(expand.T))

    nq = hl // 4
    first_b, first_c = 2 * xw // bw, 2 * xw // bw + 2

    def wide_w(rows_, at):
        return pl.BlockSpec((rows_, bw), lambda j, yr: (0, at + yr[0]))

    halo, bcc, ccc, bct, cct, slopes, fe, rows, qcols, rowt, st = call(
        setup_kernel, yv, (1,),
        [
            (b_rows, cols(bw, False)), (c_rows, cols(bw, False)), (dt_rows, whole(dt_rows.shape)),
            (rec_bc, whole(rec_bc.shape)), (rim0, whole(rim0.shape)), (rim1, whole(rim1.shape)),
            (conv_weight, wide_w(4, first_b)), (conv_weight, wide_w(4, first_c)),
            (bias, wide_w(1, first_b)), (bias, wide_w(1, first_c)),
            (par, whole((8, hl))), (exp2, whole((2 * hl, xw))),
        ],
        [
            (shape_of(8, xw + 2 * bw), whole((8, xw + 2 * bw))),
            (shape_of(two, bw, dtype=BF16), whole((two, bw))),
            (shape_of(two, bw, dtype=BF16), whole((two, bw))),
            (shape_of(bw, two, dtype=BF16), whole((bw, two))),
            (shape_of(bw, two, dtype=BF16), whole((bw, two))),
            (shape_of(2, two, bw), whole((2, two, bw))),
            (shape_of(2, two, 2 * hl, dtype=BF16), whole((2, two, 2 * hl))),
            (shape_of(8, xw), whole((8, xw))),
            (shape_of(nq, two, 8), whole((nq, two, 8))),
            (shape_of(nq, 8, two), whole((nq, 8, two))),
            (shape_of(two, 2 * hl), whole((two, 2 * hl))),
        ],
        [
            pltpu.VMEM((two + 8, bw), F32), pltpu.VMEM((two, hl), F32),
            pltpu.VMEM((2 * hl, two), F32),
        ],
        4, 4 << 20,
    )
    send_chunk(1, [rec_bc])

    def own(c):
        return pl.BlockSpec((Q, SUB), lambda j, yr: (0, (yr[0] * chunks + c) * subs + j))

    def weight(rows_, c):
        return pl.BlockSpec((rows_, SUB), lambda j, yr: (0, (yr[0] * chunks + c) * subs + j))

    def band(rows_, c, first=0):
        return pl.BlockSpec((rows_, SUB), lambda j, yr: (0, first + c * subs + j))

    def group(c):
        return pl.BlockSpec((two, N), lambda j, yr: (0, c // per_group))

    def group_t(c):
        return pl.BlockSpec((N, two), lambda j, yr: (c // per_group, 0))

    local = pl.BlockSpec((two, SUB), lambda j, yr: (0, j))
    local8 = pl.BlockSpec((8, SUB), lambda j, yr: (0, j))
    wave = pl.BlockSpec((N, SUB), lambda j, yr: (0, j))
    arrived = pl.BlockSpec((2, Q, SUB), lambda j, yr: (0, 0, j))

    states = []
    xcs, dyos, sls = [], [], []

    def state(c, after):
        nonlocal states
        slot = pl.BlockSpec((1, N, SUB), lambda j, yr: (c, 0, j))
        big = shape_of(chunks, N, cw, dtype=BF16)
        tall = shape_of(two, cw, dtype=BF16)
        t, u, xc, dyo, sl = call(
            state_kernel, yv, (subs,),
            [
                (x_rows, own(c)), (dy_rows, own(c)), (rec[c], arrived), (halo, band(8, c)),
                (conv_weight, weight(4, c)), (bias, weight(1, c)), (bct, group_t(c)),
                (cct, group_t(c)), (fe, whole(fe.shape)), (exp2, band(2 * hl, c)), (rows, band(8, c)),
            ],
            [(big, slot), (big, slot), (tall, local), (tall, local), (tall, local)],
            [pltpu.VMEM((two + 8, SUB), F32)],
            3, 4 << 20, keep=states, after=after,
        )
        states = [t, u]
        xcs.append(xc)
        dyos.append(dyo)
        sls.append(sl)
        return xc

    yis, dxis, dcbs = [], [], []

    def within(c, after):
        yi, dxi, dcb = call(
            within_kernel, yv, (subs,),
            [
                (xcs[c], local), (dyos[c], local),
                (qcols, pl.BlockSpec((1, two, 8), lambda j, yr: (c * subs + j, 0, 0))),
                (rowt, pl.BlockSpec((1, 8, two), lambda j, yr: (c * subs + j, 0, 0))),
                (bcc, group(c)), (ccc, group(c)),
            ],
            [
                (shape_of(two, cw), local), (shape_of(two, cw), local),
                (shape_of(2, Q, Q), whole((2, Q, Q))),
            ],
            [pltpu.VMEM((4, Q, Q), F32)],
            3, 4 << 20, after=after,
        )
        yis.append(yi)
        dxis.append(dxi)
        dcbs.append(dcb)
        return dcb

    finals = []
    sums = []
    got_x = []

    def across(c, ents, leas, after):
        nonlocal finals
        full = shape_of(Q, 2 * xw, dtype=BF16)
        strip = shape_of(8, base + xw)
        out = call(
            across_kernel, yv, (subs,),
            [
                (x_rows, own(c)), (rec[c], pl.BlockSpec((1, Q, SUB), lambda j, yr: (0, 0, j))),
                (halo, band(8, c)), (conv_weight, weight(4, c)), (xcs[c], local), (dyos[c], local),
                (sls[c], local), (yis[c], local), (dxis[c], local),
                (bcc, group(c)), (ccc, group(c)), (bct, group_t(c)), (cct, group_t(c)),
                (fe, whole(fe.shape)), (exp2, band(2 * hl, c)),
                (seg, pl.BlockSpec((SUB, hl), lambda j, yr: (c * subs + j, 0))), (rows, band(8, c)),
            ] + [(v, pl.BlockSpec(memory_space=pl.ANY)) for v in ents + leas],
            [
                (full, own(c)), (full, own(c)), (strip, band(8, c, bands)), (strip, band(8, c, bands)),
                (shape_of(2, Q, cw, dtype=BF16), arrived), (shape_of(two, N), whole((two, N))),
                (shape_of(two, N), whole((two, N))), (shape_of(2, two, hl), whole((2, two, hl))),
                (shape_of(8, cw), local8),
            ],
            [
                pltpu.VMEM((two + 8, SUB), F32), pltpu.VMEM((two + 8, SUB), F32),
                pltpu.VMEM((2, two, SUB), BF16), pltpu.VMEM((N, cw), BF16), pltpu.VMEM((N, cw), BF16),
                pltpu.SemaphoreType.DMA, pltpu.SemaphoreType.DMA,
            ],
            6, 6 << 20, keep=finals, after=after,
        )
        finals = list(out[:4])
        sums.append(out[5:])
        got_x.append(lax.ppermute(out[4], "sp", swap))
        return out[8]

    def unpack(c, after):
        full = shape_of(Q, 2 * xw, dtype=BF16)
        finals[:2] = call(
            unpack_kernel, yv, (1,),
            [(got_x[c], whole((2, Q, cw)))],
            [(full, cols(cw, True, chunks, c)), (full, cols(cw, True, chunks, c))],
            [], 1, 1 << 20, keep=finals[:2], after=after,
        )

    grads_bc = []

    def finish(g, last, after):
        nonlocal grads_bc
        full = shape_of(Q, 2 * bw, dtype=BF16)
        strip = shape_of(8, base + xw)

        def wg(at):
            return pl.BlockSpec((4, N), lambda j, yr: (0, (2 * xw + at) // N + yr[0] * groups + g))

        def rec_at(at):
            return pl.BlockSpec((Q, N), lambda j, yr: (0, at // N + g))

        def halo_at(at):
            return pl.BlockSpec((8, N), lambda j, yr: (0, (xw + at) // N + g))

        tok_own = cols(N, False, groups, g)
        ins = [
            (b_rows, tok_own), (c_rows, tok_own), (rec_bc, rec_at(0)), (rec_bc, rec_at(bw)),
            (halo, halo_at(0)), (halo, halo_at(bw)), (conv_weight, wg(0)), (conv_weight, wg(2 * bw)),
            (slopes, pl.BlockSpec((2, two, N), lambda j, yr: (0, 0, g))),
            (bcc, pl.BlockSpec((two, N), lambda j, yr: (0, g))),
            (ccc, pl.BlockSpec((two, N), lambda j, yr: (0, g))),
        ]
        for c in range(g * per_group, (g + 1) * per_group):
            ins += [
                (sums[c][0], whole((two, N))), (sums[c][1], whole((two, N))),
                (dcbs[c], whole((2, Q, Q))),
            ]
        place = pl.BlockSpec((8, piece), lambda j, yr: (0, g))
        send_w = piece if last else 2 * N
        outs = [
            (strip, place), (strip, place), (full, tok_own), (full, tok_own),
            (shape_of(Q, send_w, dtype=BF16), whole((Q, send_w))),
        ]
        scratch = [
            pltpu.VMEM((two + 8, N), F32), pltpu.VMEM((two + 8, N), F32), pltpu.VMEM((2, two, N), F32),
        ]
        if last:
            ins += [(st, whole(st.shape)), (par, whole(par.shape)), (seg, whole(seg.shape))]
            ins += [(s[2], whole(s[2].shape)) for s in sums]
            ins += [(s[3], whole(s[3].shape)) for s in sums]
            outs.append((shape_of(Q, 2 * hl, dtype=BF16), whole((Q, 2 * hl))))
            scratch.append(pltpu.VMEM((two, 2 * hl), BF16))
        kernel = finish_last_kernel if last else finish_kernel
        count = len(ins)

        def reordered(yr, *refs):
            red, head, gb, gc = refs[count : count + 4]
            kernel(yr, *refs[:count], gb, gc, red, head, *refs[count + 4 :])

        out = call(
            reordered, yv, (1,), ins, outs, scratch, 3, 4 << 20,
            keep=finals[2:4] + grads_bc, after=after,
        )
        finals[2:4] = out[:2]
        grads_bc = list(out[2:4])
        return lax.ppermute(out[4], "sp", swap), (out[5] if last else out[4])

    evens = pairs(lambda i: i ^ 2)
    odds = pairs(lambda i: ((i + 2) ^ 2) - 2 if 2 <= i < devices - 2 else None)
    zero = jnp.zeros((N, cw), BF16)
    in_e, in_o = zero, zero
    ins_e, ins_o = [], []
    steps = chunks + spots - 2
    state(0, [])
    send_chunk(2, [rec[0]])
    got_bc = []
    waits = []
    for t in range(steps + 1):
        if t:
            ins_e.append(in_e)
            ins_o.append(in_o)
        token = []
        if t < steps:

            def slot(back):
                def at(j, yr):
                    c = t - (spots - 1 - yr[1] if back else yr[1])
                    return (jnp.clip(c, 0, chunks - 1), 0, j)

                return pl.BlockSpec((1, N, SUB), at)

            def slot_row(back):
                def at(j, yr):
                    c = t - (spots - 1 - yr[1] if back else yr[1])
                    return (0, jnp.clip(c, 0, chunks - 1) * subs + j)

                return pl.BlockSpec((8, SUB), at)

            moving = shape_of(N, cw, dtype=BF16)
            out_e, out_o = call(
                hop_kernel, yv, (subs,),
                [
                    (in_e, wave), (in_o, wave), (states[0], slot(False)), (states[1], slot(True)),
                    (rows, slot_row(False)), (rows, slot_row(True)),
                ],
                [(moving, wave), (moving, wave)],
                [], 1, 3 << 20, after=waits,
            )
            token = [out_e]
            in_e = lax.ppermute(out_e, "sp", evens)
            in_o = lax.ppermute(out_o, "sp", odds)
        waits = []
        if t + 1 < chunks:
            waits.append(state(t + 1, token))
            if t + 3 < chunks:
                send_chunk(t + 3, [rec[t + 1]])
        if t < chunks:
            waits.append(within(t, token))
        c = t + 1 - spots
        if 0 <= c < chunks:
            ents = [(ins_o if k % 2 == 0 else ins_e)[c + k - 1] for k in range(1, spots)]
            leas = [(ins_o if (spots - 1 - k) % 2 else ins_e)[c + k - 1] for k in range(1, spots)]
            waits.append(across(c, ents, leas, token))
            if c == chunks - 2:
                unpack(0, token)
                got, tok = finish(0, False, token)
                got_bc.append(got)
                waits += [tok, finals[0]]
            if c == chunks - 1:
                unpack(1, [])
                unpack(2, [])
    got, gdt_own = finish(1, True, [finals[0]])
    got_bc.append(got)
    unpack(3, [gdt_own])
    y_all, gx_all, red, heads_ = finals

    hw = (base + xw) // 2
    slab = shape_of(8, hw)

    def side(other):
        if other:
            return pl.BlockSpec((8, hw), lambda j, yr: (0, 1 - yr[3]))
        return pl.BlockSpec((8, hw), lambda j, yr: (0, yr[3]))

    def add(items, after=()):
        (out,) = call(
            add_kernel, yv, (1,), items, [(slab, whole((8, hw)))], [], 1, 1 << 20, after=after
        )
        return out

    theirs = add([(red, side(True))])
    mine = add([(red, side(False)), (lax.ppermute(theirs, "dp", pairs(lambda i: i ^ 1, dp_size)), whole((8, hw)))])
    size = 2
    while size < dp_size:
        mine = mine + lax.ppermute(mine, "dp", pairs(lambda i: i ^ size, dp_size))
        size *= 2
    size = 2
    while size < devices:
        ways = 4 if size * 4 <= devices else 2
        got = [lax.ppermute(mine, "sp", pairs(lambda i: i ^ (size * k))) for k in range(1, ways)]
        size *= ways
        mine = add([(v, whole((8, hw))) for v in [mine] + got], [y_all] if size >= devices else [])
    mine = jnp.stack([mine, lax.ppermute(mine, "sp", swap)])
    theirs = lax.ppermute(mine, "dp", pairs(lambda i: i ^ 1, dp_size))

    next0 = lax.ppermute(heads_, "sp", pairs(lambda i: i - 1 if i % 2 == 0 else None))
    next1 = lax.ppermute(heads_, "sp", pairs(lambda i: i - 2 if i % 2 else None))
    full = shape_of(Q, 2 * bw, dtype=BF16)
    gb, gc, gdt = call(
        close_kernel, yv, (1,),
        [
            (got_bc[0], whole(got_bc[0].shape)), (got_bc[1], whole(got_bc[1].shape)),
            (gdt_own, whole(gdt_own.shape)),
        ],
        [
            (full, cols(bw, True)), (full, cols(bw, True)),
            (shape_of(Q, 2 * hl, dtype=BF16), whole((Q, 2 * hl))),
        ],
        [], 1, 1 << 20, keep=grads_bc,
    )
    last = [pl.BlockSpec((16, v.shape[1]), lambda j, yr: (Q // 16 - 1, 0)) for v in (gx_all, gb, gc)]
    kept = [gx_all, gb, gc]
    grad_x, grad_b, grad_c = pl.pallas_call(
        rim_kernel,
        out_shape=[shape_of(*v.shape, dtype=BF16) for v in kept],
        grid_spec=pltpu.PrefetchScalarGridSpec(
            num_scalar_prefetch=1,
            grid=(1,),
            in_specs=[whole(next0.shape), whole(next1.shape), whole(conv_weight.shape)] + last,
            out_specs=last,
        ),
        compiler_params=params(),
        cost_estimate=cost(1, 1 << 20),
        input_output_aliases={4: 0, 5: 1, 6: 2},
    )(yv, next0, next1, conv_weight, *kept)

    def summed(*refs):
        sums_kernel(*refs, wide=xw)

    gw, gbias, gheads = call(
        summed, yv, (1,),
        [(mine, whole(mine.shape)), (theirs, whole(theirs.shape))],
        [
            (shape_of(4, bias.shape[1]), whole((4, bias.shape[1]))),
            (shape_of(1, bias.shape[1]), whole((1, bias.shape[1]))),
            (shape_of(8, 2 * hl), whole((8, 2 * hl))),
        ],
        [pltpu.VMEM((2, 8, base + xw), F32)], 1, 1 << 20, after=[grad_x, gdt],
    )

    per_dev = 2 * hl // devices
    head_total = lax.dynamic_slice(gheads, (0, me * per_dev), (3, per_dev))
    return (
        y_all[None], grad_x[None], grad_b[None], grad_c[None], gdt[None], gw, gbias[0], head_total,
    )


def solution(mesh):
    rows = P("dp", "sp", None)
    in_specs = (rows, rows, rows, rows, P(), P(), P(), P(), P(), rows)
    out_specs = (rows, rows, rows, rows, rows, P(), P(), P(None, "sp"))
    return jax.shard_map(
        per_device, mesh=mesh, in_specs=in_specs, out_specs=out_specs, check_vma=False
    )
```

time: 238 us -> 196 us (0.82)
  Pallas kernels: 63.7 us -> 98.6 us
  other arithmetic: 31.6 us -> 0.18 us
  local copies, waits for them, and re-layouts: 30 us -> 12.3 us
  waiting for transfers between devices: 43.2 us -> 26.6 us
  starting transfers between devices: 66.7 us -> 56.6 us
    pallas_call x14 -> x36, Pallas kernels: 63.7 us -> 98.6 us  [the longest x35 96.2 us: call(): pl.pallas_call(run, out_shape=[o[0] for o in outs], grid_spec=pltpu.Prefe...]
    ppermute x30 -> x32, waiting for transfers between devices: 43.2 us -> 19.4 us  [the longest x2 6.54 us: finish(): return (lax.ppermute(out[4], 'sp', swap), out[5] if last else out[4])]
    ppermute x30 -> x32, starting transfers between devices: 63.8 us -> 50.2 us  [the longest x6 21.7 us: per_device(): in_e = lax.ppermute(out_e, 'sp', evens)]
    convert_element_type x13 -> x0, other arithmetic: 12.5 us -> none  [the longest x2 4.71 us: per_device(): seg = (lanes[:, None] == jnp.arange(hl)[None, :]).astype(BF16)]
    ppermute x1, waiting for transfers between devices: 0.01 us -> 7.24 us  [per_device(): rec_bc = lax.ppermute(msg, 'sp', swap)]
    another operation x9 -> x2, other arithmetic: 5.65 us -> 0.1 us  [the longest x1 0.08 us: per_device(): yv = jnp.stack([y, z, lax.rem(z, 2), core]).astype(jnp.int32)]
    slice x19 -> x0, local copies, waits for them, and re-layouts: 5.52 us -> none  [the longest x2 1.57 us: rim_add(): next1[:, lo:lo + width]]
    dynamic_slice x6 -> x2, local copies, waits for them, and re-layouts: 5.15 us -> 0.72 us  [the longest x1 0.65 us: per_device(): head_total = lax.dynamic_slice(gheads, (0, me * per_dev), (3, per_dev))]
  transfers between devices with their start and end apart: 31 -> 33, of which waited for: 13 -> 11; matrix products, arithmetic and copies ran while one was open for 16% -> 0% of each run, Pallas kernels for 12% -> 48%
where the time goes in v2:
time: 196 us; the launch traced here: 195 us
  Pallas kernels  98.6 us (50%)
  starting transfers between devices  56.6 us (29%)
  waiting for transfers between devices  26.6 us (14%)
  local copies, waits for them, and re-layouts  12.3 us (6%)
    pallas_call x35, Pallas kernels, call(): pl.pallas_call(run, out_shape=[o[0] for o in outs], grid_spec=pltpu.Prefe...  96.2 us
    ppermute x6, starting transfers between devices, per_device(): in_e = lax.ppermute(out_e, 'sp', evens)  21.7 us
    unnamed x44, local copies, waits for them, and re-layouts  10.7 us
    ppermute x1, waiting for transfers between devices, per_device(): rec_bc = lax.ppermute(msg, 'sp', swap)  7.24 us
    ppermute x2, waiting for transfers between devices, finish(): return (lax.ppermute(out[4], 'sp', swap), out[5] if last else out[4])  6.54 us
    ppermute x1, starting transfers between devices, per_device(): rec_bc = lax.ppermute(msg, 'sp', swap)  6.42 us
    ppermute x4, starting transfers between devices, send_chunk(): rec.append(lax.ppermute(out, 'sp', swap))  6.38 us
    ppermute x3, starting transfers between devices, per_device(): lax.ppermute(mine, 'sp', pairs(lambda i: i ^ size * k))  4.45 us
  transfers between devices with their start and end apart: 33, of which 11 were waited for; matrix products, arithmetic and copies ran while one was open for 0% of the time, Pallas kernels for 48%

profile of v2, /device:TPU:0, one launch (start us, length us, event | category | flops | bytes accessed | tf_op | source)
XLA Modules:
  0.0 195.4 jit_solution(10601871945007041485)
XLA Ops:
  9.0 6.4 %collective-permute-start = (bf16[128,1152]{1,0:T(8,128)(2,1)}, bf16[128,1152]{1,0:T(8,128)(2,1)}, u32[]{:S(2)}, u32[]{:S(2)}) collective-permute-start(bf16[128,1152]{1,0:T(8,128)(2,1)} %get-tuple-element.128.refs_2_), channel_id=1, source_target_pairs={{0,1},{1,0},{2,3},{3,2},{4,5},{5,4},{6,7},{7,6},{8,9},{9,8},{10,11... | collective-permute-start | bytes 884744 | tf_op jit(solution)/shard_map/ppermute | solution.py:629
  16.4 7.2 %collective-permute-done.refs_2_.refs_3_ = bf16[128,1152]{1,0:T(8,128)(2,1)} collective-permute-done((bf16[128,1152]{1,0:T(8,128)(2,1)}, bf16[128,1152]{1,0:T(8,128)(2,1)}, u32[]{:S(2)}, u32[]{:S(2)}) %collective-permute-start) | collective-permute-done | bytes 294944 | tf_op jit(solution)/shard_map/ppermute | solution.py:629
  25.9 2.1 %collective-permute-start.1 = (bf16[2,128,1024]{2,1,0:T(8,128)(2,1)S(1)}, bf16[2,128,1024]{2,1,0:T(8,128)(2,1)S(1)}, u32[]{:S(2)}, u32[]{:S(2)}) collective-permute-start(bf16[2,128,1024]{2,1,0:T(8,128)(2,1)S(1)} %shard_map.180), channel_id=1, source_target_pairs={{0,1},{1,0},{2,3},{3,2},{4,5},{5,4},{6,7},{7,6},{8,9},{9,8},{10,11... | collective-permute-start | bytes 1572872 | tf_op jit(solution)/shard_map/ppermute | solution.py:642
  28.1 4.6 %shard_map.182 = (f32[8,5120]{1,0:T(8,128)S(1)}, bf16[256,512]{1,0:T(8,128)(2,1)S(1)}, bf16[256,512]{1,0:T(8,128)(2,1)S(1)}, bf16[512,256]{1,0:T(8,128)(2,1)S(1)...) custom-call(s32[4]{0:T(128)S(1)} %pad_add_fusion.yr.yv, ...), custom_call_target="tpu_custom_call" | custom-call | flops 4000000000 | bytes 4194304 | tf_op jit(solution)/shard_map/pallas_call | solution.py:561
  35.4 2.1 %collective-permute-start.6 = (bf16[2,128,1024]{2,1,0:T(8,128)(2,1)S(1)}, bf16[2,128,1024]{2,1,0:T(8,128)(2,1)S(1)}, u32[]{:S(2)}, u32[]{:S(2)}) collective-permute-start(bf16[2,128,1024]{2,1,0:T(8,128)(2,1)S(1)} %shard_map.184), channel_id=1, source_target_pairs={{0,1},{1,0},{2,3},{3,2},{4,5},{5,4},{6,7},{7,6},{8,9},{9,8},{10,11... | collective-permute-start | bytes 1572872 | tf_op jit(solution)/shard_map/ppermute | solution.py:642
  37.5 4.1 %shard_map.185 = (bf16[4,256,1024]{2,1,0:T(8,128)(2,1)S(1)}, bf16[4,256,1024]{2,1,0:T(8,128)(2,1)S(1)}, bf16[256,1024]{1,0:T(8,128)(2,1)S(1)}, bf16[256,1024]{1,0:T(8,128)(2,1)S(1)}, bf16[256,1024]{1,0:T(8,128)(2,1)S(1)}) custom-call(s32[4]{0:T(128)S(1)} %pad_add_fusion.yr.yv, bf16[128,8192]{1,0:T(8,128)(2,1)S(1)} %bitcast.37, ...), custom_call_target="tpu_custom_call" | custom-call | flops 3000000000 | bytes 4194304 | tf_op jit(solution)/shard_map/pallas_call | solution.py:561
  43.9 5.5 %collective-permute-start.7 = (bf16[256,1024]{1,0:T(8,128)(2,1)S(1)}, bf16[256,1024]{1,0:T(8,128)(2,1)S(1)}, u32[]{:S(2)}, u32[]{:S(2)}) collective-permute-start(bf16[256,1024]{1,0:T(8,128)(2,1)S(1)} %get-tuple-element.137.refs_13_.refs_6_), channel_id=1, source_target_pairs={{0,2},{1,3},{2,0},{3,1},{4,6},{5,7},{6,4},{7,5},{8,10},{9,11},{10,... | collective-permute-start | bytes 1572872 | tf_op jit(solution)/shard_map/ppermute | solution.py:905
  49.4 3.5 %shard_map.188 = (f32[256,1024]{1,0:T(8,128)S(1)}, f32[256,1024]{1,0:T(8,128)S(1)}, f32[2,128,128]{2,1,0:T(8,128)S(1)}) custom-call(s32[4]{0:T(128)S(1)} %pad_add_fusion.yr.yv, bf16[256,1024]{1,0:T(8,128)(2,1)S(1)} %get-tuple-element.142.refs_0_.refs_4_, bf16[256,1024]{1,0:T(8,128)(2,1)S(1)} %get-tuple-element.143.refs_1_.refs_5_, ...), custom_call_target="tpu_custom_call" | custom-call | flops 3000000000 | bytes 4194304 | tf_op jit(solution)/shard_map/pallas_call | solution.py:561
  55.5 4.2 %shard_map.187 = (bf16[4,256,1024]{2,1,0:T(8,128)(2,1)S(1)}, bf16[4,256,1024]{2,1,0:T(8,128)(2,1)S(1)}, bf16[256,1024]{1,0:T(8,128)(2,1)S(1)}, bf16[256,1024]{1,0:T(8,128)(2,1)S(1)}, bf16[256,1024]{1,0:T(8,128)(2,1)S(1)}) custom-call(s32[4]{0:T(128)S(1)} %pad_add_fusion.yr.yv, ...), custom_call_target="tpu_custom_call", output_to_operand_aliasing={{0}: (12, {}), {1}: (13, {})} | custom-call | flops 3000000000 | bytes 4194304 | tf_op jit(solution)/shard_map/pallas_call | solution.py:561
  62.2 3.5 %collective-permute-start.9 = (bf16[256,1024]{1,0:T(8,128)(2,1)S(1)}, bf16[256,1024]{1,0:T(8,128)(2,1)S(1)}, u32[]{:S(2)}, u32[]{:S(2)}) collective-permute-start(bf16[256,1024]{1,0:T(8,128)(2,1)S(1)} %get-tuple-element.149.refs_13_.refs_6_), channel_id=1, source_target_pairs={{0,2},{1,3},{2,0},{3,1},{4,6},{5,7},{6,4},{7,5},{8,10},{9,11},{10,... | collective-permute-start | bytes 1572872 | tf_op jit(solution)/shard_map/ppermute | solution.py:905
  65.6 3.4 %shard_map.191 = (f32[256,1024]{1,0:T(8,128)S(1)}, f32[256,1024]{1,0:T(8,128)S(1)}, f32[2,128,128]{2,1,0:T(8,128)S(1)}) custom-call(s32[4]{0:T(128)S(1)} %pad_add_fusion.yr.yv, bf16[256,1024]{1,0:T(8,128)(2,1)S(1)} %get-tuple-element.141.refs_6_.refs_0_.refs_4_, bf16[256,1024]{1,0:T(8,128)(2,1)S(1)} %get-tuple-element.154.refs_1_.refs_5_, ...), custom_call_target="tpu_custom_call" | custom-call | flops 3000000000 | bytes 4194304 | tf_op jit(solution)/shard_map/pallas_call | solution.py:561
  69.1 4.2 %shard_map.190 = (bf16[4,256,1024]{2,1,0:T(8,128)(2,1)S(1)}, bf16[4,256,1024]{2,1,0:T(8,128)(2,1)S(1)}, bf16[256,1024]{1,0:T(8,128)(2,1)S(1)}, bf16[256,1024]{1,0:T(8,128)(2,1)S(1)}, bf16[256,1024]{1,0:T(8,128)(2,1)S(1)}) custom-call(s32[4]{0:T(128)S(1)} %pad_add_fusion.yr.yv, ...), custom_call_target="tpu_custom_call", output_to_operand_aliasing={{0}: (12, {}), {1}: (13, {})} | custom-call | flops 3000000000 | bytes 4194304 | tf_op jit(solution)/shard_map/pallas_call | solution.py:561
  77.2 4.6 %collective-permute-start.11 = (bf16[256,1024]{1,0:T(8,128)(2,1)S(1)}, bf16[256,1024]{1,0:T(8,128)(2,1)S(1)}, u32[]{:S(2)}, u32[]{:S(2)}) collective-permute-start(bf16[256,1024]{1,0:T(8,128)(2,1)S(1)} %get-tuple-element.156.refs_13_.refs_6_), channel_id=1, source_target_pairs={{0,2},{1,3},{2,0},{3,1},{4,6},{5,7},{6,4},{7,5},{8,10},{9,11},{10,... | collective-permute-start | bytes 1572872 | tf_op jit(solution)/shard_map/ppermute | solution.py:905
  81.8 3.5 %shard_map.194 = (f32[256,1024]{1,0:T(8,128)S(1)}, f32[256,1024]{1,0:T(8,128)S(1)}, f32[2,128,128]{2,1,0:T(8,128)S(1)}) custom-call(s32[4]{0:T(128)S(1)} %pad_add_fusion.yr.yv, bf16[256,1024]{1,0:T(8,128)(2,1)S(1)} %get-tuple-element.153.refs_6_.refs_0_.refs_4_, bf16[256,1024]{1,0:T(8,128)(2,1)S(1)} %get-tuple-element.163.refs_1_.refs_5_, ...), custom_call_target="tpu_custom_call" | custom-call | flops 3000000000 | bytes 4194304 | tf_op jit(solution)/shard_map/pallas_call | solution.py:561
  85.3 4.2 %shard_map.193 = (bf16[4,256,1024]{2,1,0:T(8,128)(2,1)S(1)}, bf16[4,256,1024]{2,1,0:T(8,128)(2,1)S(1)}, bf16[256,1024]{1,0:T(8,128)(2,1)S(1)}, bf16[256,1024]{1,0:T(8,128)(2,1)S(1)}, bf16[256,1024]{1,0:T(8,128)(2,1)S(1)}) custom-call(s32[4]{0:T(128)S(1)} %pad_add_fusion.yr.yv, ...), custom_call_target="tpu_custom_call", output_to_operand_aliasing={{0}: (12, {}), {1}: (13, {})} | custom-call | flops 3000000000 | bytes 4194304 | tf_op jit(solution)/shard_map/pallas_call | solution.py:561
  92.3 3.5 %collective-permute-start.13 = (bf16[256,1024]{1,0:T(8,128)(2,1)S(1)}, bf16[256,1024]{1,0:T(8,128)(2,1)S(1)}, u32[]{:S(2)}, u32[]{:S(2)}) collective-permute-start(bf16[256,1024]{1,0:T(8,128)(2,1)S(1)} %get-tuple-element.165.refs_6_.refs_23_), channel_id=1, source_target_pairs={{0,2},{1,3},{2,0},{3,1},{4,6},{5,7},{6,4},{7,5},{8,10},{9,11},{10,... | collective-permute-start | bytes 1572872 | tf_op jit(solution)/shard_map/ppermute | solution.py:905
  95.8 7.7 %shard_map.197 = (bf16[128,8192]{1,0:T(8,128)(2,1)}, bf16[128,8192]{1,0:T(8,128)(2,1)}, f32[8,5376]{1,0:T(8,128)S(1)}, f32[8,5376]{1,0:T(8,128)S(1)}, bf16[2,128...) custom-call(s32[4]{0:T(128)S(1)} %pad_add_fusion.yr.yv, ...), custom_call_target="tpu_custom_call" | custom-call | flops 6000000000 | bytes 6291456 | tf_op jit(solution)/shard_map/pallas_call | solution.py:561
  104.8 3.5 %shard_map.196 = (f32[256,1024]{1,0:T(8,128)S(1)}, f32[256,1024]{1,0:T(8,128)S(1)}, f32[2,128,128]{2,1,0:T(8,128)S(1)}) custom-call(s32[4]{0:T(128)S(1)} %pad_add_fusion.yr.yv, bf16[256,1024]{1,0:T(8,128)(2,1)S(1)} %get-tuple-element.157.refs_6_.refs_0_.refs_4_, bf16[256,1024]{1,0:T(8,128)(2,1)S(1)} %get-tuple-element.158.refs_1_.refs_5_, ...), custom_call_target="tpu_custom_call" | custom-call | flops 3000000000 | bytes 4194304 | tf_op jit(solution)/shard_map/pallas_call | solution.py:561
  110.6 2.9 %collective-permute-start.16 = (bf16[256,1024]{1,0:T(8,128)(2,1)S(1)}, bf16[256,1024]{1,0:T(8,128)(2,1)S(1)}, u32[]{:S(2)}, u32[]{:S(2)}) collective-permute-start(bf16[256,1024]{1,0:T(8,128)(2,1)S(1)} %get-tuple-element.175.refs_27_), channel_id=1, source_target_pairs={{0,2},{1,3},{2,0},{3,1},{4,6},{5,7},{6,4},{7,5},{8,10},{9,11},{10,... | collective-permute-start | bytes 1572872 | tf_op jit(solution)/shard_map/ppermute | solution.py:905
  113.4 7.7 %shard_map.199 = (bf16[128,8192]{1,0:T(8,128)(2,1)}, bf16[128,8192]{1,0:T(8,128)(2,1)}, f32[8,5376]{1,0:T(8,128)S(1)}, f32[8,5376]{1,0:T(8,128)S(1)}, bf16[2,128...) custom-call(s32[4]{0:T(128)S(1)} %pad_add_fusion.yr.yv, ...), custom_call_target="tpu_custom_call", output_to_operand_aliasing={{0}: (24, {}), {1}: (25, {}), {2}: (26, {}), {3}: (27, {})} | custom-call | flops 6000000000 | bytes 6291456 | tf_op jit(solution)/shard_map/pallas_call | solution.py:561
  122.1 2.5 %shard_map.200 = (bf16[256,1024]{1,0:T(8,128)(2,1)S(1)}, bf16[256,1024]{1,0:T(8,128)(2,1)}) custom-call(s32[4]{0:T(128)S(1)} %pad_add_fusion.yr.yv, bf16[256,1024]{1,0:T(8,128)(2,1)S(1)} %collective-permute-done.16.refs_0_.refs_19_.refs_22_, bf16[256,1024]{1,0:T(8,128)(2,1)S(1)} %collective-permute-done.15.refs_1_.refs_18_.refs_21_, ...), custom_call_target="tpu_custom_call" | custom-call | flops 1000000000 | bytes 3145728 | tf_op jit(solution)/shard_map/pallas_call | solution.py:561
  126.4 7.7 %shard_map.201 = (bf16[128,8192]{1,0:T(8,128)(2,1)}, bf16[128,8192]{1,0:T(8,128)(2,1)}, f32[8,5376]{1,0:T(8,128)S(1)}, f32[8,5376]{1,0:T(8,128)S(1)}, bf16[2,128...) custom-call(s32[4]{0:T(128)S(1)} %pad_add_fusion.yr.yv, ...), custom_call_target="tpu_custom_call", output_to_operand_aliasing={{0}: (24, {}), {1}: (25, {}), {2}: (26, {}), {3}: (27, {})} | custom-call | flops 6000000000 | bytes 6291456 | tf_op jit(solution)/shard_map/pallas_call | solution.py:561
  136.4 3.1 %shard_map.203 = (f32[8,5376]{1,0:T(8,128)S(1)}, f32[8,5376]{1,0:T(8,128)S(1)}, bf16[128,1024]{1,0:T(8,128)(2,1)}, bf16[128,1024]{1,0:T(8,128)(2,1)}, bf16[128,512]{1,0:T(8,128)(2,1)S(1)}) custom-call(s32[4]{0:T(128)S(1)} %pad_add_fusion.yr.yv, bf16[128,1024]{1,0:T(8,128)(2,1)S(1)} %bitcast.58, ...), custom_call_target="tpu_custom_call", output_to_operand_aliasing={{0}: (18, {}), {1}: (19, {})} | custom-call | flops 3000000000 | bytes 4194304 | tf_op jit(solution)/shard_map/pallas_call | solution.py:561
  139.4 7.7 %shard_map.204 = (bf16[128,8192]{1,0:T(8,128)(2,1)}, bf16[128,8192]{1,0:T(8,128)(2,1)}, f32[8,5376]{1,0:T(8,128)S(1)}, f32[8,5376]{1,0:T(8,128)S(1)}, bf16[2,128...) custom-call(s32[4]{0:T(128)S(1)} %pad_add_fusion.yr.yv, ...), custom_call_target="tpu_custom_call", output_to_operand_aliasing={{0}: (24, {}), {1}: (25, {}), {2}: (26, {}), {3}: (27, {})} | custom-call | flops 6000000000 | bytes 6291456 | tf_op jit(solution)/shard_map/pallas_call | solution.py:561
  152.9 3.7 %shard_map.207 = (f32[8,5376]{1,0:T(8,128)S(1)}, f32[8,5376]{1,0:T(8,128)S(1)}, bf16[128,1024]{1,0:T(8,128)(2,1)}, bf16[128,1024]{1,0:T(8,128)(2,1)}, bf16[128,6...) custom-call(s32[4]{0:T(128)S(1)} %pad_add_fusion.yr.yv, ...), custom_call_target="tpu_custom_call", output_to_operand_aliasing={{0}: (29, {}), {1}: (30, {}), {2}: (31, {}), {3}: (32, {})} | custom-call | flops 3000000000 | bytes 4194304 | tf_op jit(solution)/shard_map/pallas_call | solution.py:561
  160.5 3.1 %collective-permute-done.27 = f32[8,2688]{1,0:T(8,128)S(1)} collective-permute-done((f32[8,2688]{1,0:T(8,128)S(1)}, f32[8,2688]{1,0:T(8,128)S(1)}, u32[]{:S(2)}, u32[]{:S(2)}) %collective-permute-start.27) | collective-permute-done | bytes 86048 | tf_op jit(solution)/shard_map/ppermute | solution.py:950
  165.5 2.7 %collective-permute-start.28 = (f32[8,2688]{1,0:T(8,128)S(1)}, f32[8,2688]{1,0:T(8,128)S(1)}, u32[]{:S(2)}, u32[]{:S(2)}) collective-permute-start(f32[8,2688]{1,0:T(8,128)S(1)} %add.11.refs_0_), channel_id=1, source_target_pairs={{0,2},{1,3},{2,0},{3,1},{4,6},{5,7},{6,4},{7,5},{8,10},{9,11},{10,... | collective-permute-start | bytes 258056 | tf_op jit(solution)/shard_map/ppermute | solution.py:955
  171.0 2.4 %collective-permute-done.29.refs_2_ = f32[8,2688]{1,0:T(8,128)S(1)} collective-permute-done((f32[8,2688]{1,0:T(8,128)S(1)}, f32[8,2688]{1,0:T(8,128)S(1)}, u32[]{:S(2)}, u32[]{:S(2)}) %collective-permute-start.29) | collective-permute-done | bytes 86048 | tf_op jit(solution)/shard_map/ppermute | solution.py:955
  179.1 2.5 %collective-permute-start.25 = (bf16[128,640]{1,0:T(8,128)(2,1)S(1)}, bf16[128,640]{1,0:T(8,128)(2,1)S(1)}, u32[]{:S(2)}, u32[]{:S(2)}) collective-permute-start(bf16[128,640]{1,0:T(8,128)(2,1)S(1)} %get-tuple-element.235), channel_id=1, source_target_pairs={{0,1},{1,0},{2,3},{3,2},{4,5},{5,4},{6,7},{7,6},{8,9},{9,8},{10,11... | collective-permute-start | bytes 491528 | tf_op jit(solution)/shard_map/ppermute | solution.py:861
  181.6 2.3 %collective-permute-done.24.refs_0_ = bf16[128,512]{1,0:T(8,128)(2,1)S(1)} collective-permute-done((bf16[128,512]{1,0:T(8,128)(2,1)S(1)}, bf16[128,512]{1,0:T(8,128)(2,1)S(1)}, u32[]{:S(2)}, u32[]{:S(2)}) %collective-permute-start.24) | collective-permute-done | bytes 131104 | tf_op jit(solution)/shard_map/ppermute | solution.py:861
  183.9 4.2 %collective-permute-done.25.refs_1_ = bf16[128,640]{1,0:T(8,128)(2,1)S(1)} collective-permute-done((bf16[128,640]{1,0:T(8,128)(2,1)S(1)}, bf16[128,640]{1,0:T(8,128)(2,1)S(1)}, u32[]{:S(2)}, u32[]{:S(2)}) %collective-permute-start.25) | collective-permute-done | bytes 163872 | tf_op jit(solution)/shard_map/ppermute | solution.py:861
  189.5 2.4 %shard_map.210 = (bf16[128,8192]{1,0:T(8,128)(2,1)}, bf16[128,1024]{1,0:T(8,128)(2,1)}, bf16[128,1024]{1,0:T(8,128)(2,1)}) custom-call(s32[4]{0:T(128)S(1)} %pad_add_fusion.yr.yv, f32[8,5376]{1,0:T(8,128)S(1)} %collective-permute-done.22.next0, ...), custom_call_target="tpu_custom_call", output_to_operand_aliasing={{0}: (4, {}), {1}: (5, {}), {2}: (6, {})} | custom-call | flops 1000000000 | bytes 1048576 | tf_op jit(solution)/shard_map/pallas_call | solution.py:978
  (124 shorter events, 61.6 us)
Async XLA Ops:
  7.0 21.0 %collective-permute-start.4 = (bf16[16,5120]{1,0:T(8,128)(2,1)}, bf16[16,5120]{1,0:T(8,128)(2,1)S(1)}, u32[]{:S(2)}, u32[]{:S(2)}) collective-permute-start(bf16[16,5120]{1,0:T(8,128)(2,1)} %get-tuple-element.248), channel_id=1, source_target_pairs={{1,3},{3,5},{5,7},{9,11},{11,13},{13,15},{17,19},{19,21},{21,23},{... | collective-permute-start | bytes 491528 | tf_op jit(solution)/shard_map/ppermute | solution.py:631
  7.7 20.3 %collective-permute-start.3 = (bf16[16,5120]{1,0:T(8,128)(2,1)}, bf16[16,5120]{1,0:T(8,128)(2,1)}, u32[]{:S(2)}, u32[]{:S(2)}) collective-permute-start(bf16[16,5120]{1,0:T(8,128)(2,1)} %get-tuple-element.249), channel_id=1, source_target_pairs={{1,2},{3,4},{5,6},{9,10},{11,12},{13,14},{17,18},{19,20},{21,22},{... | collective-permute-start | bytes 491528 | tf_op jit(solution)/shard_map/ppermute | solution.py:630
  9.0 14.6 %collective-permute-start = (bf16[128,1152]{1,0:T(8,128)(2,1)}, bf16[128,1152]{1,0:T(8,128)(2,1)}, u32[]{:S(2)}, u32[]{:S(2)}) collective-permute-start(bf16[128,1152]{1,0:T(8,128)(2,1)} %get-tuple-element.128.refs_2_), channel_id=1, source_target_pairs={{0,1},{1,0},{2,3},{3,2},{4,5},{5,4},{6,7},{7,6},{8,9},{9,8},{10,11... | collective-permute-start | bytes 884744 | tf_op jit(solution)/shard_map/ppermute | solution.py:629
  16.1 18.7 %collective-permute-start.5 = (bf16[2,128,1024]{2,1,0:T(8,128)(2,1)S(1)}, bf16[2,128,1024]{2,1,0:T(8,128)(2,1)S(1)}, u32[]{:S(2)}, u32[]{:S(2)}) collective-permute-start(bf16[2,128,1024]{2,1,0:T(8,128)(2,1)S(1)} %shard_map.183), channel_id=1, source_target_pairs={{0,1},{1,0},{2,3},{3,2},{4,5},{5,4},{6,7},{7,6},{8,9},{9,8},{10,11... | collective-permute-start | bytes 1572872 | tf_op jit(solution)/shard_map/ppermute | solution.py:642
  25.9 27.0 %collective-permute-start.1 = (bf16[2,128,1024]{2,1,0:T(8,128)(2,1)S(1)}, bf16[2,128,1024]{2,1,0:T(8,128)(2,1)S(1)}, u32[]{:S(2)}, u32[]{:S(2)}) collective-permute-start(bf16[2,128,1024]{2,1,0:T(8,128)(2,1)S(1)} %shard_map.180), channel_id=1, source_target_pairs={{0,1},{1,0},{2,3},{3,2},{4,5},{5,4},{6,7},{7,6},{8,9},{9,8},{10,11... | collective-permute-start | bytes 1572872 | tf_op jit(solution)/shard_map/ppermute | solution.py:642
  35.4 33.7 %collective-permute-start.6 = (bf16[2,128,1024]{2,1,0:T(8,128)(2,1)S(1)}, bf16[2,128,1024]{2,1,0:T(8,128)(2,1)S(1)}, u32[]{:S(2)}, u32[]{:S(2)}) collective-permute-start(bf16[2,128,1024]{2,1,0:T(8,128)(2,1)S(1)} %shard_map.184), channel_id=1, source_target_pairs={{0,1},{1,0},{2,3},{3,2},{4,5},{5,4},{6,7},{7,6},{8,9},{9,8},{10,11... | collective-permute-start | bytes 1572872 | tf_op jit(solution)/shard_map/ppermute | solution.py:642
  43.2 16.5 %collective-permute-start.8 = (bf16[256,1024]{1,0:T(8,128)(2,1)S(1)}, bf16[256,1024]{1,0:T(8,128)(2,1)S(1)}, u32[]{:S(2)}, u32[]{:S(2)}) collective-permute-start(bf16[256,1024]{1,0:T(8,128)(2,1)S(1)} %get-tuple-element.140), channel_id=1, source_target_pairs={{2,4},{3,5},{4,2},{5,3},{10,12},{11,13},{12,10},{13,11},{18,20},{1... | collective-permute-start | bytes 1572872 | tf_op jit(solution)/shard_map/ppermute | solution.py:906
  43.9 16.0 %collective-permute-start.7 = (bf16[256,1024]{1,0:T(8,128)(2,1)S(1)}, bf16[256,1024]{1,0:T(8,128)(2,1)S(1)}, u32[]{:S(2)}, u32[]{:S(2)}) collective-permute-start(bf16[256,1024]{1,0:T(8,128)(2,1)S(1)} %get-tuple-element.137.refs_13_.refs_6_), channel_id=1, source_target_pairs={{0,2},{1,3},{2,0},{3,1},{4,6},{5,7},{6,4},{7,5},{8,10},{9,11},{10,... | collective-permute-start | bytes 1572872 | tf_op jit(solution)/shard_map/ppermute | solution.py:905
  53.5 31.8 %collective-permute-start.2 = (bf16[2,128,1024]{2,1,0:T(8,128)(2,1)S(1)}, bf16[2,128,1024]{2,1,0:T(8,128)(2,1)S(1)}, u32[]{:S(2)}, u32[]{:S(2)}) collective-permute-start(bf16[2,128,1024]{2,1,0:T(8,128)(2,1)S(1)} %shard_map.181), channel_id=1, source_target_pairs={{0,1},{1,0},{2,3},{3,2},{4,5},{5,4},{6,7},{7,6},{8,9},{9,8},{10,11... | collective-permute-start | bytes 1572872 | tf_op jit(solution)/shard_map/ppermute | solution.py:642
  61.5 11.8 %collective-permute-start.10 = (bf16[256,1024]{1,0:T(8,128)(2,1)S(1)}, bf16[256,1024]{1,0:T(8,128)(2,1)S(1)}, u32[]{:S(2)}, u32[]{:S(2)}) collective-permute-start(bf16[256,1024]{1,0:T(8,128)(2,1)S(1)} %get-tuple-element.152), channel_id=1, source_target_pairs={{2,4},{3,5},{4,2},{5,3},{10,12},{11,13},{12,10},{13,11},{18,20},{1... | collective-permute-start | bytes 1572872 | tf_op jit(solution)/shard_map/ppermute | solution.py:906
  62.2 12.8 %collective-permute-start.9 = (bf16[256,1024]{1,0:T(8,128)(2,1)S(1)}, bf16[256,1024]{1,0:T(8,128)(2,1)S(1)}, u32[]{:S(2)}, u32[]{:S(2)}) collective-permute-start(bf16[256,1024]{1,0:T(8,128)(2,1)S(1)} %get-tuple-element.149.refs_13_.refs_6_), channel_id=1, source_target_pairs={{0,2},{1,3},{2,0},{3,1},{4,6},{5,7},{6,4},{7,5},{8,10},{9,11},{10,... | collective-permute-start | bytes 1572872 | tf_op jit(solution)/shard_map/ppermute | solution.py:905
  76.5 12.9 %collective-permute-start.12 = (bf16[256,1024]{1,0:T(8,128)(2,1)S(1)}, bf16[256,1024]{1,0:T(8,128)(2,1)S(1)}, u32[]{:S(2)}, u32[]{:S(2)}) collective-permute-start(bf16[256,1024]{1,0:T(8,128)(2,1)S(1)} %get-tuple-element.160), channel_id=1, source_target_pairs={{2,4},{3,5},{4,2},{5,3},{10,12},{11,13},{12,10},{13,11},{18,20},{1... | collective-permute-start | bytes 1572872 | tf_op jit(solution)/shard_map/ppermute | solution.py:906
  77.2 12.7 %collective-permute-start.11 = (bf16[256,1024]{1,0:T(8,128)(2,1)S(1)}, bf16[256,1024]{1,0:T(8,128)(2,1)S(1)}, u32[]{:S(2)}, u32[]{:S(2)}) collective-permute-start(bf16[256,1024]{1,0:T(8,128)(2,1)S(1)} %get-tuple-element.156.refs_13_.refs_6_), channel_id=1, source_target_pairs={{0,2},{1,3},{2,0},{3,1},{4,6},{5,7},{6,4},{7,5},{8,10},{9,11},{10,... | collective-permute-start | bytes 1572872 | tf_op jit(solution)/shard_map/ppermute | solution.py:905
  91.4 16.9 %collective-permute-start.14 = (bf16[256,1024]{1,0:T(8,128)(2,1)S(1)}, bf16[256,1024]{1,0:T(8,128)(2,1)S(1)}, u32[]{:S(2)}, u32[]{:S(2)}) collective-permute-start(bf16[256,1024]{1,0:T(8,128)(2,1)S(1)} %get-tuple-element.168), channel_id=1, source_target_pairs={{2,4},{3,5},{4,2},{5,3},{10,12},{11,13},{12,10},{13,11},{18,20},{1... | collective-permute-start | bytes 1572872 | tf_op jit(solution)/shard_map/ppermute | solution.py:906
  92.3 16.0 %collective-permute-start.13 = (bf16[256,1024]{1,0:T(8,128)(2,1)S(1)}, bf16[256,1024]{1,0:T(8,128)(2,1)S(1)}, u32[]{:S(2)}, u32[]{:S(2)}) collective-permute-start(bf16[256,1024]{1,0:T(8,128)(2,1)S(1)} %get-tuple-element.165.refs_6_.refs_23_), channel_id=1, source_target_pairs={{0,2},{1,3},{2,0},{3,1},{4,6},{5,7},{6,4},{7,5},{8,10},{9,11},{10,... | collective-permute-start | bytes 1572872 | tf_op jit(solution)/shard_map/ppermute | solution.py:905
  103.5 31.5 %collective-permute-start.18 = (bf16[2,128,1024]{2,1,0:T(8,128)(2,1)S(1)}, bf16[2,128,1024]{2,1,0:T(8,128)(2,1)S(1)}, u32[]{:S(2)}, u32[]{:S(2)}) collective-permute-start(bf16[2,128,1024]{2,1,0:T(8,128)(2,1)S(1)} %get-tuple-element.185), channel_id=1, source_target_pairs={{0,1},{1,0},{2,3},{3,2},{4,5},{5,4},{6,7},{7,6},{8,9},{9,8},{10,11... | collective-permute-start | bytes 1572872 | tf_op jit(solution)/shard_map/ppermute | solution.py:792
  109.9 12.2 %collective-permute-start.15 = (bf16[256,1024]{1,0:T(8,128)(2,1)S(1)}, bf16[256,1024]{1,0:T(8,128)(2,1)S(1)}, u32[]{:S(2)}, u32[]{:S(2)}) collective-permute-start(bf16[256,1024]{1,0:T(8,128)(2,1)S(1)} %get-tuple-element.174), channel_id=1, source_target_pairs={{2,4},{3,5},{4,2},{5,3},{10,12},{11,13},{12,10},{13,11},{18,20},{1... | collective-permute-start | bytes 1572872 | tf_op jit(solution)/shard_map/ppermute | solution.py:906
  110.6 11.6 %collective-permute-start.16 = (bf16[256,1024]{1,0:T(8,128)(2,1)S(1)}, bf16[256,1024]{1,0:T(8,128)(2,1)S(1)}, u32[]{:S(2)}, u32[]{:S(2)}) collective-permute-start(bf16[256,1024]{1,0:T(8,128)(2,1)S(1)} %get-tuple-element.175.refs_27_), channel_id=1, source_target_pairs={{0,2},{1,3},{2,0},{3,1},{4,6},{5,7},{6,4},{7,5},{8,10},{9,11},{10,... | collective-permute-start | bytes 1572872 | tf_op jit(solution)/shard_map/ppermute | solution.py:905
  121.2 27.4 %collective-permute-start.21 = (bf16[2,128,1024]{2,1,0:T(8,128)(2,1)S(1)}, bf16[2,128,1024]{2,1,0:T(8,128)(2,1)S(1)}, u32[]{:S(2)}, u32[]{:S(2)}) collective-permute-start(bf16[2,128,1024]{2,1,0:T(8,128)(2,1)S(1)} %get-tuple-element.208), channel_id=1, source_target_pairs={{0,1},{1,0},{2,3},{3,2},{4,5},{5,4},{6,7},{7,6},{8,9},{9,8},{10,11... | collective-permute-start | bytes 1572872 | tf_op jit(solution)/shard_map/ppermute | solution.py:792
  124.7 14.8 %collective-permute-start.17 = (bf16[256,1024]{1,0:T(8,128)(2,1)S(1)}, bf16[256,1024]{1,0:T(8,128)(2,1)S(1)}, u32[]{:S(2)}, u32[]{:S(2)}) collective-permute-start(bf16[256,1024]{1,0:T(8,128)(2,1)S(1)} %get-tuple-element.184.refs_27_.refs_3_.refs_19_), channel_id=1, source_target_pairs={{0,2},{1,3},{2,0},{3,1},{4,6},{5,7},{6,4},{7,5},{8,10},{9,11},{10,... | collective-permute-start | bytes 1572872 | tf_op jit(solution)/shard_map/ppermute | solution.py:905
  134.1 15.8 %collective-permute-start.20 = (bf16[2,128,1024]{2,1,0:T(8,128)(2,1)S(1)}, bf16[2,128,1024]{2,1,0:T(8,128)(2,1)S(1)}, u32[]{:S(2)}, u32[]{:S(2)}) collective-permute-start(bf16[2,128,1024]{2,1,0:T(8,128)(2,1)S(1)} %get-tuple-element.207), channel_id=1, source_target_pairs={{0,1},{1,0},{2,3},{3,2},{4,5},{5,4},{6,7},{7,6},{8,9},{9,8},{10,11... | collective-permute-start | bytes 1572872 | tf_op jit(solution)/shard_map/ppermute | solution.py:792
  147.2 21.0 %collective-permute-start.19 = (bf16[2,128,1024]{2,1,0:T(8,128)(2,1)S(1)}, bf16[2,128,1024]{2,1,0:T(8,128)(2,1)S(1)}, u32[]{:S(2)}, u32[]{:S(2)}) collective-permute-start(bf16[2,128,1024]{2,1,0:T(8,128)(2,1)S(1)} %get-tuple-element.206), channel_id=1, source_target_pairs={{0,1},{1,0},{2,3},{3,2},{4,5},{5,4},{6,7},{7,6},{8,9},{9,8},{10,11... | collective-permute-start | bytes 1572872 | tf_op jit(solution)/shard_map/ppermute | solution.py:792
  159.0 4.7 %collective-permute-start.27 = (f32[8,2688]{1,0:T(8,128)S(1)}, f32[8,2688]{1,0:T(8,128)S(1)}, u32[]{:S(2)}, u32[]{:S(2)}) collective-permute-start(f32[8,2688]{1,0:T(8,128)S(1)} %shard_map.212), channel_id=1, source_target_pairs={{0,16},{8,24},{16,0},{24,8},{1,17},{9,25},{17,1},{25,9},{2,18},{10... | collective-permute-start | bytes 258056 | tf_op jit(solution)/shard_map/ppermute | solution.py:950
  163.7 7.3 %collective-permute-start.30 = (f32[8,2688]{1,0:T(8,128)S(1)}, f32[8,2688]{1,0:T(8,128)S(1)}, u32[]{:S(2)}, u32[]{:S(2)}) collective-permute-start(f32[8,2688]{1,0:T(8,128)S(1)} %add.11.refs_0_), channel_id=1, source_target_pairs={{0,6},{1,7},{2,4},{3,5},{4,2},{5,3},{6,0},{7,1},{8,14},{9,15},{10,... | collective-permute-start | bytes 258056 | tf_op jit(solution)/shard_map/ppermute | solution.py:955
  165.1 8.3 %collective-permute-start.29 = (f32[8,2688]{1,0:T(8,128)S(1)}, f32[8,2688]{1,0:T(8,128)S(1)}, u32[]{:S(2)}, u32[]{:S(2)}) collective-permute-start(f32[8,2688]{1,0:T(8,128)S(1)} %add.11.refs_0_), channel_id=1, source_target_pairs={{0,4},{1,5},{2,6},{3,7},{4,0},{5,1},{6,2},{7,3},{8,12},{9,13},{10,... | collective-permute-start | bytes 258056 | tf_op jit(solution)/shard_map/ppermute | solution.py:955
  165.5 8.0 %collective-permute-start.28 = (f32[8,2688]{1,0:T(8,128)S(1)}, f32[8,2688]{1,0:T(8,128)S(1)}, u32[]{:S(2)}, u32[]{:S(2)}) collective-permute-start(f32[8,2688]{1,0:T(8,128)S(1)} %add.11.refs_0_), channel_id=1, source_target_pairs={{0,2},{1,3},{2,0},{3,1},{4,6},{5,7},{6,4},{7,5},{8,10},{9,11},{10,... | collective-permute-start | bytes 258056 | tf_op jit(solution)/shard_map/ppermute | solution.py:955
  175.6 5.9 %collective-permute-start.31 = (f32[8,2688]{1,0:T(8,128)S(1)}, f32[8,2688]{1,0:T(8,128)S(1)}, u32[]{:S(2)}, u32[]{:S(2)}) collective-permute-start(f32[8,2688]{1,0:T(8,128)S(1)} %shard_map.213), channel_id=1, source_target_pairs={{0,1},{1,0},{2,3},{3,2},{4,5},{5,4},{6,7},{7,6},{8,9},{9,8},{10,11... | collective-permute-start | bytes 258056 | tf_op jit(solution)/shard_map/ppermute | solution.py:958
  176.8 7.1 %collective-permute-start.24 = (bf16[128,512]{1,0:T(8,128)(2,1)S(1)}, bf16[128,512]{1,0:T(8,128)(2,1)S(1)}, u32[]{:S(2)}, u32[]{:S(2)}) collective-permute-start(bf16[128,512]{1,0:T(8,128)(2,1)S(1)} %get-tuple-element.234), channel_id=1, source_target_pairs={{0,1},{1,0},{2,3},{3,2},{4,5},{5,4},{6,7},{7,6},{8,9},{9,8},{10,11... | collective-permute-start | bytes 393224 | tf_op jit(solution)/shard_map/ppermute | solution.py:861
  177.7 11.7 %collective-permute-start.23 = (f32[8,5376]{1,0:T(8,128)S(1)}, f32[8,5376]{1,0:T(8,128)S(1)}, u32[]{:S(2)}, u32[]{:S(2)}) collective-permute-start(f32[8,5376]{1,0:T(8,128)S(1)} %get-tuple-element.232), channel_id=1, source_target_pairs={{3,1},{5,3},{7,5},{11,9},{13,11},{15,13},{19,17},{21,19},{23,21},{... | collective-permute-start | bytes 516104 | tf_op jit(solution)/shard_map/ppermute | solution.py:962
  178.4 11.1 %collective-permute-start.22 = (f32[8,5376]{1,0:T(8,128)S(1)}, f32[8,5376]{1,0:T(8,128)S(1)}, u32[]{:S(2)}, u32[]{:S(2)}) collective-permute-start(f32[8,5376]{1,0:T(8,128)S(1)} %get-tuple-element.232), channel_id=1, source_target_pairs={{2,1},{4,3},{6,5},{10,9},{12,11},{14,13},{18,17},{20,19},{22,21},{... | collective-permute-start | bytes 516104 | tf_op jit(solution)/shard_map/ppermute | solution.py:961
  179.1 9.1 %collective-permute-start.25 = (bf16[128,640]{1,0:T(8,128)(2,1)S(1)}, bf16[128,640]{1,0:T(8,128)(2,1)S(1)}, u32[]{:S(2)}, u32[]{:S(2)}) collective-permute-start(bf16[128,640]{1,0:T(8,128)(2,1)S(1)} %get-tuple-element.235), channel_id=1, source_target_pairs={{0,1},{1,0},{2,3},{3,2},{4,5},{5,4},{6,7},{7,6},{8,9},{9,8},{10,11... | collective-permute-start | bytes 491528 | tf_op jit(solution)/shard_map/ppermute | solution.py:861
  181.6 10.3 %collective-permute-start.32 = (f32[2,8,2688]{2,1,0:T(8,128)S(1)}, f32[2,8,2688]{2,1,0:T(8,128)S(1)}, u32[]{:S(2)}, u32[]{:S(2)}) collective-permute-start(f32[2,8,2688]{2,1,0:T(8,128)S(1)} %pad_maximum_fusion.refs_0_), channel_id=1, source_target_pairs={{0,8},{8,0},{16,24},{24,16},{1,9},{9,1},{17,25},{25,17},{2,10},{10... | collective-permute-start | bytes 516104 | tf_op jit(solution)/shard_map/ppermute | solution.py:959
  (23 other events, 67.0 us)

commit v3 on v2

--- a/solution.py
+++ b/solution.py
@@ -99,44 +99,96 @@
     return dx, jnp.concatenate(dw, axis=0)
 
 
-def pack_small_kernel(yv, b, c, dt, xr, br, cr, msg_ref, rim_ref):
-    width = b.shape[1]
-    msg_ref[:, 0:width] = b[...]
-    msg_ref[:, width : 2 * width] = c[...]
-    msg_ref[:, 2 * width :] = dt[...]
-    half = xr.shape[1] // 2
+def copies(pairs, sems):
+    moves = [pltpu.make_async_copy(src, dst, sems.at[i]) for i, (src, dst) in enumerate(pairs)]
+    for m in moves:
+        m.start()
+    for m in moves:
+        m.wait()
+
+
+def pack_rim_kernel(yv, x, b, c, out, xt, bt, ct, sems):
+    half = x.shape[1] // 2
+    width = b.shape[1] // 2
+    step = 2 * width
+    copies([(src.at[pl.ds(Q - 16, 16)], dst) for src, dst in ((x, xt), (b, bt), (c, ct))], sems)
+    x3, b3, c3 = [r[...].astype(F32)[13:16] for r in (xt, bt, ct)]
+    blocks = half // step + 1
     for k in range(2):
-        rim_ref[k, :, 0:half] = xr[:, k * half : (k + 1) * half]
-        rim_ref[k, :, half : half + width] = br[:, k * width : (k + 1) * width]
-        rim_ref[k, :, half + width :] = cr[:, k * width : (k + 1) * width]
-
-
-def pack_kernel(yv, x, dy, out):
-    out[0] = x[...]
-    out[1] = dy[...]
-
-
-def unpack_kernel(yv, got, y_ref, gx_ref):
+        items = []
+        for r in range(3):
+            for i in range(blocks - 1):
+                at = k * half + i * step
+                items.append(x3[r : r + 1, at : at + step])
+            mine = slice(k * width, (k + 1) * width)
+            items.append(jnp.concatenate([b3[r : r + 1, mine], c3[r : r + 1, mine]], axis=1))
+        items.append(jnp.zeros((16 - 3 * blocks, step), F32))
+        out[16 * k : 16 * (k + 1)] = jnp.concatenate(items, axis=0).astype(BF16)
+
+
+def pack_small_kernel(yv, b, c, dt, out, sems):
+    width = b.shape[1] // 2
+    at = pl.multiple_of((1 - yv[0]) * width, 128)
+    copies(
+        [
+            (b.at[:, pl.ds(at, width)], out.at[pl.ds(0, Q), pl.ds(0, width)]),
+            (c.at[:, pl.ds(at, width)], out.at[pl.ds(0, Q), pl.ds(width, width)]),
+            (dt, out.at[pl.ds(0, Q), pl.ds(2 * width, dt.shape[1])]),
+        ],
+        sems,
+    )
+
+
+def pack_kernel(yv, x, dy, out, sems, *, chunk, chunks):
+    width = out.shape[2]
+    at = pl.multiple_of(((1 - yv[0]) * chunks + chunk) * width, 128)
+    copies([(x.at[:, pl.ds(at, width)], out.at[0]), (dy.at[:, pl.ds(at, width)], out.at[1])], sems)
+
+
+def unpack_kernel(yv, got, y_ref, gx_ref, mark):
     y_ref[...] = got[0]
     gx_ref[...] = got[1]
+    mark[...] = jnp.zeros(mark.shape, F32)
 
 
 def setup_kernel(
-    yv, b_own, c_own, dt_own, rec, rim0, rim1, wb, wc, bb, bc_, par, exp2,
+    yv, b_own, c_own, dt_own, rec, rim, rim_e, rim_o, wb, wc, bb, bc_, par, exp2,
     halo_ref, bc_ref, cc_ref, bt_ref, ct_ref, ds_ref, fe_ref, rows_ref, cols_ref, rowt_ref, st_ref,
-    xs, dts, xs2,
+    xs, dts, xs2, rims,
 ):
     y = yv[0]
     width = b_own.shape[1]
     heads = par.shape[1]
     half = halo_ref.shape[1] - 2 * width
-    halo_ref[...] = (rim0[...].astype(F32) + rim1[...].astype(F32))[8:16]
+
+    @pl.when(y == 0)
+    def _():
+        rims[...] = rim[0:16].astype(F32)
+
+    @pl.when((y != 0) & (yv[2] == 0))
+    def _():
+        rims[...] = rim_o[16:32].astype(F32)
+
+    @pl.when((y != 0) & (yv[2] != 0))
+    def _():
+        rims[...] = rim_e[16:32].astype(F32)
+
+    blocks = halo_ref.shape[1] // rim.shape[1]
+    keep = jnp.where(yv[1] == 0, 0.0, 1.0)
+    halo_ref[...] = keep * jnp.concatenate(
+        [jnp.zeros((5, halo_ref.shape[1]), F32)]
+        + [
+            jnp.concatenate([rims[r * blocks + i : r * blocks + i + 1] for i in range(blocks)], axis=1)
+            for r in range(3)
+        ],
+        axis=0,
+    )
     for i, (own, w, bias, out, out_t) in enumerate(
         ((b_own, wb, bb, bc_ref, bt_ref), (c_own, wc, bc_, cc_ref, ct_ref))
     ):
         at = i * width
         xs[0:8] = halo_ref[:, half + at : half + at + width]
-        in_order(y, own[...], rec[:, at : at + width], xs, 8)
+        in_order(y, own[...], rec[0:Q, at : at + width], xs, 8)
         v, slope = gates(conv_sum(xs, w, bias, 2 * Q))
         out[...] = v.astype(BF16)
         out_t[...] = jnp.transpose(v).astype(BF16)
@@ -145,11 +197,11 @@
     @pl.when(y == 0)
     def _():
         dts[0:Q] = dt_own[:, 0:heads].astype(F32)
-        dts[Q : 2 * Q] = rec[:, 2 * width : 2 * width + heads].astype(F32)
+        dts[Q : 2 * Q] = rec[0:Q, 2 * width : 2 * width + heads].astype(F32)
 
     @pl.when(y != 0)
     def _():
-        dts[0:Q] = rec[:, 2 * width + heads : 2 * width + 2 * heads].astype(F32)
+        dts[0:Q] = rec[0:Q, 2 * width + heads : 2 * width + 2 * heads].astype(F32)
         dts[Q : 2 * Q] = dt_own[:, heads : 2 * heads].astype(F32)
 
     raw = dts[...] + par[1:2]
@@ -202,15 +254,18 @@
 
 
 def hop_kernel(yv, in_e, in_o, t, u, row_f, row_b, out_e, out_o):
+    row_f = row_f[2:3] * jnp.where(yv[1] == 0, 0.0, 1.0)
+    row_b = row_b[2:3] * jnp.where(yv[4] == 0, 0.0, 1.0)
+
     @pl.when(yv[2] == 0)
     def _():
-        out_e[...] = (row_f[2:3] * in_o[...].astype(F32) + t[0].astype(F32)).astype(BF16)
-        out_o[...] = (row_b[2:3] * in_e[...].astype(F32) + u[0].astype(F32)).astype(BF16)
+        out_e[...] = (row_f * in_o[...].astype(F32) + t[0].astype(F32)).astype(BF16)
+        out_o[...] = (row_b * in_e[...].astype(F32) + u[0].astype(F32)).astype(BF16)
 
     @pl.when(yv[2] != 0)
     def _():
-        out_o[...] = (row_f[2:3] * in_e[...].astype(F32) + t[0].astype(F32)).astype(BF16)
-        out_e[...] = (row_b[2:3] * in_o[...].astype(F32) + u[0].astype(F32)).astype(BF16)
+        out_o[...] = (row_f * in_e[...].astype(F32) + t[0].astype(F32)).astype(BF16)
+        out_e[...] = (row_b * in_o[...].astype(F32) + u[0].astype(F32)).astype(BF16)
 
 
 def within_kernel(yv, xc, dyo, cols, rowt, bc, cc, yi_ref, dxi_ref, dcb_ref, cb):
@@ -389,11 +444,11 @@
 
 def finish_last_kernel(
     yv, b_own, c_own, b_rec, c_rec, b_halo, c_halo, wb, wc, slope, bc, cc,
-    dc0, db0, dcb0, dc1, db1, dcb1, st, par, seg, *rest,
+    dc0, db0, dcb0, dc1, db1, dcb1, st, par, seg, heads_before, *rest,
 ):
-    chunks = (len(rest) - 10) // 2
+    chunks = (len(rest) - 11) // 2
     wvs, ends, rest = rest[:chunks], rest[chunks : 2 * chunks], rest[2 * chunks :]
-    gb_ref, gc_ref, red_ref, head_ref, send_ref, gdt_ref, xs, gs, gv, gd = rest
+    gb_ref, gc_ref, red_ref, head_ref, send_ref, gdt_ref, next_ref, xs, gs, gv, gd = rest
     y = yv[0]
     finish_group(
         yv, b_own, c_own, b_rec, c_rec, b_halo, c_halo, wb, wc, slope, bc, cc,
@@ -431,6 +486,22 @@
         axis=1,
     )
     head_ref[:, 2 * N :] = jnp.zeros((8, head_ref.shape[1] - 2 * N), F32)
+    piece = head_ref.shape[1]
+    items = []
+    for r in range(3):
+        row = slice(r, r + 1)
+        items += [heads_before[row, 2 * piece + i * cw : 2 * piece + (i + 1) * cw] for i in range(chunks)]
+        items.append(
+            jnp.concatenate(
+                [
+                    heads_before[row, 0:N], head_ref[row, 0:N],
+                    heads_before[row, N : 2 * N], head_ref[row, N : 2 * N],
+                ],
+                axis=1,
+            )
+        )
+    items.append(jnp.zeros((16 - 3 * (chunks + 1), cw), F32))
+    next_ref[...] = jnp.concatenate(items, axis=0)
     gd[...] = jnp.concatenate([draw, draw], axis=1).astype(BF16)
 
     @pl.when(y == 0)
@@ -449,6 +520,11 @@
     for r in refs[1:-1]:
         total = total + r[...]
     refs[-1][...] = total
+
+
+def join_kernel(yv, first, second, out):
+    out[0] = first[...]
+    out[1] = second[...]
 
 
 def close_kernel(yv, got0, got1, gdt_own, gb_ref, gc_ref, gdt_ref):
@@ -469,39 +545,46 @@
         gdt_ref[...] = jnp.where(low, got, own).astype(BF16)
 
 
-def rim_kernel(yv, next0, next1, w, gx, gb, gc, gx_ref, gb_ref, gc_ref):
-    wide = gx.shape[1] // 2
-    base = next0.shape[1] - wide
-    step = base // 2
-
-    def add(src, dst, pieces):
-        at = 0
-        for ref, lo, size, wlo in pieces:
-            h = ref[:, lo : lo + size]
-            k = w[:, wlo : wlo + size]
-            more = jnp.concatenate(
-                [
-                    jnp.zeros((13, size), F32),
-                    k[0:1] * h[0:1],
-                    k[0:1] * h[1:2] + k[1:2] * h[0:1],
-                    k[0:1] * h[2:3] + k[1:2] * h[1:2] + k[2:3] * h[0:1],
-                ],
-                axis=0,
-            )
-            dst[:, at : at + size] = (src[:, at : at + size].astype(F32) + more).astype(BF16)
-            at += size
-
-    both = (next0, next1)
-    add(gx, gx_ref, [(both[k], base, wide, k * wide) for k in range(2)])
-    for i, (src, dst) in enumerate(((gb, gb_ref), (gc, gc_ref))):
-        first = 2 * wide + i * 4 * N
-        add(
-            src, dst,
-            [(both[k], g * step + i * N, N, first + (2 * k + g) * N) for k in range(2) for g in range(2)],
+def rim_kernel(yv, next0, next_e, next_o, w, gx, gb, gc, gx_ref, gb_ref, gc_ref, mark, both):
+    mark[...] = jnp.zeros(mark.shape, F32)
+    both[0] = next0[...]
+
+    @pl.when(yv[2] == 0)
+    def _():
+        both[1] = next_e[...]
+
+    @pl.when(yv[2] != 0)
+    def _():
+        both[1] = next_o[...]
+
+    step = next0.shape[1]
+    blocks = gx.shape[1] // 2 // step
+    keep = jnp.where((yv[0] == 0) | (yv[4] == 0), 0.0, 1.0)
+
+    def add(src, dst, lo, half, block, at, width, to):
+        h = [keep * both[half, r * (blocks + 1) + block : r * (blocks + 1) + block + 1, at : at + width] for r in range(3)]
+        k = w[:, lo : lo + width]
+        more = jnp.concatenate(
+            [
+                jnp.zeros((13, width), F32),
+                k[0:1] * h[0],
+                k[0:1] * h[1] + k[1:2] * h[0],
+                k[0:1] * h[2] + k[1:2] * h[1] + k[2:3] * h[0],
+            ],
+            axis=0,
         )
-
-
-def sums_kernel(yv, mine, theirs, gw_ref, gb_ref, gh_ref, both, *, wide):
+        dst[:, to : to + width] = (src[:, to : to + width].astype(F32) + more).astype(BF16)
+
+    for half in range(2):
+        for i in range(blocks):
+            at = (half * blocks + i) * step
+            add(gx, gx_ref, at, half, i, 0, step, at)
+        for i, (src, dst) in enumerate(((gb, gb_ref), (gc, gc_ref))):
+            to = half * step // 2
+            add(src, dst, (2 * blocks + i) * step + to, half, blocks, i * step // 2, step // 2, to)
+
+
+def sums_kernel(yv, mine, theirs, gw_ref, gb_ref, gh_ref, both, *, wide, heads):
     width = mine.shape[2]
 
     @pl.when(yv[3] == 0)
@@ -516,7 +599,6 @@
 
     base = 2 * width - wide
     step = base // 2
-    heads = gh_ref.shape[1] // 2
 
     def fill(order):
         for k in range(2):
@@ -529,9 +611,18 @@
                     gw_ref[:, to : to + N] = v[0:4, g * step + i * N : g * step + (i + 1) * N]
                     gb_ref[:, to : to + N] = v[4:5, g * step + i * N : g * step + (i + 1) * N]
         at = step + 2 * N
-        gh_ref[...] = jnp.concatenate(
+        values = jnp.concatenate(
             [both[order[0]][:, at : at + heads], both[order[1]][:, at : at + heads]], axis=1
         )
+        per_dev = gh_ref.shape[1]
+        row = lax.broadcasted_iota(jnp.int32, (2 * heads, per_dev), 0)
+        col = lax.broadcasted_iota(jnp.int32, (2 * heads, per_dev), 1)
+        pick = jnp.where(row == col + yv[5] * per_dev, 1.0, 0.0).astype(BF16)
+        hi = values.astype(BF16)
+        rest = values - hi.astype(F32)
+        mid = rest.astype(BF16)
+        low = (rest - mid.astype(F32)).astype(BF16)
+        gh_ref[...] = (dot(hi, pick) + dot(mid, pick) + dot(low, pick))[0:3]
 
     @pl.when(yv[0] == 0)
     def _():
@@ -586,7 +677,7 @@
     y = lax.rem(me, 2)
     z = me // 2
     core = lax.rem(lax.axis_index("dp"), 2)
-    yv = jnp.stack([y, z, lax.rem(z, 2), core]).astype(jnp.int32)
+    yv = jnp.stack([y, z, lax.rem(z, 2), core, spots - 1 - z, me]).astype(jnp.int32)
     xw = x_rows.shape[1] // 2
     bw = b_rows.shape[1] // 2
     hl = dt_rows.shape[1] // 2
@@ -611,37 +702,61 @@
             return pl.BlockSpec((Q, width), lambda j, yr: (0, (1 - yr[0]) * step + plus))
         return pl.BlockSpec((Q, width), lambda j, yr: (0, yr[0] * step + plus))
 
-    def tail(width):
-        return pl.BlockSpec((16, width), lambda j, yr: (Q // 16 - 1, 0))
-
-    msg, rims = call(
-        pack_small_kernel, yv, (1,),
+    def joint(v, fn):
+        moves = []
+        for d in range(dp_size):
+            for i in range(devices):
+                to = fn(i)
+                if to is None or not 0 <= to < devices:
+                    moves.append((d * devices + i, (d ^ 1) * devices + i))
+                else:
+                    moves.append((d * devices + i, d * devices + to))
+        return lax.ppermute(v, ("dp", "sp"), moves)
+
+    def slant(i):
+        return i + 1 if i % 2 else i - 1
+
+    def evens(i):
+        return i ^ 2
+
+    def odds(i):
+        return ((i + 2) ^ 2) - 2 if 2 <= i < devices - 2 else None
+
+    in_hbm = pl.BlockSpec(memory_space=pltpu.MemorySpace.HBM)
+    anywhere = pl.BlockSpec(memory_space=pl.ANY)
+    (msg,) = call(
+        pack_small_kernel, yv, (1,), [(b_rows, in_hbm), (c_rows, in_hbm), (dt_rows, in_hbm)],
+        [(shape_of(Q, 2 * bw + 2 * hl, dtype=BF16), anywhere)],
+        [pltpu.SemaphoreType.DMA((3,))], 1, 1 << 20,
+    )
+    rec_bc = lax.ppermute(msg, "sp", swap)
+    (rim_out,) = call(
+        pack_rim_kernel, yv, (1,), [(x_rows, in_hbm), (b_rows, in_hbm), (c_rows, in_hbm)],
+        [(shape_of(32, 2 * bw, dtype=BF16), whole((32, 2 * bw)))],
         [
-            (b_rows, cols(bw, True)), (c_rows, cols(bw, True)), (dt_rows, whole(dt_rows.shape)),
-            (x_rows, tail(2 * xw)), (b_rows, tail(2 * bw)), (c_rows, tail(2 * bw)),
+            pltpu.VMEM((16, 2 * xw), BF16), pltpu.VMEM((16, 2 * bw), BF16),
+            pltpu.VMEM((16, 2 * bw), BF16), pltpu.SemaphoreType.DMA((3,)),
         ],
-        [
-            (shape_of(Q, 2 * bw + 2 * hl, dtype=BF16), whole((Q, 2 * bw + 2 * hl))),
-            (shape_of(2, 16, xw + 2 * bw, dtype=BF16), whole((2, 16, xw + 2 * bw))),
-        ],
-        [], 1, 2 << 20,
-    )
-    rec_bc = lax.ppermute(msg, "sp", swap)
-    rim0 = lax.ppermute(rims[0], "sp", pairs(lambda i: i + 1 if i % 2 else None))
-    rim1 = lax.ppermute(rims[1], "sp", pairs(lambda i: i + 2 if i % 2 else None))
-
+        1, 1 << 20, after=[msg],
+    )
+    rim = joint(rim_out, slant)
+    rim_e = joint(rim_out, evens)
+    rim_o = joint(rim_out, odds)
     rec = []
 
     def send_chunk(c, after):
+        def kernel(*refs):
+            pack_kernel(*refs, chunk=c, chunks=chunks)
+
         (out,) = call(
-            pack_kernel, yv, (1,),
-            [(x_rows, cols(cw, True, chunks, c)), (dy_rows, cols(cw, True, chunks, c))],
-            [(shape_of(2, Q, cw, dtype=BF16), whole((2, Q, cw)))],
-            [], 1, 1 << 20, after=after,
+            kernel, yv, (1,), [(x_rows, in_hbm), (dy_rows, in_hbm)],
+            [(shape_of(2, Q, cw, dtype=BF16), anywhere)],
+            [pltpu.SemaphoreType.DMA((2,))], 1, 1 << 20, after=after,
         )
         rec.append(lax.ppermute(out, "sp", swap))
-
-    send_chunk(0, [msg])
+        return out
+
+    send_chunk(0, [rim_out])
 
     par = lax.dynamic_slice_in_dim(
         jnp.concatenate([jnp.stack([a_log, dt_bias, skip_gain]), jnp.zeros((5, 2 * hl), F32)], 0),
@@ -662,7 +777,7 @@
         setup_kernel, yv, (1,),
         [
             (b_rows, cols(bw, False)), (c_rows, cols(bw, False)), (dt_rows, whole(dt_rows.shape)),
-            (rec_bc, whole(rec_bc.shape)), (rim0, whole(rim0.shape)), (rim1, whole(rim1.shape)),
+            (rec_bc, whole(rec_bc.shape)), (rim, whole(rim.shape)), (rim_e, whole(rim.shape)), (rim_o, whole(rim.shape)),
             (conv_weight, wide_w(4, first_b)), (conv_weight, wide_w(4, first_c)),
             (bias, wide_w(1, first_b)), (bias, wide_w(1, first_c)),
             (par, whole((8, hl))), (exp2, whole((2 * hl, xw))),
@@ -682,7 +797,7 @@
         ],
         [
             pltpu.VMEM((two + 8, bw), F32), pltpu.VMEM((two, hl), F32),
-            pltpu.VMEM((2 * hl, two), F32),
+            pltpu.VMEM((2 * hl, two), F32), pltpu.VMEM((16, rim.shape[1]), F32),
         ],
         4, 4 << 20,
     )
@@ -794,12 +909,16 @@
 
     def unpack(c, after):
         full = shape_of(Q, 2 * xw, dtype=BF16)
-        finals[:2] = call(
+        *finals[:2], mark = call(
             unpack_kernel, yv, (1,),
             [(got_x[c], whole((2, Q, cw)))],
-            [(full, cols(cw, True, chunks, c)), (full, cols(cw, True, chunks, c))],
+            [
+                (full, cols(cw, True, chunks, c)), (full, cols(cw, True, chunks, c)),
+                (shape_of(8, 128), whole((8, 128))),
+            ],
             [], 1, 1 << 20, keep=finals[:2], after=after,
         )
+        return mark
 
     grads_bc = []
 
@@ -841,9 +960,11 @@
         ]
         if last:
             ins += [(st, whole(st.shape)), (par, whole(par.shape)), (seg, whole(seg.shape))]
+            ins.append((finals[3], whole(finals[3].shape)))
             ins += [(s[2], whole(s[2].shape)) for s in sums]
             ins += [(s[3], whole(s[3].shape)) for s in sums]
             outs.append((shape_of(Q, 2 * hl, dtype=BF16), whole((Q, 2 * hl))))
+            outs.append((shape_of(16, cw), whole((16, cw))))
             scratch.append(pltpu.VMEM((two, 2 * hl), BF16))
         kernel = finish_last_kernel if last else finish_kernel
         count = len(ins)
@@ -858,10 +979,8 @@
         )
         finals[2:4] = out[:2]
         grads_bc = list(out[2:4])
-        return lax.ppermute(out[4], "sp", swap), (out[5] if last else out[4])
-
-    evens = pairs(lambda i: i ^ 2)
-    odds = pairs(lambda i: ((i + 2) ^ 2) - 2 if 2 <= i < devices - 2 else None)
+        return lax.ppermute(out[4], "sp", swap), out[4:]
+
     zero = jnp.zeros((N, cw), BF16)
     in_e, in_o = zero, zero
     ins_e, ins_o = [], []
@@ -902,8 +1021,8 @@
                 [], 1, 3 << 20, after=waits,
             )
             token = [out_e]
-            in_e = lax.ppermute(out_e, "sp", evens)
-            in_o = lax.ppermute(out_o, "sp", odds)
+            in_e = joint(out_e, evens)
+            in_o = joint(out_o, odds)
         waits = []
         if t + 1 < chunks:
             waits.append(state(t + 1, token))
@@ -917,17 +1036,13 @@
             leas = [(ins_o if (spots - 1 - k) % 2 else ins_e)[c + k - 1] for k in range(1, spots)]
             waits.append(across(c, ents, leas, token))
             if c == chunks - 2:
-                unpack(0, token)
+                mark = unpack(0, token)
                 got, tok = finish(0, False, token)
                 got_bc.append(got)
-                waits += [tok, finals[0]]
-            if c == chunks - 1:
-                unpack(1, [])
-                unpack(2, [])
-    got, gdt_own = finish(1, True, [finals[0]])
+                waits += [tok[0], mark]
+    got, (_, gdt_own, next_rows) = finish(1, True, [])
     got_bc.append(got)
-    unpack(3, [gdt_own])
-    y_all, gx_all, red, heads_ = finals
+    red = finals[2]
 
     hw = (base + xw) // 2
     slab = shape_of(8, hw)
@@ -947,19 +1062,25 @@
     mine = add([(red, side(False)), (lax.ppermute(theirs, "dp", pairs(lambda i: i ^ 1, dp_size)), whole((8, hw)))])
     size = 2
     while size < dp_size:
-        mine = mine + lax.ppermute(mine, "dp", pairs(lambda i: i ^ size, dp_size))
+        got = lax.ppermute(mine, "dp", pairs(lambda i: i ^ size, dp_size))
+        marks = []
+        if size == 2:
+            marks = [unpack(1, [mine]), unpack(2, [mine])]
+        mine = add([(mine, whole((8, hw))), (got, whole((8, hw)))], marks)
         size *= 2
+    mark = unpack(3, [mine])
+    y_all, gx_all = finals[:2]
     size = 2
     while size < devices:
         ways = 4 if size * 4 <= devices else 2
         got = [lax.ppermute(mine, "sp", pairs(lambda i: i ^ (size * k))) for k in range(1, ways)]
         size *= ways
-        mine = add([(v, whole((8, hw))) for v in [mine] + got], [y_all] if size >= devices else [])
-    mine = jnp.stack([mine, lax.ppermute(mine, "sp", swap)])
-    theirs = lax.ppermute(mine, "dp", pairs(lambda i: i ^ 1, dp_size))
-
-    next0 = lax.ppermute(heads_, "sp", pairs(lambda i: i - 1 if i % 2 == 0 else None))
-    next1 = lax.ppermute(heads_, "sp", pairs(lambda i: i - 2 if i % 2 else None))
+        mine = add([(v, whole((8, hw))) for v in [mine] + got], [mark] if size >= devices else [])
+    got_y = lax.ppermute(mine, "sp", swap)
+
+    next0 = joint(next_rows, slant)
+    next_e = joint(next_rows, evens)
+    next_o = joint(next_rows, odds)
     full = shape_of(Q, 2 * bw, dtype=BF16)
     gb, gc, gdt = call(
         close_kernel, yv, (1,),
@@ -971,26 +1092,34 @@
             (full, cols(bw, True)), (full, cols(bw, True)),
             (shape_of(Q, 2 * hl, dtype=BF16), whole((Q, 2 * hl))),
         ],
-        [], 1, 1 << 20, keep=grads_bc,
-    )
+        [], 1, 1 << 20, keep=grads_bc, after=[mine],
+    )
+    (mine,) = call(
+        join_kernel, yv, (1,), [(mine, whole((8, hw))), (got_y, whole((8, hw)))],
+        [(shape_of(2, 8, hw), whole((2, 8, hw)))], [], 1, 1 << 20, after=[gdt],
+    )
+    theirs = lax.ppermute(mine, "dp", pairs(lambda i: i ^ 1, dp_size))
     last = [pl.BlockSpec((16, v.shape[1]), lambda j, yr: (Q // 16 - 1, 0)) for v in (gx_all, gb, gc)]
     kept = [gx_all, gb, gc]
-    grad_x, grad_b, grad_c = pl.pallas_call(
+    grad_x, grad_b, grad_c, mark = pl.pallas_call(
         rim_kernel,
-        out_shape=[shape_of(*v.shape, dtype=BF16) for v in kept],
+        out_shape=[shape_of(*v.shape, dtype=BF16) for v in kept] + [shape_of(8, 128)],
         grid_spec=pltpu.PrefetchScalarGridSpec(
             num_scalar_prefetch=1,
             grid=(1,),
-            in_specs=[whole(next0.shape), whole(next1.shape), whole(conv_weight.shape)] + last,
-            out_specs=last,
+            in_specs=[whole(next0.shape)] * 3 + [whole(conv_weight.shape)] + last,
+            out_specs=last + [whole((8, 128))],
+            scratch_shapes=[pltpu.VMEM((2, 16, cw), F32)],
         ),
         compiler_params=params(),
         cost_estimate=cost(1, 1 << 20),
-        input_output_aliases={4: 0, 5: 1, 6: 2},
-    )(yv, next0, next1, conv_weight, *kept)
+        input_output_aliases={5: 0, 6: 1, 7: 2},
+    )(yv, next0, next_e, next_o, conv_weight, *kept)
+
+    per_dev = 2 * hl // devices
 
     def summed(*refs):
-        sums_kernel(*refs, wide=xw)
+        sums_kernel(*refs, wide=xw, heads=hl)
 
     gw, gbias, gheads = call(
         summed, yv, (1,),
@@ -998,15 +1127,13 @@
         [
             (shape_of(4, bias.shape[1]), whole((4, bias.shape[1]))),
             (shape_of(1, bias.shape[1]), whole((1, bias.shape[1]))),
-            (shape_of(8, 2 * hl), whole((8, 2 * hl))),
+            (shape_of(3, per_dev), whole((3, per_dev))),
         ],
-        [pltpu.VMEM((2, 8, base + xw), F32)], 1, 1 << 20, after=[grad_x, gdt],
-    )
-
-    per_dev = 2 * hl // devices
-    head_total = lax.dynamic_slice(gheads, (0, me * per_dev), (3, per_dev))
+        [pltpu.VMEM((2, 8, base + xw), F32)], 1, 1 << 20, after=[mark],
+    )
+
     return (
-        y_all[None], grad_x[None], grad_b[None], grad_c[None], gdt[None], gw, gbias[0], head_total,
+        y_all[None], grad_x[None], grad_b[None], grad_c[None], gdt[None], gw, gbias[0], gheads,
     )
 
 

time: 196 us -> 181 us (0.923)
  starting transfers between devices: 56.6 us -> 35 us
  waiting for transfers between devices: 26.6 us -> 40 us
  local copies, waits for them, and re-layouts: 12.3 us -> 5.52 us
    ppermute x19 -> x21, starting transfers between devices: 34.8 us -> 18.3 us  [the longest x17 13.2 us: joint(): return lax.ppermute(v, ('dp', 'sp'), moves)]
    ppermute x19 -> x21, waiting for transfers between devices: 12 us -> 26.5 us  [the longest x17 23.9 us: joint(): return lax.ppermute(v, ('dp', 'sp'), moves)]
    unnamed x44 -> x37, local copies, waits for them, and re-layouts: 10.7 us -> 5.23 us
    ppermute x1, starting transfers between devices: 6.42 us -> 1.52 us  [per_device(): rec_bc = lax.ppermute(msg, 'sp', swap)]
    pallas_call x35 -> x38, Pallas kernels: 96.2 us -> 97 us  [call(): pl.pallas_call(run, out_shape=[o[0] for o in outs], grid_spec=pltpu.Prefe...]
  transfers between devices with their start and end apart: 33 -> 35, of which waited for: 11 -> 14; matrix products, arithmetic and copies ran while one was open for 0% -> 0% of each run, Pallas kernels for 48% -> 52%
where the time goes in v3:
time: 181 us
  Pallas kernels  99.4 us (55%)
  waiting for transfers between devices  40 us (22%)
  starting transfers between devices  35 us (19%)
  local copies, waits for them, and re-layouts  5.52 us (3%)
    pallas_call x38, Pallas kernels, call(): pl.pallas_call(run, out_shape=[o[0] for o in outs], grid_spec=pltpu.Prefe...  97 us
    ppermute x17, waiting for transfers between devices, joint(): return lax.ppermute(v, ('dp', 'sp'), moves)  23.9 us
    ppermute x17, starting transfers between devices, joint(): return lax.ppermute(v, ('dp', 'sp'), moves)  13.2 us
    ppermute x1, waiting for transfers between devices, per_device(): rec_bc = lax.ppermute(msg, 'sp', swap)  7.06 us
    ppermute x4, starting transfers between devices, send_chunk(): rec.append(lax.ppermute(out, 'sp', swap))  6.05 us
    unnamed x37, local copies, waits for them, and re-layouts  5.23 us
    ppermute x4, starting transfers between devices, across(): got_x.append(lax.ppermute(out[4], 'sp', swap))  4.55 us
    ppermute x3, waiting for transfers between devices, per_device(): lax.ppermute(mine, 'sp', pairs(lambda i: i ^ size * k))  4.42 us
  transfers between devices with their start and end apart: 35, of which 14 were waited for; matrix products, arithmetic and copies ran while one was open for 0% of the time, Pallas kernels for 52%

profile of v3, /device:TPU:0, one launch (start us, length us, event | category | flops | bytes accessed | tf_op | source)
XLA Modules:
  0.0 181.0 jit_solution(4497848533552415448)
XLA Ops:
  6.1 4.1 %collective-permute-start.4 = (bf16[32,1024]{1,0:T(8,128)(2,1)S(1)}, bf16[32,1024]{1,0:T(8,128)(2,1)}, u32[]{:S(2)}, u32[]{:S(2)}) collective-permute-start(bf16[32,1024]{1,0:T(8,128)(2,1)S(1)} %shard_map.182.refs_2_), channel_id=1, source_target_pairs={{0,2},{1,3},{2,0},{3,1},{4,6},{5,7},{6,4},{7,5},{8,10},{9,11},{10,... | collective-permute-start | bytes 196616 | tf_op jit(solution)/shard_map/ppermute | solution.py:714
  13.2 7.1 %collective-permute-done.refs_2_.refs_3_ = bf16[128,1152]{1,0:T(8,128)(2,1)S(1)} collective-permute-done((bf16[128,1152]{1,0:T(8,128)(2,1)}, bf16[128,1152]{1,0:T(8,128)(2,1)S(1)}, u32[]{:S(2)}, u32[]{:S(2)}) %collective-permute-start) | collective-permute-done | bytes 294944 | tf_op jit(solution)/shard_map/ppermute | solution.py:732
  22.5 2.4 %collective-permute-start.1 = (bf16[2,128,1024]{2,1,0:T(8,128)(2,1)S(1)}, bf16[2,128,1024]{2,1,0:T(8,128)(2,1)S(1)}, u32[]{:S(2)}, u32[]{:S(2)}) collective-permute-start(bf16[2,128,1024]{2,1,0:T(8,128)(2,1)S(1)} %shard_map.180), channel_id=1, source_target_pairs={{0,1},{1,0},{2,3},{3,2},{4,5},{5,4},{6,7},{7,6},{8,9},{9,8},{10,11... | collective-permute-start | bytes 1572872 | tf_op jit(solution)/shard_map/ppermute | solution.py:756
  25.1 4.6 %shard_map.183 = (f32[8,5120]{1,0:T(8,128)S(1)}, bf16[256,512]{1,0:T(8,128)(2,1)S(1)}, bf16[256,512]{1,0:T(8,128)(2,1)S(1)}, bf16[512,256]{1,0:T(8,128)(2,1)S(1)...) custom-call(s32[6]{0:T(128)S(1)} %stack.36.yr.yv, ...), custom_call_target="tpu_custom_call" | custom-call | flops 4000000000 | bytes 4194304 | tf_op jit(solution)/shard_map/pallas_call | solution.py:652
  32.3 2.4 %collective-permute-start.7 = (bf16[2,128,1024]{2,1,0:T(8,128)(2,1)S(1)}, bf16[2,128,1024]{2,1,0:T(8,128)(2,1)S(1)}, u32[]{:S(2)}, u32[]{:S(2)}) collective-permute-start(bf16[2,128,1024]{2,1,0:T(8,128)(2,1)S(1)} %shard_map.185), channel_id=1, source_target_pairs={{0,1},{1,0},{2,3},{3,2},{4,5},{5,4},{6,7},{7,6},{8,9},{9,8},{10,11... | collective-permute-start | bytes 1572872 | tf_op jit(solution)/shard_map/ppermute | solution.py:756
  34.8 4.1 %shard_map.186 = (bf16[4,256,1024]{2,1,0:T(8,128)(2,1)S(1)}, bf16[4,256,1024]{2,1,0:T(8,128)(2,1)S(1)}, bf16[256,1024]{1,0:T(8,128)(2,1)S(1)}, bf16[256,1024]{1,0:T(8,128)(2,1)S(1)}, bf16[256,1024]{1,0:T(8,128)(2,1)S(1)}) custom-call(s32[6]{0:T(128)S(1)} %stack.36.yr.yv, bf16[128,8192]{1,0:T(8,128)(2,1)S(1)} %bitcast.33, bf16[128,8192]{1,0:T(8,128)(2,1)S(1)} %bitcast.24, ...), custom_call_target="tpu_custom_call" | custom-call | flops 3000000000 | bytes 4194304 | tf_op jit(solution)/shard_map/pallas_call | solution.py:652
  40.6 2.3 %collective-permute-start.8 = (bf16[256,1024]{1,0:T(8,128)(2,1)S(1)}, bf16[256,1024]{1,0:T(8,128)(2,1)S(1)}, u32[]{:S(2)}, u32[]{:S(2)}) collective-permute-start(bf16[256,1024]{1,0:T(8,128)(2,1)S(1)} %get-tuple-element.137.refs_13_.refs_6_), channel_id=1, source_target_pairs={{0,2},{1,3},{2,0},{3,1},{4,6},{5,7},{6,4},{7,5},{8,10},{9,11},{10,... | collective-permute-start | bytes 1572872 | tf_op jit(solution)/shard_map/ppermute | solution.py:714
  42.9 3.5 %shard_map.189 = (f32[256,1024]{1,0:T(8,128)S(1)}, f32[256,1024]{1,0:T(8,128)S(1)}, f32[2,128,128]{2,1,0:T(8,128)S(1)}) custom-call(s32[6]{0:T(128)S(1)} %stack.36.yr.yv, bf16[256,1024]{1,0:T(8,128)(2,1)S(1)} %get-tuple-element.142.refs_0_.refs_4_, bf16[256,1024]{1,0:T(8,128)(2,1)S(1)} %get-tuple-element.143.refs_1_.refs_5_, ...), custom_call_target="tpu_custom_call" | custom-call | flops 3000000000 | bytes 4194304 | tf_op jit(solution)/shard_map/pallas_call | solution.py:652
  47.6 4.2 %shard_map.188 = (bf16[4,256,1024]{2,1,0:T(8,128)(2,1)S(1)}, bf16[4,256,1024]{2,1,0:T(8,128)(2,1)S(1)}, bf16[256,1024]{1,0:T(8,128)(2,1)S(1)}, bf16[256,1024]{1,0:T(8,128)(2,1)S(1)}, bf16[256,1024]{1,0:T(8,128)(2,1)S(1)}) custom-call(s32[6]{0:T(128)S(1)} %stack.36.yr.yv, ...), custom_call_target="tpu_custom_call", output_to_operand_aliasing={{0}: (12, {}), {1}: (13, {})} | custom-call | flops 3000000000 | bytes 4194304 | tf_op jit(solution)/shard_map/pallas_call | solution.py:652
  51.8 3.1 %collective-permute-done.8.refs_0_.refs_17_.refs_20_ = bf16[256,1024]{1,0:T(8,128)(2,1)S(1)} collective-permute-done((bf16[256,1024]{1,0:T(8,128)(2,1)S(1)}, bf16[256,1024]{1,0:T(8,128)(2,1)S(1)}, u32[]{:S(2)}, u32[]{:S(2)}) %collective-permute-start.8) | collective-permute-done | bytes 524320 | tf_op jit(solution)/shard_map/ppermute | solution.py:714
  57.6 3.5 %shard_map.192 = (f32[256,1024]{1,0:T(8,128)S(1)}, f32[256,1024]{1,0:T(8,128)S(1)}, f32[2,128,128]{2,1,0:T(8,128)S(1)}) custom-call(s32[6]{0:T(128)S(1)} %stack.36.yr.yv, bf16[256,1024]{1,0:T(8,128)(2,1)S(1)} %get-tuple-element.141.refs_6_.refs_0_.refs_4_, bf16[256,1024]{1,0:T(8,128)(2,1)S(1)} %get-tuple-element.154.refs_1_.refs_5_, ...), custom_call_target="tpu_custom_call" | custom-call | flops 3000000000 | bytes 4194304 | tf_op jit(solution)/shard_map/pallas_call | solution.py:652
  61.1 4.2 %shard_map.191 = (bf16[4,256,1024]{2,1,0:T(8,128)(2,1)S(1)}, bf16[4,256,1024]{2,1,0:T(8,128)(2,1)S(1)}, bf16[256,1024]{1,0:T(8,128)(2,1)S(1)}, bf16[256,1024]{1,0:T(8,128)(2,1)S(1)}, bf16[256,1024]{1,0:T(8,128)(2,1)S(1)}) custom-call(s32[6]{0:T(128)S(1)} %stack.36.yr.yv, ...), custom_call_target="tpu_custom_call", output_to_operand_aliasing={{0}: (12, {}), {1}: (13, {})} | custom-call | flops 3000000000 | bytes 4194304 | tf_op jit(solution)/shard_map/pallas_call | solution.py:652
  65.3 5.6 %collective-permute-done.10.refs_0_.refs_17_.refs_20_ = bf16[256,1024]{1,0:T(8,128)(2,1)S(1)} collective-permute-done((bf16[256,1024]{1,0:T(8,128)(2,1)S(1)}, bf16[256,1024]{1,0:T(8,128)(2,1)S(1)}, u32[]{:S(2)}, u32[]{:S(2)}) %collective-permute-start.10) | collective-permute-done | bytes 524320 | tf_op jit(solution)/shard_map/ppermute | solution.py:714
  73.2 3.5 %shard_map.195 = (f32[256,1024]{1,0:T(8,128)S(1)}, f32[256,1024]{1,0:T(8,128)S(1)}, f32[2,128,128]{2,1,0:T(8,128)S(1)}) custom-call(s32[6]{0:T(128)S(1)} %stack.36.yr.yv, bf16[256,1024]{1,0:T(8,128)(2,1)S(1)} %get-tuple-element.153.refs_6_.refs_0_.refs_4_, bf16[256,1024]{1,0:T(8,128)(2,1)S(1)} %get-tuple-element.163.refs_1_.refs_5_, ...), custom_call_target="tpu_custom_call" | custom-call | flops 3000000000 | bytes 4194304 | tf_op jit(solution)/shard_map/pallas_call | solution.py:652
  76.7 4.2 %shard_map.194 = (bf16[4,256,1024]{2,1,0:T(8,128)(2,1)S(1)}, bf16[4,256,1024]{2,1,0:T(8,128)(2,1)S(1)}, bf16[256,1024]{1,0:T(8,128)(2,1)S(1)}, bf16[256,1024]{1,0:T(8,128)(2,1)S(1)}, bf16[256,1024]{1,0:T(8,128)(2,1)S(1)}) custom-call(s32[6]{0:T(128)S(1)} %stack.36.yr.yv, ...), custom_call_target="tpu_custom_call", output_to_operand_aliasing={{0}: (12, {}), {1}: (13, {})} | custom-call | flops 3000000000 | bytes 4194304 | tf_op jit(solution)/shard_map/pallas_call | solution.py:652
  80.9 5.9 %collective-permute-done.12.refs_0_.refs_19_.refs_22_.refs_17_.refs_20_ = bf16[256,1024]{1,0:T(8,128)(2,1)S(1)} collective-permute-done((bf16[256,1024]{1,0:T(8,128)(2,1)S(1)}, bf16[256,1024]{1,0:T(8,128)(2,1)S(1)}, u32[]{:S(2)}, u32[]{:S(2)}) %collective-permute-start.12) | collective-permute-done | bytes 524320 | tf_op jit(solution)/shard_map/ppermute | solution.py:714
  89.2 7.7 %shard_map.198 = (bf16[128,8192]{1,0:T(8,128)(2,1)}, bf16[128,8192]{1,0:T(8,128)(2,1)}, f32[8,5376]{1,0:T(8,128)S(1)}, f32[8,5376]{1,0:T(8,128)S(1)}, bf16[2,128...) custom-call(s32[6]{0:T(128)S(1)} %stack.36.yr.yv, ...), custom_call_target="tpu_custom_call" | custom-call | flops 6000000000 | bytes 6291456 | tf_op jit(solution)/shard_map/pallas_call | solution.py:652
  96.9 2.1 %collective-permute-start.19 = (bf16[2,128,1024]{2,1,0:T(8,128)(2,1)S(1)}, bf16[2,128,1024]{2,1,0:T(8,128)(2,1)S(1)}, u32[]{:S(2)}, u32[]{:S(2)}) collective-permute-start(bf16[2,128,1024]{2,1,0:T(8,128)(2,1)S(1)} %get-tuple-element.185), channel_id=1, source_target_pairs={{0,1},{1,0},{2,3},{3,2},{4,5},{5,4},{6,7},{7,6},{8,9},{9,8},{10,11... | collective-permute-start | bytes 1572872 | tf_op jit(solution)/shard_map/ppermute | solution.py:907
  99.0 3.5 %shard_map.197 = (f32[256,1024]{1,0:T(8,128)S(1)}, f32[256,1024]{1,0:T(8,128)S(1)}, f32[2,128,128]{2,1,0:T(8,128)S(1)}) custom-call(s32[6]{0:T(128)S(1)} %stack.36.yr.yv, bf16[256,1024]{1,0:T(8,128)(2,1)S(1)} %get-tuple-element.157.refs_6_.refs_0_.refs_4_, bf16[256,1024]{1,0:T(8,128)(2,1)S(1)} %get-tuple-element.158.refs_1_.refs_5_, ...), custom_call_target="tpu_custom_call" | custom-call | flops 3000000000 | bytes 4194304 | tf_op jit(solution)/shard_map/pallas_call | solution.py:652
  105.9 8.0 %shard_map.200 = (bf16[128,8192]{1,0:T(8,128)(2,1)}, bf16[128,8192]{1,0:T(8,128)(2,1)}, f32[8,5376]{1,0:T(8,128)S(1)}, f32[8,5376]{1,0:T(8,128)S(1)}, bf16[2,128...) custom-call(s32[6]{0:T(128)S(1)} %stack.36.yr.yv, ...), custom_call_target="tpu_custom_call", output_to_operand_aliasing={{0}: (24, {}), {1}: (25, {}), {2}: (26, {}), {3}: (27, {})} | custom-call | flops 6000000000 | bytes 6291456 | tf_op jit(solution)/shard_map/pallas_call | solution.py:652
  115.2 3.5 %collective-permute-done.17.refs_0_.refs_19_.refs_22_ = bf16[256,1024]{1,0:T(8,128)(2,1)S(1)} collective-permute-done((bf16[256,1024]{1,0:T(8,128)(2,1)S(1)}, bf16[256,1024]{1,0:T(8,128)(2,1)S(1)}, u32[]{:S(2)}, u32[]{:S(2)}) %collective-permute-start.17) | collective-permute-done | bytes 524320 | tf_op jit(solution)/shard_map/ppermute | solution.py:714
  118.7 2.6 %shard_map.201 = (bf16[256,1024]{1,0:T(8,128)(2,1)S(1)}, bf16[256,1024]{1,0:T(8,128)(2,1)}) custom-call(s32[6]{0:T(128)S(1)} %stack.36.yr.yv, bf16[256,1024]{1,0:T(8,128)(2,1)S(1)} %collective-permute-done.17.refs_0_.refs_19_.refs_22_, bf16[256,1024]{1,0:T(8,128)(2,1)S(1)} %collective-permute-done.16.refs_1_.refs_18_.refs_21_, ...), custom_call_target="tpu_custom_call" | custom-call | flops 1000000000 | bytes 3145728 | tf_op jit(solution)/shard_map/pallas_call | solution.py:652
  121.9 7.7 %shard_map.202 = (bf16[128,8192]{1,0:T(8,128)(2,1)}, bf16[128,8192]{1,0:T(8,128)(2,1)}, f32[8,5376]{1,0:T(8,128)S(1)}, f32[8,5376]{1,0:T(8,128)S(1)}, bf16[2,128...) custom-call(s32[6]{0:T(128)S(1)} %stack.36.yr.yv, ...), custom_call_target="tpu_custom_call", output_to_operand_aliasing={{0}: (24, {}), {1}: (25, {}), {2}: (26, {}), {3}: (27, {})} | custom-call | flops 6000000000 | bytes 6291456 | tf_op jit(solution)/shard_map/pallas_call | solution.py:652
  131.4 2.2 %shard_map.204 = (f32[8,5376]{1,0:T(8,128)S(1)}, f32[8,5376]{1,0:T(8,128)S(1)}, bf16[128,1024]{1,0:T(8,128)(2,1)}, bf16[128,1024]{1,0:T(8,128)(2,1)}, bf16[128,512]{1,0:T(8,128)(2,1)S(1)}) custom-call(s32[6]{0:T(128)S(1)} %stack.36.yr.yv, bf16[128,1024]{1,0:T(8,128)(2,1)S(1)} %bitcast.51, ...), custom_call_target="tpu_custom_call", output_to_operand_aliasing={{0}: (18, {}), {1}: (19, {})} | custom-call | flops 3000000000 | bytes 4194304 | tf_op jit(solution)/shard_map/pallas_call | solution.py:652
  134.7 7.7 %shard_map.205 = (bf16[128,8192]{1,0:T(8,128)(2,1)}, bf16[128,8192]{1,0:T(8,128)(2,1)}, f32[8,5376]{1,0:T(8,128)S(1)}, f32[8,5376]{1,0:T(8,128)S(1)}, bf16[2,128...) custom-call(s32[6]{0:T(128)S(1)} %stack.36.yr.yv, ...), custom_call_target="tpu_custom_call", output_to_operand_aliasing={{0}: (24, {}), {1}: (25, {}), {2}: (26, {}), {3}: (27, {})} | custom-call | flops 6000000000 | bytes 6291456 | tf_op jit(solution)/shard_map/pallas_call | solution.py:652
  143.2 2.9 %shard_map.206 = (f32[8,5376]{1,0:T(8,128)S(1)}, f32[8,5376]{1,0:T(8,128)S(1)}, bf16[128,1024]{1,0:T(8,128)(2,1)}, bf16[128,1024]{1,0:T(8,128)(2,1)}, bf16[128,6...) custom-call(s32[6]{0:T(128)S(1)} %stack.36.yr.yv, ...), custom_call_target="tpu_custom_call", output_to_operand_aliasing={{0}: (30, {}), {1}: (31, {}), {2}: (32, {}), {3}: (33, {})} | custom-call | flops 3000000000 | bytes 4194304 | tf_op jit(solution)/shard_map/pallas_call | solution.py:652
  155.1 2.3 %collective-permute-start.32 = (f32[8,2688]{1,0:T(8,128)S(1)}, f32[8,2688]{1,0:T(8,128)S(1)}, u32[]{:S(2)}, u32[]{:S(2)}) collective-permute-start(f32[8,2688]{1,0:T(8,128)S(1)} %shard_map.211.refs_3_.refs_0_), channel_id=1, source_target_pairs={{0,6},{1,7},{2,4},{3,5},{4,2},{5,3},{6,0},{7,1},{8,14},{9,15},{10,... | collective-permute-start | bytes 258056 | tf_op jit(solution)/shard_map/ppermute | solution.py:1076
  157.4 2.1 %collective-permute-start.30 = (f32[8,2688]{1,0:T(8,128)S(1)}, f32[8,2688]{1,0:T(8,128)S(1)}, u32[]{:S(2)}, u32[]{:S(2)}) collective-permute-start(f32[8,2688]{1,0:T(8,128)S(1)} %shard_map.211.refs_3_.refs_0_), channel_id=1, source_target_pairs={{0,2},{1,3},{2,0},{3,1},{4,6},{5,7},{6,4},{7,5},{8,10},{9,11},{10,... | collective-permute-start | bytes 258056 | tf_op jit(solution)/shard_map/ppermute | solution.py:1076
  162.3 3.0 %collective-permute-done.31.refs_2_ = f32[8,2688]{1,0:T(8,128)S(1)} collective-permute-done((f32[8,2688]{1,0:T(8,128)S(1)}, f32[8,2688]{1,0:T(8,128)S(1)}, u32[]{:S(2)}, u32[]{:S(2)}) %collective-permute-start.31) | collective-permute-done | bytes 86048 | tf_op jit(solution)/shard_map/ppermute | solution.py:1076
  168.0 2.4 %collective-permute-done.33.refs_1_ = f32[8,2688]{1,0:T(8,128)S(1)} collective-permute-done((f32[8,2688]{1,0:T(8,128)S(1)}, f32[8,2688]{1,0:T(8,128)S(1)}, u32[]{:S(2)}, u32[]{:S(2)}) %collective-permute-start.33) | collective-permute-done | bytes 86048 | tf_op jit(solution)/shard_map/ppermute | solution.py:1079
  173.3 3.9 %collective-permute-done.26.next_e = f32[16,1024]{1,0:T(8,128)S(1)} collective-permute-done((f32[16,1024]{1,0:T(8,128)S(1)}, f32[16,1024]{1,0:T(8,128)S(1)}, u32[]{:S(2)}, u32[]{:S(2)}) %collective-permute-start.26) | collective-permute-done | bytes 65568 | tf_op jit(solution)/shard_map/ppermute | solution.py:714
  177.2 2.4 %shard_map.215 = (bf16[128,8192]{1,0:T(8,128)(2,1)}, bf16[128,1024]{1,0:T(8,128)(2,1)}, bf16[128,1024]{1,0:T(8,128)(2,1)}, f32[8,128]{1,0:T(8,128)S(1)}) custom-call(s32[6]{0:T(128)S(1)} %stack.36.yr.yv, f32[16,1024]{1,0:T(8,128)S(1)} %collective-permute-done.25.next0, ...), custom_call_target="tpu_custom_call", output_to_operand_aliasing={{0}: (5, {}), {1}: (6, {}), {2}: (7, {})} | custom-call | flops 1000000000 | bytes 1048576 | tf_op jit(solution)/shard_map/pallas_call | solution.py:1104
  (120 shorter events, 51.4 us)
Async XLA Ops:
  5.6 19.4 %collective-permute-start.5 = (bf16[32,1024]{1,0:T(8,128)(2,1)S(1)}, bf16[32,1024]{1,0:T(8,128)(2,1)}, u32[]{:S(2)}, u32[]{:S(2)}) collective-permute-start(bf16[32,1024]{1,0:T(8,128)(2,1)S(1)} %shard_map.182.refs_2_), channel_id=1, source_target_pairs={{0,8},{1,9},{2,4},{3,5},{4,2},{5,3},{6,14},{7,15},{8,0},{9,1},{10,... | collective-permute-start | bytes 196616 | tf_op jit(solution)/shard_map/ppermute | solution.py:714
  6.1 18.8 %collective-permute-start.4 = (bf16[32,1024]{1,0:T(8,128)(2,1)S(1)}, bf16[32,1024]{1,0:T(8,128)(2,1)}, u32[]{:S(2)}, u32[]{:S(2)}) collective-permute-start(bf16[32,1024]{1,0:T(8,128)(2,1)S(1)} %shard_map.182.refs_2_), channel_id=1, source_target_pairs={{0,2},{1,3},{2,0},{3,1},{4,6},{5,7},{6,4},{7,5},{8,10},{9,11},{10,... | collective-permute-start | bytes 196616 | tf_op jit(solution)/shard_map/ppermute | solution.py:714
  10.3 14.7 %collective-permute-start.3 = (bf16[32,1024]{1,0:T(8,128)(2,1)S(1)}, bf16[32,1024]{1,0:T(8,128)(2,1)}, u32[]{:S(2)}, u32[]{:S(2)}) collective-permute-start(bf16[32,1024]{1,0:T(8,128)(2,1)S(1)} %shard_map.182.refs_2_), channel_id=1, source_target_pairs={{0,8},{1,2},{2,1},{3,4},{4,3},{5,6},{6,5},{7,15},{8,0},{9,10},{10,... | collective-permute-start | bytes 196616 | tf_op jit(solution)/shard_map/ppermute | solution.py:714
  10.3 10.0 %collective-permute-start = (bf16[128,1152]{1,0:T(8,128)(2,1)}, bf16[128,1152]{1,0:T(8,128)(2,1)S(1)}, u32[]{:S(2)}, u32[]{:S(2)}) collective-permute-start(bf16[128,1152]{1,0:T(8,128)(2,1)} %shard_map.179.refs_3_), channel_id=1, source_target_pairs={{0,1},{1,0},{2,3},{3,2},{4,5},{5,4},{6,7},{7,6},{8,9},{9,8},{10,11... | collective-permute-start | bytes 884744 | tf_op jit(solution)/shard_map/ppermute | solution.py:732
  12.4 19.1 %collective-permute-start.6 = (bf16[2,128,1024]{2,1,0:T(8,128)(2,1)S(1)}, bf16[2,128,1024]{2,1,0:T(8,128)(2,1)S(1)}, u32[]{:S(2)}, u32[]{:S(2)}) collective-permute-start(bf16[2,128,1024]{2,1,0:T(8,128)(2,1)S(1)} %shard_map.184), channel_id=1, source_target_pairs={{0,1},{1,0},{2,3},{3,2},{4,5},{5,4},{6,7},{7,6},{8,9},{9,8},{10,11... | collective-permute-start | bytes 1572872 | tf_op jit(solution)/shard_map/ppermute | solution.py:756
  22.5 23.8 %collective-permute-start.1 = (bf16[2,128,1024]{2,1,0:T(8,128)(2,1)S(1)}, bf16[2,128,1024]{2,1,0:T(8,128)(2,1)S(1)}, u32[]{:S(2)}, u32[]{:S(2)}) collective-permute-start(bf16[2,128,1024]{2,1,0:T(8,128)(2,1)S(1)} %shard_map.180), channel_id=1, source_target_pairs={{0,1},{1,0},{2,3},{3,2},{4,5},{5,4},{6,7},{7,6},{8,9},{9,8},{10,11... | collective-permute-start | bytes 1572872 | tf_op jit(solution)/shard_map/ppermute | solution.py:756
  32.3 28.7 %collective-permute-start.7 = (bf16[2,128,1024]{2,1,0:T(8,128)(2,1)S(1)}, bf16[2,128,1024]{2,1,0:T(8,128)(2,1)S(1)}, u32[]{:S(2)}, u32[]{:S(2)}) collective-permute-start(bf16[2,128,1024]{2,1,0:T(8,128)(2,1)S(1)} %shard_map.185), channel_id=1, source_target_pairs={{0,1},{1,0},{2,3},{3,2},{4,5},{5,4},{6,7},{7,6},{8,9},{9,8},{10,11... | collective-permute-start | bytes 1572872 | tf_op jit(solution)/shard_map/ppermute | solution.py:756
  40.5 11.3 %collective-permute-start.9 = (bf16[256,1024]{1,0:T(8,128)(2,1)S(1)}, bf16[256,1024]{1,0:T(8,128)(2,1)S(1)}, u32[]{:S(2)}, u32[]{:S(2)}) collective-permute-start(bf16[256,1024]{1,0:T(8,128)(2,1)S(1)} %get-tuple-element.140), channel_id=1, source_target_pairs={{0,8},{1,9},{2,4},{3,5},{4,2},{5,3},{6,14},{7,15},{8,0},{9,1},{10,... | collective-permute-start | bytes 1572872 | tf_op jit(solution)/shard_map/ppermute | solution.py:714
  40.6 14.3 %collective-permute-start.8 = (bf16[256,1024]{1,0:T(8,128)(2,1)S(1)}, bf16[256,1024]{1,0:T(8,128)(2,1)S(1)}, u32[]{:S(2)}, u32[]{:S(2)}) collective-permute-start(bf16[256,1024]{1,0:T(8,128)(2,1)S(1)} %get-tuple-element.137.refs_13_.refs_6_), channel_id=1, source_target_pairs={{0,2},{1,3},{2,0},{3,1},{4,6},{5,7},{6,4},{7,5},{8,10},{9,11},{10,... | collective-permute-start | bytes 1572872 | tf_op jit(solution)/shard_map/ppermute | solution.py:714
  47.0 29.7 %collective-permute-start.2 = (bf16[2,128,1024]{2,1,0:T(8,128)(2,1)S(1)}, bf16[2,128,1024]{2,1,0:T(8,128)(2,1)S(1)}, u32[]{:S(2)}, u32[]{:S(2)}) collective-permute-start(bf16[2,128,1024]{2,1,0:T(8,128)(2,1)S(1)} %shard_map.181), channel_id=1, source_target_pairs={{0,1},{1,0},{2,3},{3,2},{4,5},{5,4},{6,7},{7,6},{8,9},{9,8},{10,11... | collective-permute-start | bytes 1572872 | tf_op jit(solution)/shard_map/ppermute | solution.py:756
  56.4 8.8 %collective-permute-start.11 = (bf16[256,1024]{1,0:T(8,128)(2,1)S(1)}, bf16[256,1024]{1,0:T(8,128)(2,1)S(1)}, u32[]{:S(2)}, u32[]{:S(2)}) collective-permute-start(bf16[256,1024]{1,0:T(8,128)(2,1)S(1)} %get-tuple-element.152), channel_id=1, source_target_pairs={{0,8},{1,9},{2,4},{3,5},{4,2},{5,3},{6,14},{7,15},{8,0},{9,1},{10,... | collective-permute-start | bytes 1572872 | tf_op jit(solution)/shard_map/ppermute | solution.py:714
  56.5 14.3 %collective-permute-start.10 = (bf16[256,1024]{1,0:T(8,128)(2,1)S(1)}, bf16[256,1024]{1,0:T(8,128)(2,1)S(1)}, u32[]{:S(2)}, u32[]{:S(2)}) collective-permute-start(bf16[256,1024]{1,0:T(8,128)(2,1)S(1)} %get-tuple-element.149.refs_13_.refs_6_), channel_id=1, source_target_pairs={{0,2},{1,3},{2,0},{3,1},{4,6},{5,7},{6,4},{7,5},{8,10},{9,11},{10,... | collective-permute-start | bytes 1572872 | tf_op jit(solution)/shard_map/ppermute | solution.py:714
  72.4 8.5 %collective-permute-start.13 = (bf16[256,1024]{1,0:T(8,128)(2,1)S(1)}, bf16[256,1024]{1,0:T(8,128)(2,1)S(1)}, u32[]{:S(2)}, u32[]{:S(2)}) collective-permute-start(bf16[256,1024]{1,0:T(8,128)(2,1)S(1)} %get-tuple-element.160), channel_id=1, source_target_pairs={{0,8},{1,9},{2,4},{3,5},{4,2},{5,3},{6,14},{7,15},{8,0},{9,1},{10,... | collective-permute-start | bytes 1572872 | tf_op jit(solution)/shard_map/ppermute | solution.py:714
  72.5 14.3 %collective-permute-start.12 = (bf16[256,1024]{1,0:T(8,128)(2,1)S(1)}, bf16[256,1024]{1,0:T(8,128)(2,1)S(1)}, u32[]{:S(2)}, u32[]{:S(2)}) collective-permute-start(bf16[256,1024]{1,0:T(8,128)(2,1)S(1)} %get-tuple-element.156.refs_13_.refs_6_), channel_id=1, source_target_pairs={{0,2},{1,3},{2,0},{3,1},{4,6},{5,7},{6,4},{7,5},{8,10},{9,11},{10,... | collective-permute-start | bytes 1572872 | tf_op jit(solution)/shard_map/ppermute | solution.py:714
  88.3 14.1 %collective-permute-start.15 = (bf16[256,1024]{1,0:T(8,128)(2,1)S(1)}, bf16[256,1024]{1,0:T(8,128)(2,1)S(1)}, u32[]{:S(2)}, u32[]{:S(2)}) collective-permute-start(bf16[256,1024]{1,0:T(8,128)(2,1)S(1)} %get-tuple-element.168), channel_id=1, source_target_pairs={{0,8},{1,9},{2,4},{3,5},{4,2},{5,3},{6,14},{7,15},{8,0},{9,1},{10,... | collective-permute-start | bytes 1572872 | tf_op jit(solution)/shard_map/ppermute | solution.py:714
  88.4 14.3 %collective-permute-start.14 = (bf16[256,1024]{1,0:T(8,128)(2,1)S(1)}, bf16[256,1024]{1,0:T(8,128)(2,1)S(1)}, u32[]{:S(2)}, u32[]{:S(2)}) collective-permute-start(bf16[256,1024]{1,0:T(8,128)(2,1)S(1)} %get-tuple-element.165.refs_6_.refs_23_), channel_id=1, source_target_pairs={{0,2},{1,3},{2,0},{3,1},{4,6},{5,7},{6,4},{7,5},{8,10},{9,11},{10,... | collective-permute-start | bytes 1572872 | tf_op jit(solution)/shard_map/ppermute | solution.py:714
  96.9 33.2 %collective-permute-start.19 = (bf16[2,128,1024]{2,1,0:T(8,128)(2,1)S(1)}, bf16[2,128,1024]{2,1,0:T(8,128)(2,1)S(1)}, u32[]{:S(2)}, u32[]{:S(2)}) collective-permute-start(bf16[2,128,1024]{2,1,0:T(8,128)(2,1)S(1)} %get-tuple-element.185), channel_id=1, source_target_pairs={{0,1},{1,0},{2,3},{3,2},{4,5},{5,4},{6,7},{7,6},{8,9},{9,8},{10,11... | collective-permute-start | bytes 1572872 | tf_op jit(solution)/shard_map/ppermute | solution.py:907
  104.3 10.9 %collective-permute-start.16 = (bf16[256,1024]{1,0:T(8,128)(2,1)S(1)}, bf16[256,1024]{1,0:T(8,128)(2,1)S(1)}, u32[]{:S(2)}, u32[]{:S(2)}) collective-permute-start(bf16[256,1024]{1,0:T(8,128)(2,1)S(1)} %get-tuple-element.174), channel_id=1, source_target_pairs={{0,8},{1,9},{2,4},{3,5},{4,2},{5,3},{6,14},{7,15},{8,0},{9,1},{10,... | collective-permute-start | bytes 1572872 | tf_op jit(solution)/shard_map/ppermute | solution.py:714
  104.4 14.3 %collective-permute-start.17 = (bf16[256,1024]{1,0:T(8,128)(2,1)S(1)}, bf16[256,1024]{1,0:T(8,128)(2,1)S(1)}, u32[]{:S(2)}, u32[]{:S(2)}) collective-permute-start(bf16[256,1024]{1,0:T(8,128)(2,1)S(1)} %get-tuple-element.175.refs_27_), channel_id=1, source_target_pairs={{0,2},{1,3},{2,0},{3,1},{4,6},{5,7},{6,4},{7,5},{8,10},{9,11},{10,... | collective-permute-start | bytes 1572872 | tf_op jit(solution)/shard_map/ppermute | solution.py:714
  113.9 36.1 %collective-permute-start.22 = (bf16[2,128,1024]{2,1,0:T(8,128)(2,1)S(1)}, bf16[2,128,1024]{2,1,0:T(8,128)(2,1)S(1)}, u32[]{:S(2)}, u32[]{:S(2)}) collective-permute-start(bf16[2,128,1024]{2,1,0:T(8,128)(2,1)S(1)} %get-tuple-element.208), channel_id=1, source_target_pairs={{0,1},{1,0},{2,3},{3,2},{4,5},{5,4},{6,7},{7,6},{8,9},{9,8},{10,11... | collective-permute-start | bytes 1572872 | tf_op jit(solution)/shard_map/ppermute | solution.py:907
  121.3 13.5 %collective-permute-start.18 = (bf16[256,1024]{1,0:T(8,128)(2,1)S(1)}, bf16[256,1024]{1,0:T(8,128)(2,1)S(1)}, u32[]{:S(2)}, u32[]{:S(2)}) collective-permute-start(bf16[256,1024]{1,0:T(8,128)(2,1)S(1)} %get-tuple-element.184.refs_27_.refs_3_.refs_19_), channel_id=1, source_target_pairs={{0,2},{1,3},{2,0},{3,1},{4,6},{5,7},{6,4},{7,5},{8,10},{9,11},{10,... | collective-permute-start | bytes 1572872 | tf_op jit(solution)/shard_map/ppermute | solution.py:714
  129.6 23.2 %collective-permute-start.21 = (bf16[2,128,1024]{2,1,0:T(8,128)(2,1)S(1)}, bf16[2,128,1024]{2,1,0:T(8,128)(2,1)S(1)}, u32[]{:S(2)}, u32[]{:S(2)}) collective-permute-start(bf16[2,128,1024]{2,1,0:T(8,128)(2,1)S(1)} %get-tuple-element.207), channel_id=1, source_target_pairs={{0,1},{1,0},{2,3},{3,2},{4,5},{5,4},{6,7},{7,6},{8,9},{9,8},{10,11... | collective-permute-start | bytes 1572872 | tf_op jit(solution)/shard_map/ppermute | solution.py:907
  142.5 14.9 %collective-permute-start.20 = (bf16[2,128,1024]{2,1,0:T(8,128)(2,1)S(1)}, bf16[2,128,1024]{2,1,0:T(8,128)(2,1)S(1)}, u32[]{:S(2)}, u32[]{:S(2)}) collective-permute-start(bf16[2,128,1024]{2,1,0:T(8,128)(2,1)S(1)} %get-tuple-element.206), channel_id=1, source_target_pairs={{0,1},{1,0},{2,3},{3,2},{4,5},{5,4},{6,7},{7,6},{8,9},{9,8},{10,11... | collective-permute-start | bytes 1572872 | tf_op jit(solution)/shard_map/ppermute | solution.py:907
  146.7 20.1 %collective-permute-start.28 = (bf16[128,512]{1,0:T(8,128)(2,1)S(1)}, bf16[128,512]{1,0:T(8,128)(2,1)S(1)}, u32[]{:S(2)}, u32[]{:S(2)}) collective-permute-start(bf16[128,512]{1,0:T(8,128)(2,1)S(1)} %get-tuple-element.236), channel_id=1, source_target_pairs={{0,1},{1,0},{2,3},{3,2},{4,5},{5,4},{6,7},{7,6},{8,9},{9,8},{10,11... | collective-permute-start | bytes 393224 | tf_op jit(solution)/shard_map/ppermute | solution.py:982
  148.2 18.6 %collective-permute-start.29 = (bf16[128,640]{1,0:T(8,128)(2,1)S(1)}, bf16[128,640]{1,0:T(8,128)(2,1)S(1)}, u32[]{:S(2)}, u32[]{:S(2)}) collective-permute-start(bf16[128,640]{1,0:T(8,128)(2,1)S(1)} %get-tuple-element.237), channel_id=1, source_target_pairs={{0,1},{1,0},{2,3},{3,2},{4,5},{5,4},{6,7},{7,6},{8,9},{9,8},{10,11... | collective-permute-start | bytes 491528 | tf_op jit(solution)/shard_map/ppermute | solution.py:982
  149.9 4.6 %collective-permute-start.24 = (f32[8,2688]{1,0:T(8,128)S(1)}, f32[8,2688]{1,0:T(8,128)S(1)}, u32[]{:S(2)}, u32[]{:S(2)}) collective-permute-start(f32[8,2688]{1,0:T(8,128)S(1)} %shard_map.208.refs_3_.refs_0_), channel_id=1, source_target_pairs={{0,16},{8,24},{16,0},{24,8},{1,17},{9,25},{17,1},{25,9},{2,18},{10... | collective-permute-start | bytes 258056 | tf_op jit(solution)/shard_map/ppermute | solution.py:1065
  155.1 7.2 %collective-permute-start.32 = (f32[8,2688]{1,0:T(8,128)S(1)}, f32[8,2688]{1,0:T(8,128)S(1)}, u32[]{:S(2)}, u32[]{:S(2)}) collective-permute-start(f32[8,2688]{1,0:T(8,128)S(1)} %shard_map.211.refs_3_.refs_0_), channel_id=1, source_target_pairs={{0,6},{1,7},{2,4},{3,5},{4,2},{5,3},{6,0},{7,1},{8,14},{9,15},{10,... | collective-permute-start | bytes 258056 | tf_op jit(solution)/shard_map/ppermute | solution.py:1076
  157.3 8.0 %collective-permute-start.31 = (f32[8,2688]{1,0:T(8,128)S(1)}, f32[8,2688]{1,0:T(8,128)S(1)}, u32[]{:S(2)}, u32[]{:S(2)}) collective-permute-start(f32[8,2688]{1,0:T(8,128)S(1)} %shard_map.211.refs_3_.refs_0_), channel_id=1, source_target_pairs={{0,4},{1,5},{2,6},{3,7},{4,0},{5,1},{6,2},{7,3},{8,12},{9,13},{10,... | collective-permute-start | bytes 258056 | tf_op jit(solution)/shard_map/ppermute | solution.py:1076
  157.4 7.9 %collective-permute-start.30 = (f32[8,2688]{1,0:T(8,128)S(1)}, f32[8,2688]{1,0:T(8,128)S(1)}, u32[]{:S(2)}, u32[]{:S(2)}) collective-permute-start(f32[8,2688]{1,0:T(8,128)S(1)} %shard_map.211.refs_3_.refs_0_), channel_id=1, source_target_pairs={{0,2},{1,3},{2,0},{3,1},{4,6},{5,7},{6,4},{7,5},{8,10},{9,11},{10,... | collective-permute-start | bytes 258056 | tf_op jit(solution)/shard_map/ppermute | solution.py:1076
  165.9 4.6 %collective-permute-start.33 = (f32[8,2688]{1,0:T(8,128)S(1)}, f32[8,2688]{1,0:T(8,128)S(1)}, u32[]{:S(2)}, u32[]{:S(2)}) collective-permute-start(f32[8,2688]{1,0:T(8,128)S(1)} %shard_map.213.refs_5_.refs_0_), channel_id=1, source_target_pairs={{0,1},{1,0},{2,3},{3,2},{4,5},{5,4},{6,7},{7,6},{8,9},{9,8},{10,11... | collective-permute-start | bytes 258056 | tf_op jit(solution)/shard_map/ppermute | solution.py:1079
  171.7 7.9 %collective-permute-start.34 = (f32[2,8,2688]{2,1,0:T(8,128)S(1)}, f32[2,8,2688]{2,1,0:T(8,128)S(1)}, u32[]{:S(2)}, u32[]{:S(2)}) collective-permute-start(f32[2,8,2688]{2,1,0:T(8,128)S(1)} %shard_map.216.refs_0_), channel_id=1, source_target_pairs={{0,8},{8,0},{16,24},{24,16},{1,9},{9,1},{17,25},{25,17},{2,10},{10... | collective-permute-start | bytes 516104 | tf_op jit(solution)/shard_map/ppermute | solution.py:1101
  172.3 4.9 %collective-permute-start.26 = (f32[16,1024]{1,0:T(8,128)S(1)}, f32[16,1024]{1,0:T(8,128)S(1)}, u32[]{:S(2)}, u32[]{:S(2)}) collective-permute-start(f32[16,1024]{1,0:T(8,128)S(1)} %get-tuple-element.234), channel_id=1, source_target_pairs={{0,2},{1,3},{2,0},{3,1},{4,6},{5,7},{6,4},{7,5},{8,10},{9,11},{10,... | collective-permute-start | bytes 196616 | tf_op jit(solution)/shard_map/ppermute | solution.py:714
  (21 other events, 55.0 us)
